TPU v7x, 512 devices: a whole 4x4x16 slice. The times are simulated.
512 devices in a mesh: lat: 32 (over z_hi, x, core), lon: 16 (over y, z_lo).
Axes of the slice: x: 4, y: 4, z: 16 (z_hi: 4, z_lo: 4; z = z_hi * 4 + z_lo), core: 2. Of those that a mesh axis runs over, the one named last changes fastest.
Arguments:
- state_field: float32 [384, 384, 256], P('lat', 'lon'), may hold values from -6 to 6
- cotangent: bfloat16 [384, 384, 256], P('lat', 'lon'), may hold values from -6 to 6
- depthwise: float32 [49, 256], replicated, may hold values from -0.875 to 0.875
- norm_gain: float32 [256], replicated, may hold values from 0.4 to 1.6
- w_in: bfloat16 [256, 1024], replicated, may hold values from -0.375 to 0.375
- w_out: bfloat16 [1024, 256], replicated, may hold values from -0.1875 to 0.1875
Outputs:
- block_out: bfloat16 [384, 384, 256], P('lat', 'lon')
- grad_input: bfloat16 [384, 384, 256], P('lat', 'lon')
- weight_grads: float32 [1024, 512], P(('lat', 'lon'))
- grad_depthwise: float32 [49, 256], replicated
- grad_gain: float32 [256], replicated
All inputs are finite; a program needn't handle non-finite values.
Results may differ from a plain program's by a relative error of at most 0.0052.
Values sent between devices are 32-bit elements; how exact they have to be, the bound alone decides.
No kernel may reach another device: no remote copies, remote signals or barrier semaphores. Data moves between devices by JAX's collectives and lax.ppermute only.
A program may use at most 64 MiB of HBM per device.

v0:
```python
import math

import jax
import jax.numpy as jnp
from jax import lax
from jax.sharding import PartitionSpec as P


def padded_2(cells, sides, width, closed):
    for axis, dim in sides:
        count = lax.axis_size(axis)
        ends = count if closed else count - 1
        head = lax.slice_in_dim(cells, 0, width, axis=dim)
        tail = lax.slice_in_dim(cells, cells.shape[dim] - width, cells.shape[dim], axis=dim)
        cells = jnp.concatenate(
            [
                lax.ppermute(tail, axis, [(i, (i + 1) % count) for i in range(ends)]),
                cells,
                lax.ppermute(head, axis, [((i + 1) % count, i) for i in range(ends)]),
            ],
            axis=dim,
        )
    return cells


def shifted(value, axis, by):
    peers = lax.axis_size(axis)
    return lax.ppermute(value, axis, [(i, (i + by) % peers) for i in range(peers)])


def gelu_value(values):
    return 0.5 * values * (1.0 + lax.erf(values * 0.7071067811865476))


def gelu_slope(values):
    return (
        0.5 * (1.0 + lax.erf(values * 0.7071067811865476))
        + values * jnp.exp(-0.5 * values * values) * 0.3989422804014327
    )


def layer_norm(convolved, norm_gain):
    average = jnp.mean(convolved, axis=-1, keepdims=True)
    centred_raw = convolved - average
    variance = jnp.mean(centred_raw * centred_raw, axis=-1, keepdims=True)
    inv_std = 1.0 / jnp.sqrt(variance + 1e-06)
    centred = centred_raw * inv_std
    normed = (centred * norm_gain).astype(jnp.bfloat16)
    return (normed, centred, inv_std)


def lat_halo(values):
    return padded_2(values, (("lat", 0),), 3, False)


def lon_halo(values):
    return padded_2(values, (("lon", 1),), 3, True)


def opposite(top_rows, bottom_rows):
    return shifted((top_rows, bottom_rows), "lon", lax.axis_size("lon") // 2)


def widen_rows(values):
    is_first = lax.axis_index("lat") == 0
    is_last = lax.axis_index("lat") == lax.axis_size("lat") - 1
    padded = lat_halo(values)
    top_rows, bottom_rows = opposite(jnp.flip(values[:3], 0), jnp.flip(values[-3:], 0))
    upper_rows = jnp.where(is_first, top_rows, padded[:3])
    lower_rows = jnp.where(is_last, bottom_rows, padded[-3:])
    return jnp.concatenate([upper_rows, padded[3:-3], lower_rows], 0)


def widen_columns(values):
    return lon_halo(values)


def fold_rows(tap_grid):
    is_first = lax.axis_index("lat") == 0
    is_last = lax.axis_index("lat") == lax.axis_size("lat") - 1
    height = tap_grid.shape[0] - 6
    filler = jnp.zeros((height - 6,) + tap_grid.shape[1:], tap_grid.dtype)
    rim_rows = jnp.concatenate([tap_grid[:3], filler, tap_grid[-3:]], 0)
    returned = lat_halo(rim_rows)
    top_rows, bottom_rows = opposite(jnp.flip(tap_grid[:3], 0), jnp.flip(tap_grid[-3:], 0))
    upper_rows = jnp.where(is_first, top_rows, returned[:3])
    lower_rows = jnp.where(is_last, bottom_rows, returned[-3:])
    interior = tap_grid[3:-3]
    return interior.at[:3].add(upper_rows).at[-3:].add(lower_rows)


def fold_columns(tap_grid):
    breadth = tap_grid.shape[1] - 6
    filler = jnp.zeros((tap_grid.shape[0], breadth - 6, tap_grid.shape[2]), tap_grid.dtype)
    rim_cols = jnp.concatenate([tap_grid[:, :3], filler, tap_grid[:, -3:]], 1)
    returned = lon_halo(rim_cols)
    interior = tap_grid[:, 3:-3]
    return interior.at[:, :3].add(returned[:, :3]).at[:, -3:].add(returned[:, -3:])


def apply_taps(extended, depthwise, height, breadth):
    running = jnp.zeros((height, breadth, extended.shape[2]), jnp.float32)
    for row_off in range(7):
        for col_off in range(7):
            running = (
                running
                + depthwise[7 * row_off + col_off]
                * extended[row_off : row_off + height, col_off : col_off + breadth]
            )
    return running


def adjoint_taps(grad_conv, depthwise, height, breadth):
    padded = jnp.pad(grad_conv, ((6, 6), (6, 6), (0, 0)))
    running = jnp.zeros((height + 6, breadth + 6, grad_conv.shape[2]), jnp.float32)
    for row_off in range(7):
        for col_off in range(7):
            running = (
                running
                + depthwise[7 * row_off + col_off]
                * padded[6 - row_off : 12 - row_off + height, 6 - col_off : 12 - col_off + breadth]
            )
    return running


def tap_sums(extended, grad_conv, height, breadth):
    tap_list = []
    for row_off in range(7):
        for col_off in range(7):
            tap_list.append(
                jnp.sum(
                    extended[row_off : row_off + height, col_off : col_off + breadth] * grad_conv,
                    axis=(0, 1),
                )
            )
    return jnp.stack(tap_list, 0)


def body(state_field, cotangent, depthwise, norm_gain, w_in, w_out):
    height, breadth, channels = state_field.shape
    cell_count = height * breadth
    grad_scale = 1.0 / math.sqrt(cell_count * lax.axis_size("lat") * lax.axis_size("lon"))
    extended = widen_columns(widen_rows(state_field))
    convolved = apply_taps(extended, depthwise, height, breadth)
    normed, centred, inv_std = layer_norm(convolved.reshape(cell_count, channels), norm_gain)
    pre_act = jnp.dot(normed, w_in, preferred_element_type=jnp.float32)
    hidden = gelu_value(pre_act).astype(jnp.bfloat16)
    branch = jnp.dot(hidden, w_out, preferred_element_type=jnp.float32)
    block_out = (
        (state_field.reshape(cell_count, channels) + branch)
        .astype(jnp.bfloat16)
        .reshape(height, breadth, channels)
    )
    cot_flat = cotangent.reshape(cell_count, channels)
    grad_hidden = lax.dot_general(
        cot_flat, w_out, (((1,), (1,)), ((), ())), preferred_element_type=jnp.float32
    )
    grad_pre = (grad_hidden * gelu_slope(pre_act)).astype(jnp.bfloat16)
    grad_normed = lax.dot_general(
        grad_pre, w_in, (((1,), (1,)), ((), ())), preferred_element_type=jnp.float32
    )
    scaled_grad = grad_normed * norm_gain
    grad_conv = inv_std * (
        scaled_grad
        - jnp.mean(scaled_grad, axis=-1, keepdims=True)
        - centred * jnp.mean(scaled_grad * centred, axis=-1, keepdims=True)
    )
    gain_local = jnp.sum(grad_normed * centred, axis=0)
    grad_conv = grad_conv.reshape(height, breadth, channels)
    tap_local = tap_sums(extended, grad_conv, height, breadth)
    tap_total, gain_total = lax.psum((tap_local, gain_local), ("lat", "lon"))
    tap_grid = adjoint_taps(grad_conv, depthwise, height, breadth)
    folded = fold_rows(fold_columns(tap_grid))
    grad_input = (cotangent.astype(jnp.float32) + folded).astype(jnp.bfloat16)
    left_part = jnp.einsum("pf,pc->fc", grad_pre, normed, preferred_element_type=jnp.float32)
    right_part = jnp.einsum("pf,pc->fc", hidden, cot_flat, preferred_element_type=jnp.float32)
    weight_grads = lax.psum_scatter(
        jnp.concatenate([left_part, right_part], 1) * grad_scale,
        ("lat", "lon"),
        scatter_dimension=0,
        tiled=True,
    )
    return (block_out, grad_input, weight_grads, tap_total * grad_scale, gain_total * grad_scale)


def solution(mesh):
    placed = (P("lat", "lon", None), P("lat", "lon", None), P(), P(), P(), P())
    return jax.shard_map(
        body,
        mesh=mesh,
        in_specs=placed,
        out_specs=(P("lat", "lon", None), P("lat", "lon", None), P(("lat", "lon"), None), P(), P()),
        check_vma=False,
    )
```

profile of v0, /device:TPU:1, one launch (start us, length us, event | category | flops | bytes accessed | tf_op | source)
XLA Modules:
  0.0 661.3 jit_solution(6647807032486789976)
XLA Ops:
  7.2 0.0 copy-start
  7.2 0.0 all-reduce.5.cloned.1.call-start
  7.2 1.0 fusion.115
  8.3 4.5 collective-permute-start.1
  12.8 4.8 collective-permute-start.2
  17.6 2.7 collective-permute-start.3
  20.3 5.1 collective-permute-start
  25.5 1.0 fusion.116
  26.5 1.0 fusion.117
  27.5 0.0 collective-permute-done.2
  27.6 0.0 collective-permute-done.1
  27.7 2.1 collective-permute-start.4
  29.8 7.1 %collective-permute-start.5 = (f32[18,3,256]{2,1,0:T(4,128)S(1)}, f32[18,3,256]{2,1,0:T(4,128)S(1)}, u32[]{:S(2)}, u32[]{:S(2)}) collective-permute-start(f32[18,3,256]{2,1,0:T(4,128)S(1)} %get-tuple-element.132), channel_id=1, source_target_pairs={{1,0},{2,1},{3,2},{4,3},{5,4},{6,5},{7,6},{8,7},{9,8},{10,9},{11,1... | collective-permute-start | bytes 165896 | tf_op jit(solution)/shard_map/ppermute | solution.py:19
  36.9 0.9 fusion.118
  37.8 1.2 collective-permute-done.4
  39.0 0.0 collective-permute-done.5
  39.1 0.1 maximum_maximum_fusion
  39.2 0.0 copy-start.6
  39.2 2.3 fusion.112
  41.5 0.1 div.17
  41.6 0.2 multiply_reduce_fusion.51
  41.8 0.1 sqrt.6
  41.9 0.1 fusion.107
  42.1 0.0 copy-start.3
  42.1 0.0 copy-start.5
  42.1 0.4 multiply_convert_fusion
  42.5 0.5 copy-done.3
  43.0 0.2 copy-done.5
  43.2 0.6 fusion
  43.8 0.9 multiply_reduce_fusion
  44.8 0.2 subtract_multiply_fusion
  45.0 0.3 multiply_reduce_fusion.4
  45.3 1.1 multiply_reduce_fusion.1
  46.4 0.7 multiply_reduce_fusion.47
  47.1 1.0 multiply_reduce_fusion.5
  48.1 0.5 fusion.110
  48.6 3.4 fusion.99
  52.1 0.5 fusion.119
  52.6 0.2 copy-done.2
  52.8 1.0 fusion.5
  53.8 4.4 stack.199
  58.2 116.4 %all-reduce.2 = (f32[49,256]{1,0:T(8,128)S(1)}, f32[256]{0:T(256)S(1)}) all-reduce(f32[49,256]{1,0:T(8,128)S(1)} %stack.199, f32[256]{0:T(256)} %get-tuple-element.111), channel_id=1, replica_groups=mesh['lat'=32,'lon'=16] {'lat','lon'}, use_global_device_ids=true, to_apply=%region_54.55 | all-reduce | flops 12800 | bytes 102400 | tf_op jit(solution)/shard_map/psum | solution.py:171
  174.5 0.6 broadcast_multiply_fusion
  175.2 2.3 collective-permute-start.7
  177.4 3.0 collective-permute-start.6
  180.5 1.5 maximum_multiply_fusion
  182.0 0.0 all-reduce.5.cloned.1.call-update
  182.0 4.4 collective-permute-done.6
  186.4 0.9 slice_add_fusion.3
  187.4 0.0 copy-start.4
  187.4 0.3 scatter-add.14
  187.6 0.0 collective-permute-done.7
  187.7 0.2 scatter-add.15
  188.0 1.9 collective-permute-start.8
  189.9 4.9 collective-permute-start.9
  194.8 0.6 broadcast_multiply_fusion.4
  195.3 1.9 collective-permute-start.11
  197.3 5.1 collective-permute-start.10
  202.4 0.0 collective-permute-done.8
  202.5 1.7 collective-permute-done.10
  204.2 0.7 add_convert_fusion
  204.9 447.8 %all-reduce.5.cloned.1.call-done = f32[1024,512]{0,1:T(8,128)} async-done(((f32[1024,512]{0,1:T(8,128)}), f32[1024,512]{0,1:T(8,128)}) %all-reduce.5.cloned.1.call-update) | async-done | bytes 2097168
  652.7 1.1 constant_dynamic-slice_fusion
  653.7 0.7 copy.12
  (27 shorter events, 0.3 us)
Async XLA Ops:
  7.2 34.9 %copy-start = (bf16[256,1024]{1,0:T(8,128)(2,1)S(1)}, bf16[256,1024]{1,0:T(8,128)(2,1)}, u32[]{:S(2)}) copy-start(bf16[256,1024]{1,0:T(8,128)(2,1)} %param.18) | copy-start | bytes 1572868
  7.2 20.4 %copy-start.1 = (f32[12,24,256]{2,1,0:T(8,128)S(1)}, f32[12,24,256]{2,1,0:T(8,128)}, u32[]{:S(2)}) copy-start(f32[12,24,256]{2,1,0:T(8,128)} %param.14) | copy-start | bytes 884740
  7.2 645.5 %all-reduce.5.cloned.1.call-start = ((), (), s32[]{:S(2)}) async-start(), calls=%async_computation | async-start | bytes 4194304
  8.3 19.3 %collective-permute-start.1 = (f32[3,24,256]{2,1,0:T(8,128)S(1)}, f32[3,24,256]{2,1,0:T(8,128)S(1)}, u32[]{:S(2)}, u32[]{:S(2)}) collective-permute-start(f32[3,24,256]{2,1,0:T(8,128)S(1)} %get-tuple-element.134), channel_id=1, source_target_pairs={{0,16},{16,32},{32,48},{48,64},{64,80},{80,96},{96,112},{112,128},... | collective-permute-start | bytes 221192 | tf_op jit(solution)/shard_map/ppermute | solution.py:17
  12.8 14.8 %collective-permute-start.2 = (f32[3,24,256]{2,1,0:T(8,128)S(1)}, f32[3,24,256]{2,1,0:T(8,128)S(1)}, u32[]{:S(2)}, u32[]{:S(2)}) collective-permute-start(f32[3,24,256]{2,1,0:T(8,128)S(1)} %rev.14), channel_id=1, source_target_pairs={{0,8},{1,9},{2,10},{3,11},{4,12},{5,13},{6,14},{7,15},{8,0},{9,1},... | collective-permute-start | bytes 221192 | tf_op jit(solution)/shard_map/ppermute | solution.py:28
  17.6 9.9 %collective-permute-start.3 = (f32[3,24,256]{2,1,0:T(8,128)S(1)}, f32[3,24,256]{2,1,0:T(8,128)S(1)}, u32[]{:S(2)}, u32[]{:S(2)}) collective-permute-start(f32[3,24,256]{2,1,0:T(8,128)S(1)} %get-tuple-element.133), channel_id=1, source_target_pairs={{16,0},{32,16},{48,32},{64,48},{80,64},{96,80},{112,96},{128,112},... | collective-permute-start | bytes 221192 | tf_op jit(solution)/shard_map/ppermute | solution.py:19
  20.3 7.3 %collective-permute-start = (f32[3,24,256]{2,1,0:T(8,128)S(1)}, f32[3,24,256]{2,1,0:T(8,128)S(1)}, u32[]{:S(2)}, u32[]{:S(2)}) collective-permute-start(f32[3,24,256]{2,1,0:T(8,128)S(1)} %rev.13), channel_id=1, source_target_pairs={{0,8},{1,9},{2,10},{3,11},{4,12},{5,13},{6,14},{7,15},{8,0},{9,1},... | collective-permute-start | bytes 221192 | tf_op jit(solution)/shard_map/ppermute | solution.py:28
  27.7 11.4 %collective-permute-start.4 = (f32[18,3,256]{2,1,0:T(4,128)S(1)}, f32[18,3,256]{2,1,0:T(4,128)S(1)}, u32[]{:S(2)}, u32[]{:S(2)}) collective-permute-start(f32[18,3,256]{2,1,0:T(4,128)S(1)} %get-tuple-element.131), channel_id=1, source_target_pairs={{0,1},{1,2},{2,3},{3,4},{4,5},{5,6},{6,7},{7,8},{8,9},{9,10},{10,1... | collective-permute-start | bytes 165896 | tf_op jit(solution)/shard_map/ppermute | solution.py:17
  29.8 9.3 %collective-permute-start.5 = (f32[18,3,256]{2,1,0:T(4,128)S(1)}, f32[18,3,256]{2,1,0:T(4,128)S(1)}, u32[]{:S(2)}, u32[]{:S(2)}) collective-permute-start(f32[18,3,256]{2,1,0:T(4,128)S(1)} %get-tuple-element.132), channel_id=1, source_target_pairs={{1,0},{2,1},{3,2},{4,3},{5,4},{6,5},{7,6},{8,7},{9,8},{10,9},{11,1... | collective-permute-start | bytes 165896 | tf_op jit(solution)/shard_map/ppermute | solution.py:19
  39.2 2.9 copy-start.6
  42.1 0.9 copy-start.3
  42.1 1.1 copy-start.5
  52.0 0.8 copy-start.2
  175.2 12.5 %collective-permute-start.7 = (f32[18,3,256]{2,1,0:T(4,128)S(1)}, f32[18,3,256]{2,1,0:T(4,128)S(1)}, u32[]{:S(2)}, u32[]{:S(2)}) collective-permute-start(f32[18,3,256]{2,1,0:T(4,128)S(1)} %get-tuple-element.125), channel_id=1, source_target_pairs={{1,0},{2,1},{3,2},{4,3},{5,4},{6,5},{7,6},{8,7},{9,8},{10,9},{11,1... | collective-permute-start | bytes 165896 | tf_op jit(solution)/shard_map/ppermute | solution.py:19
  177.4 9.0 %collective-permute-start.6 = (f32[18,3,256]{2,1,0:T(4,128)S(1)}, f32[18,3,256]{2,1,0:T(4,128)S(1)}, u32[]{:S(2)}, u32[]{:S(2)}) collective-permute-start(f32[18,3,256]{2,1,0:T(4,128)S(1)} %get-tuple-element.126), channel_id=1, source_target_pairs={{0,1},{1,2},{2,3},{3,4},{4,5},{5,6},{6,7},{7,8},{8,9},{9,10},{10,1... | collective-permute-start | bytes 165896 | tf_op jit(solution)/shard_map/ppermute | solution.py:17
  187.4 16.8 %copy-start.4 = (bf16[12,24,256]{2,1,0:T(8,128)(2,1)S(1)}, bf16[12,24,256]{2,1,0:T(8,128)(2,1)}, u32[]{:S(2)}) copy-start(bf16[12,24,256]{2,1,0:T(8,128)(2,1)} %param.15) | copy-start | bytes 442372
  188.0 14.5 %collective-permute-start.8 = (f32[3,24,256]{2,1,0:T(8,128)S(1)}, f32[3,24,256]{2,1,0:T(8,128)S(1)}, u32[]{:S(2)}, u32[]{:S(2)}) collective-permute-start(f32[3,24,256]{2,1,0:T(8,128)S(1)} %rev.15), channel_id=1, source_target_pairs={{0,8},{1,9},{2,10},{3,11},{4,12},{5,13},{6,14},{7,15},{8,0},{9,1},... | collective-permute-start | bytes 221192 | tf_op jit(solution)/shard_map/ppermute | solution.py:28
  189.9 12.6 %collective-permute-start.9 = (f32[3,24,256]{2,1,0:T(8,128)S(1)}, f32[3,24,256]{2,1,0:T(8,128)S(1)}, u32[]{:S(2)}, u32[]{:S(2)}) collective-permute-start(f32[3,24,256]{2,1,0:T(8,128)S(1)} %get-tuple-element.127), channel_id=1, source_target_pairs={{0,16},{16,32},{32,48},{48,64},{64,80},{80,96},{96,112},{112,128},... | collective-permute-start | bytes 221192 | tf_op jit(solution)/shard_map/ppermute | solution.py:17
  195.3 8.8 %collective-permute-start.11 = (f32[3,24,256]{2,1,0:T(8,128)S(1)}, f32[3,24,256]{2,1,0:T(8,128)S(1)}, u32[]{:S(2)}, u32[]{:S(2)}) collective-permute-start(f32[3,24,256]{2,1,0:T(8,128)S(1)} %get-tuple-element.128), channel_id=1, source_target_pairs={{16,0},{32,16},{48,32},{64,48},{80,64},{96,80},{112,96},{128,112},... | collective-permute-start | bytes 221192 | tf_op jit(solution)/shard_map/ppermute | solution.py:19
  197.3 6.9 %collective-permute-start.10 = (f32[3,24,256]{2,1,0:T(8,128)S(1)}, f32[3,24,256]{2,1,0:T(8,128)S(1)}, u32[]{:S(2)}, u32[]{:S(2)}) collective-permute-start(f32[3,24,256]{2,1,0:T(8,128)S(1)} %rev.16), channel_id=1, source_target_pairs={{0,8},{1,9},{2,10},{3,11},{4,12},{5,13},{6,14},{7,15},{8,0},{9,1},... | collective-permute-start | bytes 221192 | tf_op jit(solution)/shard_map/ppermute | solution.py:28
Sparse Core Ops, SparseCore 0:
  182.1 470.5 all-reduce.4
where the time goes:
time: 662 us; the launch traced here: 661 us
  waiting for transfers between devices  455 us (69%)
  blocking collectives  116 us (18%)
  starting transfers between devices  45.5 us (7%)
  between operations  14.5 us (2%)
  other arithmetic  14 us (2%)
  local copies, waits for them, and re-layouts  11.9 us (2%)
    unnamed x2, waiting for transfers between devices  448 us
    psum x1, blocking collectives, body(): tap_total, gain_total = lax.psum((tap_local, gain_local), ('lat', 'lon'))  116 us
    ppermute x4, starting transfers between devices, shifted(): lax.ppermute(value, axis, [(i, (i + by) % peers) for i in range(peers)])  17 us
    ppermute x4, starting transfers between devices, padded_2(): lax.ppermute(tail, axis, [(i, (i + 1) % count) for i in range(ends)])  14.5 us
    ppermute x4, starting transfers between devices, padded_2(): lax.ppermute(head, axis, [((i + 1) % count, i) for i in range(ends)])  13.9 us
  transfers between devices with their start and end apart: 13, of which 4 were waited for; matrix products, arithmetic and copies ran while one was open for 1% of the time, Pallas kernels for 0%

commit v1 on v0

v1 whole, which is shorter than its diff:
```python
import math

import jax
import jax.numpy as jnp
from jax import lax
from jax.sharding import Mesh, PartitionSpec as P

AXES = ("zh", "x", "core", "y", "zl")
SIZES = (4, 4, 2, 4, 4)
LAT = 32
LON = 16


def gelu_value(values):
    return 0.5 * values * (1.0 + lax.erf(values * 0.7071067811865476))


def gelu_slope(values):
    return (
        0.5 * (1.0 + lax.erf(values * 0.7071067811865476))
        + values * jnp.exp(-0.5 * values * values) * 0.3989422804014327
    )


def layer_norm(convolved, norm_gain):
    average = jnp.mean(convolved, axis=-1, keepdims=True)
    centred_raw = convolved - average
    variance = jnp.mean(centred_raw * centred_raw, axis=-1, keepdims=True)
    inv_std = 1.0 / jnp.sqrt(variance + 1e-06)
    centred = centred_raw * inv_std
    normed = (centred * norm_gain).astype(jnp.bfloat16)
    return (normed, centred, inv_std)


def lat_lon():
    lat = (lax.axis_index("zh") * 4 + lax.axis_index("x")) * 2 + lax.axis_index("core")
    return lat, lax.axis_index("y") * 4 + lax.axis_index("zl")


def row_pairs():
    first, second = [], []
    for lat in range(LAT):
        for lon in range(LON):
            here = lat * LON + lon
            first.append((here, (lat ^ 1) * LON + lon))
            if lat == 0 or lat == LAT - 1:
                peer = lat * LON + (lon + LON // 2) % LON
            else:
                peer = (lat - 1 if lat % 2 == 0 else lat + 1) * LON + lon
            second.append((here, peer))
    return first, second


def column_pairs():
    right, left = [], []
    for lat in range(LAT):
        for lon in range(LON):
            here = lat * LON + lon
            right.append((here, lat * LON + (lon + 1) % LON))
            left.append((here, lat * LON + (lon - 1) % LON))
    return right, left


def halo(values):
    lat, _ = lat_lon()
    even = lat % 2 == 0
    pole = (lat == 0) | (lat == LAT - 1)
    head, tail = values[:3], values[-3:]
    first, second = row_pairs()
    outer = jnp.where(even, head, tail)
    outer = jnp.where(pole, jnp.flip(outer, 0), outer)
    got_first = lax.ppermute(jnp.where(even, tail, head), AXES, first)
    got_second = lax.ppermute(outer, AXES, second)
    above = jnp.where(even, got_second, got_first)
    below = jnp.where(even, got_first, got_second)
    tall = jnp.concatenate([above, values, below], 0)
    right, left = column_pairs()
    before = lax.ppermute(tall[:, -3:], AXES, right)
    after = lax.ppermute(tall[:, :3], AXES, left)
    return jnp.concatenate([before, tall, after], 1)


def apply_taps(extended, depthwise, height, breadth):
    running = jnp.zeros((height, breadth, extended.shape[2]), jnp.float32)
    for row_off in range(7):
        for col_off in range(7):
            running = (
                running
                + depthwise[7 * row_off + col_off]
                * extended[row_off : row_off + height, col_off : col_off + breadth]
            )
    return running


def adjoint_taps(wide, depthwise, height, breadth):
    lat, _ = lat_lon()
    taps = depthwise.reshape(7, 7, -1)
    flipped = jnp.flip(taps, 0)
    upper = jnp.where(lat == 0, flipped, taps)
    lower = jnp.where(lat == LAT - 1, flipped, taps)
    rows = wide.shape[0]
    running = jnp.zeros((height, breadth, wide.shape[2]), jnp.float32)
    for row_off in range(7):
        start = 6 - row_off
        for col_off in range(7):
            weight = []
            for i in range(height):
                r = i + start
                weight.append(
                    (upper if r < 3 else lower if r >= rows - 3 else taps)[row_off, col_off]
                )
            weight = jnp.stack(weight, 0)[:, None, :]
            running = running + weight * wide[start : start + height, 6 - col_off : 6 - col_off + breadth]
    return running


def tap_sums(extended, grad_conv, height, breadth):
    tap_list = []
    for row_off in range(7):
        for col_off in range(7):
            tap_list.append(
                jnp.sum(
                    extended[row_off : row_off + height, col_off : col_off + breadth] * grad_conv,
                    axis=(0, 1),
                )
            )
    return tap_list


def body(state_field, cotangent, depthwise, norm_gain, w_in, w_out):
    height, breadth, channels = state_field.shape
    units = w_in.shape[1]
    cell_count = height * breadth
    grad_scale = 1.0 / math.sqrt(cell_count * LAT * LON)
    extended = halo(state_field)
    convolved = apply_taps(extended, depthwise, height, breadth)
    normed, centred, inv_std = layer_norm(convolved.reshape(cell_count, channels), norm_gain)
    pre_act = jnp.dot(normed, w_in, preferred_element_type=jnp.float32)
    hidden = gelu_value(pre_act).astype(jnp.bfloat16)
    branch = jnp.dot(hidden, w_out, preferred_element_type=jnp.float32)
    block_out = (
        (state_field.reshape(cell_count, channels) + branch)
        .astype(jnp.bfloat16)
        .reshape(height, breadth, channels)
    )
    cot_flat = cotangent.reshape(cell_count, channels)
    grad_hidden = lax.dot_general(
        cot_flat, w_out, (((1,), (1,)), ((), ())), preferred_element_type=jnp.float32
    )
    grad_pre = (grad_hidden * gelu_slope(pre_act)).astype(jnp.bfloat16)
    grad_normed = lax.dot_general(
        grad_pre, w_in, (((1,), (1,)), ((), ())), preferred_element_type=jnp.float32
    )
    scaled_grad = grad_normed * norm_gain
    grad_conv = inv_std * (
        scaled_grad
        - jnp.mean(scaled_grad, axis=-1, keepdims=True)
        - centred * jnp.mean(scaled_grad * centred, axis=-1, keepdims=True)
    )
    gain_local = jnp.sum(grad_normed * centred, axis=0)
    left_part = jnp.einsum("pf,pc->fc", grad_pre, normed, preferred_element_type=jnp.float32)
    right_part = jnp.einsum("pf,pc->fc", hidden, cot_flat, preferred_element_type=jnp.float32)
    local = jnp.concatenate([left_part, right_part], 1)
    local = local.reshape(4, 4, 2, 4, 8, 4, 128).transpose(2, 1, 3, 5, 0, 4, 6)
    local = local.reshape(2, 16, 128, 128)
    core = lax.axis_index("core")
    theirs = lax.ppermute(jnp.where(core == 0, local[1], local[0]), "core", [(0, 1), (1, 0)])
    mine = jnp.where(core == 0, local[0], local[1]) + theirs

    grad_conv = grad_conv.reshape(height, breadth, channels)
    taps = jnp.stack(
        tap_sums(extended, grad_conv, height, breadth)
        + [gain_local]
        + [jnp.zeros_like(gain_local)] * 14,
        0,
    ).reshape(16, 8, 128)
    wide = halo(grad_conv)
    grad_input = (
        cotangent.astype(jnp.float32) + adjoint_taps(wide, depthwise, height, breadth)
    ).astype(jnp.bfloat16)

    plane = lax.all_to_all(
        jnp.concatenate([mine, taps], 1), ("x", "y"), split_axis=0, concat_axis=0, tiled=True
    ).sum(0)
    rest = plane[:128].reshape(4, 4, 4, 2, 128).transpose(1, 2, 0, 3, 4).reshape(16, 8, 128)
    column = lax.all_to_all(
        jnp.concatenate([rest, jnp.broadcast_to(plane[128:], (16, 8, 128))], 1),
        ("zh", "zl"),
        split_axis=0,
        concat_axis=0,
        tiled=True,
    ).sum(0)
    weight_grads = column[:8].reshape(4, 2, 128).transpose(1, 0, 2).reshape(2, 512) * grad_scale
    shared = lax.all_to_all(
        jnp.broadcast_to(column[8:], (32, 8, 128)),
        ("x", "core", "y"),
        split_axis=0,
        concat_axis=0,
        tiled=True,
    )
    totals = shared.reshape(4, 2, 4, 8, 128).sum(1).reshape(64, 256) * grad_scale
    return (block_out, grad_input, weight_grads, totals[:49], totals[49])


def solution(mesh):
    split = Mesh(mesh.devices.reshape(SIZES), AXES)
    cells = P(("zh", "x", "core"), ("y", "zl"), None)
    return jax.shard_map(
        body,
        mesh=split,
        in_specs=(cells, cells, P(), P(), P(), P()),
        out_specs=(cells, cells, P(AXES, None), P(), P()),
        check_vma=False,
    )
```

time: 662 us -> 196 us (0.30)
  waiting for transfers between devices: 455 us -> 9.63 us
  blocking collectives: 116 us -> 0 us
  local copies, waits for them, and re-layouts: 11.9 us -> 90.9 us
  starting transfers between devices: 45.5 us -> 66.2 us
  between operations: 14.5 us -> 1.98 us
    unnamed x2 -> x0, waiting for transfers between devices: 448 us -> none
    psum x1 -> x0, blocking collectives: 116 us -> none  [body(): tap_total, gain_total = lax.psum((tap_local, gain_local), ('lat', 'lon'))]
    another operation x1 -> x52, local copies, waits for them, and re-layouts: 4.36 us -> 80.2 us  [the longest x48 75.1 us: adjoint_taps(): weight = jnp.stack(weight, 0)[:, None, :]]
    all_to_all x0 -> x3, starting transfers between devices: none -> 26.6 us  [the longest x1 13.9 us: body(): lax.all_to_all(jnp.concatenate([rest, jnp.broadcast_to(plane[128:], (16,...]
    ppermute x12 -> x9, starting transfers between devices: 45.4 us -> 39.6 us  [the longest x2 14.4 us: halo(): after = lax.ppermute(tall[:, :3], AXES, left)]
  transfers between devices with their start and end apart: 13 -> 12, of which waited for: 4 -> 3; matrix products, arithmetic and copies ran while one was open for 1% -> 48% of each run, Pallas kernels for 0% -> 0%
where the time goes in v1:
time: 196 us; the launch traced here: 194 us
  local copies, waits for them, and re-layouts  90.9 us (46%)
  starting transfers between devices  66.2 us (34%)
  other arithmetic  19.9 us (10%)
  waiting for transfers between devices  9.63 us (5%)
  matrix products  5.32 us (3%)
  between operations  1.98 us (1%)
    another operation x48, local copies, waits for them, and re-layouts, adjoint_taps(): weight = jnp.stack(weight, 0)[:, None, :]  75.1 us
    ppermute x2, starting transfers between devices, halo(): after = lax.ppermute(tall[:, :3], AXES, left)  14.4 us
    all_to_all x1, starting transfers between devices, body(): lax.all_to_all(jnp.concatenate([rest, jnp.broadcast_to(plane[128:], (16,...  13.9 us
    ppermute x2, starting transfers between devices, halo(): got_first = lax.ppermute(jnp.where(even, tail, head), AXES, first)  10 us
    ppermute x2, starting transfers between devices, halo(): got_second = lax.ppermute(outer, AXES, second)  8.24 us
    all_to_all x1, starting transfers between devices, body(): lax.all_to_all(jnp.concatenate([mine, taps], 1), ('x', 'y'), split_axis=0...  7.15 us
    ppermute x2, waiting for transfers between devices, halo(): before = lax.ppermute(tall[:, -3:], AXES, right)  5.8 us
    all_to_all x1, starting transfers between devices, body(): lax.all_to_all(jnp.broadcast_to(column[8:], (32, 8, 128)), ('x', 'core',...  5.52 us
  transfers between devices with their start and end apart: 12, of which 3 were waited for; matrix products, arithmetic and copies ran while one was open for 48% of the time, Pallas kernels for 0%

profile of v1, /device:TPU:1, one launch (start us, length us, event | category | flops | bytes accessed | tf_op | source)
XLA Modules:
  0.0 194.0 jit_solution(13491670517623111476)
XLA Ops:
  1.7 4.5 %collective-permute-start = (f32[3,24,256]{2,1,0:T(8,128)S(1)}, f32[3,24,256]{2,1,0:T(8,128)S(1)}, u32[]{:S(2)}, u32[]{:S(2)}) collective-permute-start(f32[3,24,256]{2,1,0:T(8,128)S(1)} %reverse_select_fusion.3), channel_id=1, source_target_pairs={{0,8},{1,9},{2,10},{3,11},{4,12},{5,13},{6,14},{7,15},{8,0},{9,1},... | collective-permute-start | bytes 221192 | tf_op jit(solution)/shard_map/ppermute | solution.py:73
  6.2 6.2 %collective-permute-start.1 = (f32[3,24,256]{2,1,0:T(8,128)S(1)}, f32[3,24,256]{2,1,0:T(8,128)S(1)}, u32[]{:S(2)}, u32[]{:S(2)}) collective-permute-start(f32[3,24,256]{2,1,0:T(8,128)S(1)} %get-tuple-element.78), channel_id=1, source_target_pairs={{0,16},{1,17},{2,18},{3,19},{4,20},{5,21},{6,22},{7,23},{8,24},{9,... | collective-permute-start | bytes 221192 | tf_op jit(solution)/shard_map/ppermute | solution.py:72
  18.0 1.9 collective-permute-start.2
  19.9 7.3 %collective-permute-start.3 = (f32[18,3,256]{2,1,0:T(4,128)S(1)}, f32[18,3,256]{2,1,0:T(4,128)S(1)}, u32[]{:S(2)}, u32[]{:S(2)}) collective-permute-start(f32[18,3,256]{2,1,0:T(4,128)S(1)} %get-tuple-element.74), channel_id=1, source_target_pairs={{0,15},{1,0},{2,1},{3,2},{4,3},{5,4},{6,5},{7,6},{8,7},{9,8},{10,9... | collective-permute-start | bytes 165896 | tf_op jit(solution)/shard_map/ppermute | solution.py:79
  28.7 2.3 %fusion.73 = (f32[12,24]{1,0:T(8,128)S(1)}, f32[12,24,256]{2,1,0:T(8,128)S(1)}) fusion(f32[18,27,256]{2,1,0:T(8,128)S(1)} %get-tuple-element.72, f32[256]{0:T(256)S(1)} %bitcast.433, f32[256]{0:T(256)S(1)} %bitcast.386, f32[256]{0:T(256)S(1)} %bitcast.387, f32[3,24,256]{2,1,0:T(8,128)S(1)} %get-tuple-element.82, f32[12,24,256]{2,1,0:T(8,128)S(1)} %copy-done.1, ...), kind=kLoop, calls=%fused_computation.314 | loop fusion | flops 7667424 | bytes 13174912 | tf_op jit(solution)/shard_map/reduce_sum | solution.py:26
  31.9 1.1 multiply_convert_fusion
  33.8 1.6 multiply_reduce_fusion
  36.4 1.4 pad_maximum_fusion
  37.8 2.9 %copy.18 = f32[1024,512]{1,0:T(8,128)} copy(f32[1024,512]{0,1:T(8,128)} %pad_maximum_fusion) | data formatting | bytes 4194304 | tf_op jit(solution)/shard_map/concatenate | solution.py:163
  40.8 2.8 %slice_select_fusion = (f32[1,4,4,4,4,8,128]{6,5,3,2,0,1,4:T(8,128)S(1)}, f32[1,4,4,4,4,8,128]{6,5,3,2,0,1,4:T(8,128)}) fusion(f32[2,4,4,4,4,8,128]{6,5,3,2,0,1,4:T(8,128)} %bitcast.322, pred[]{:T(512)S(6)} %eq.24), kind=kLoop, calls=%fused_computation.13 | loop fusion | flops 524288 | bytes 4194305 | tf_op jit(solution)/shard_map/jit(_where)/select_n | solution.py:167
  43.6 1.1 copy.20
  44.7 3.0 %collective-permute-start.8 = (f32[16,128,128]{2,1,0:T(8,128)}, f32[16,128,128]{2,1,0:T(8,128)}, u32[]{:S(2)}, u32[]{:S(2)}) collective-permute-start(f32[16,128,128]{2,1,0:T(8,128)} %bitcast.151), channel_id=1, source_target_pairs={{0,16},{16,0},{1,17},{17,1},{2,18},{18,2},{3,19},{19,3},{4,20},{20... | collective-permute-start | bytes 3145736 | tf_op jit(solution)/shard_map/ppermute | solution.py:167
  49.6 1.1 multiply_reduce_fusion.5
  50.6 1.1 multiply_reduce_fusion.1
  51.8 5.1 %stack.390 = f32[64,256]{1,0:T(8,128)S(1)} concatenate(f32[1,256]{1,0:T(1,128)} %bitcast.438, f32[1,256]{1,0:T(1,128)} %bitcast.437, f32[1,256]{1,0:T(1,128)} %bitcast.436, f32[1,256]{1,0:T(1,128)} %bitcast.336, f32[1,256]{1,0:T(1,128)} %bitcast.339, f32[1,256]{1,0:T(1,128)} %bitcast.340, f32[1,256]{1,0:T(1,128)} %bitcast.341, f32[1,256]{1,0:T(1,128)} %bitcast.359, ...), dimensions={0} | concatenate | bytes 131072 | tf_op jit(solution)/shard_map/stack | solution.py:171
  57.0 1.3 add.436
  58.3 1.1 pad_maximum_fusion.1
  59.5 7.1 %all-to-all-start = ((f32[16,136,128]{2,1,0:T(8,128)}), f32[16,136,128]{2,1,0:T(8,128)S(1)}, u32[]{:S(2)}, u32[]{:S(2)}) async-start(f32[16,136,128]{2,1,0:T(8,128)} %pad_maximum_fusion.1), calls=%async_computation | async-start | bytes 2228224 | tf_op jit(solution)/shard_map/all_to_all | solution.py:182
  67.4 3.7 %collective-permute-start.4 = (f32[3,24,256]{2,1,0:T(8,128)S(1)}, f32[3,24,256]{2,1,0:T(8,128)S(1)}, u32[]{:S(2)}, u32[]{:S(2)}) collective-permute-start(f32[3,24,256]{2,1,0:T(8,128)S(1)} %reverse_select_fusion.2), channel_id=1, source_target_pairs={{0,8},{1,9},{2,10},{3,11},{4,12},{5,13},{6,14},{7,15},{8,0},{9,1},... | collective-permute-start | bytes 221192 | tf_op jit(solution)/shard_map/ppermute | solution.py:73
  71.1 3.8 %collective-permute-start.5 = (f32[3,24,256]{2,1,0:T(8,128)S(1)}, f32[3,24,256]{2,1,0:T(8,128)S(1)}, u32[]{:S(2)}, u32[]{:S(2)}) collective-permute-start(f32[3,24,256]{2,1,0:T(8,128)S(1)} %bitcast.331), channel_id=1, source_target_pairs={{0,16},{1,17},{2,18},{3,19},{4,20},{5,21},{6,22},{7,23},{8,24},{9,... | collective-permute-start | bytes 221192 | tf_op jit(solution)/shard_map/ppermute | solution.py:72
  78.3 2.0 %stack.332 = f32[12,256]{1,0:T(8,128)} concatenate(f32[1,256]{1,0:T(1,128)} %get-tuple-element.160, f32[1,256]{1,0:T(1,128)} %get-tuple-element.160, f32[1,256]{1,0:T(1,128)} %get-tuple-element.160, f32[1,256]{1,0:T(1,128)S(1)} %copy-done.20, f32[1,256]{1,0:T(1,128)S(1)} %copy-done.20, f32[1,256]{1,0:T(1,128)S(1)} %copy-done.20, f32[1,256]{1,0:T(1,128)S(1)} %copy-done.20, ...), dimensions={0} | concatenate | bytes 24576 | tf_op jit(solution)/shard_map/stack | solution.py:112
  80.3 2.0 %stack.331 = f32[12,256]{1,0:T(8,128)} concatenate(f32[1,256]{1,0:T(1,128)} %get-tuple-element.161, f32[1,256]{1,0:T(1,128)} %get-tuple-element.161, f32[1,256]{1,0:T(1,128)} %get-tuple-element.161, f32[1,256]{1,0:T(1,128)S(1)} %copy-done.19, f32[1,256]{1,0:T(1,128)S(1)} %copy-done.19, f32[1,256]{1,0:T(1,128)S(1)} %copy-done.19, f32[1,256]{1,0:T(1,128)S(1)} %copy-done.19, ...), dimensions={0} | concatenate | bytes 24576 | tf_op jit(solution)/shard_map/stack | solution.py:112
  82.4 2.0 %stack.330 = f32[12,256]{1,0:T(8,128)} concatenate(f32[1,256]{1,0:T(1,128)} %get-tuple-element.162, f32[1,256]{1,0:T(1,128)} %get-tuple-element.162, f32[1,256]{1,0:T(1,128)} %get-tuple-element.162, f32[1,256]{1,0:T(1,128)S(1)} %copy-done.18, f32[1,256]{1,0:T(1,128)S(1)} %copy-done.18, f32[1,256]{1,0:T(1,128)S(1)} %copy-done.18, f32[1,256]{1,0:T(1,128)S(1)} %copy-done.18, ...), dimensions={0} | concatenate | bytes 24576 | tf_op jit(solution)/shard_map/stack | solution.py:112
  84.3 1.9 stack.329
  86.3 2.0 %stack.328 = f32[12,256]{1,0:T(8,128)} concatenate(f32[1,256]{1,0:T(1,128)} %get-tuple-element.164, f32[1,256]{1,0:T(1,128)} %get-tuple-element.164, f32[1,256]{1,0:T(1,128)S(1)} %copy-done.15, f32[1,256]{1,0:T(1,128)S(1)} %copy-done.15, f32[1,256]{1,0:T(1,128)S(1)} %copy-done.15, f32[1,256]{1,0:T(1,128)S(1)} %copy-done.15, f32[1,256]{1,0:T(1,128)S(1)} %copy-done.15, ...), dimensions={0} | concatenate | bytes 24576 | tf_op jit(solution)/shard_map/stack | solution.py:112
  88.2 2.0 %stack.327 = f32[12,256]{1,0:T(8,128)} concatenate(f32[1,256]{1,0:T(1,128)} %get-tuple-element.165, f32[1,256]{1,0:T(1,128)} %get-tuple-element.165, f32[1,256]{1,0:T(1,128)S(1)} %copy-done.14, f32[1,256]{1,0:T(1,128)S(1)} %copy-done.14, f32[1,256]{1,0:T(1,128)S(1)} %copy-done.14, f32[1,256]{1,0:T(1,128)S(1)} %copy-done.14, f32[1,256]{1,0:T(1,128)S(1)} %copy-done.14, ...), dimensions={0} | concatenate | bytes 24576 | tf_op jit(solution)/shard_map/stack | solution.py:112
  90.2 2.0 %stack.326 = f32[12,256]{1,0:T(8,128)} concatenate(f32[1,256]{1,0:T(1,128)} %get-tuple-element.166, f32[1,256]{1,0:T(1,128)} %get-tuple-element.166, f32[1,256]{1,0:T(1,128)S(1)} %copy-done.13, f32[1,256]{1,0:T(1,128)S(1)} %copy-done.13, f32[1,256]{1,0:T(1,128)S(1)} %copy-done.13, f32[1,256]{1,0:T(1,128)S(1)} %copy-done.13, f32[1,256]{1,0:T(1,128)S(1)} %copy-done.13, ...), dimensions={0} | concatenate | bytes 24576 | tf_op jit(solution)/shard_map/stack | solution.py:112
  92.2 1.9 stack.325
  94.1 2.0 %stack.324 = f32[12,256]{1,0:T(8,128)} concatenate(f32[1,256]{1,0:T(1,128)} %get-tuple-element.168, f32[1,256]{1,0:T(1,128)} %get-tuple-element.168, f32[1,256]{1,0:T(1,128)S(1)} %copy-done.11, f32[1,256]{1,0:T(1,128)S(1)} %copy-done.11, f32[1,256]{1,0:T(1,128)S(1)} %copy-done.11, f32[1,256]{1,0:T(1,128)S(1)} %copy-done.11, f32[1,256]{1,0:T(1,128)S(1)} %copy-done.11, ...), dimensions={0} | concatenate | bytes 24576 | tf_op jit(solution)/shard_map/stack | solution.py:112
  96.1 1.9 stack.323
  98.0 1.9 stack.322
  99.9 1.9 stack.321
  101.8 1.9 stack.320
  103.7 1.9 stack.319
  105.5 1.9 stack.318
  108.2 1.9 stack.316
  110.1 1.9 stack.315
  111.9 1.9 stack.314
  113.8 1.9 stack.313
  115.7 1.9 stack.312
  117.6 1.9 stack.311
  119.5 1.9 stack.310
  121.3 1.8 stack.309
  123.1 2.0 %stack.308 = f32[12,256]{1,0:T(8,128)} concatenate(f32[1,256]{1,0:T(1,128)S(1)} %get-tuple-element.140, f32[1,256]{1,0:T(1,128)S(1)} %get-tuple-element.140, f32[1,256]{1,0:T(1,128)S(1)} %get-tuple-element.140, f32[1,256]{1,0:T(1,128)S(1)} %get-tuple-element.140, f32[1,256]{1,0:T(1,128)S(1)} %get-tuple-element.140, f32[1,256]{1,0:T(1,128)S(1)} %get-tuple-element.140, ...), dimensions={0} | concatenate | bytes 24576 | tf_op jit(solution)/shard_map/stack | solution.py:112
  125.1 2.0 %stack.307 = f32[12,256]{1,0:T(8,128)} concatenate(f32[1,256]{1,0:T(1,128)S(1)} %get-tuple-element.141, f32[1,256]{1,0:T(1,128)S(1)} %get-tuple-element.141, f32[1,256]{1,0:T(1,128)S(1)} %get-tuple-element.141, f32[1,256]{1,0:T(1,128)S(1)} %get-tuple-element.141, f32[1,256]{1,0:T(1,128)S(1)} %get-tuple-element.141, f32[1,256]{1,0:T(1,128)S(1)} %get-tuple-element.141, ...), dimensions={0} | concatenate | bytes 24576 | tf_op jit(solution)/shard_map/stack | solution.py:112
  127.1 2.0 %stack.306 = f32[12,256]{1,0:T(8,128)} concatenate(f32[1,256]{1,0:T(1,128)S(1)} %get-tuple-element.143, f32[1,256]{1,0:T(1,128)S(1)} %get-tuple-element.143, f32[1,256]{1,0:T(1,128)S(1)} %get-tuple-element.143, f32[1,256]{1,0:T(1,128)S(1)} %get-tuple-element.143, f32[1,256]{1,0:T(1,128)S(1)} %get-tuple-element.143, f32[1,256]{1,0:T(1,128)S(1)} %get-tuple-element.143, ...), dimensions={0} | concatenate | bytes 24576 | tf_op jit(solution)/shard_map/stack | solution.py:112
  129.0 2.0 %stack.305 = f32[12,256]{1,0:T(8,128)} concatenate(f32[1,256]{1,0:T(1,128)S(1)} %get-tuple-element.144, f32[1,256]{1,0:T(1,128)S(1)} %get-tuple-element.144, f32[1,256]{1,0:T(1,128)S(1)} %get-tuple-element.144, f32[1,256]{1,0:T(1,128)S(1)} %get-tuple-element.144, f32[1,256]{1,0:T(1,128)S(1)} %get-tuple-element.144, f32[1,256]{1,0:T(1,128)S(1)} %get-tuple-element.144, ...), dimensions={0} | concatenate | bytes 24576 | tf_op jit(solution)/shard_map/stack | solution.py:112
  131.0 2.0 %stack.304 = f32[12,256]{1,0:T(8,128)} concatenate(f32[1,256]{1,0:T(1,128)S(1)} %get-tuple-element.145, f32[1,256]{1,0:T(1,128)S(1)} %get-tuple-element.145, f32[1,256]{1,0:T(1,128)S(1)} %get-tuple-element.145, f32[1,256]{1,0:T(1,128)S(1)} %get-tuple-element.145, f32[1,256]{1,0:T(1,128)S(1)} %get-tuple-element.145, f32[1,256]{1,0:T(1,128)S(1)} %get-tuple-element.145, ...), dimensions={0} | concatenate | bytes 24576 | tf_op jit(solution)/shard_map/stack | solution.py:112
  133.0 1.9 %stack.303 = f32[12,256]{1,0:T(8,128)} concatenate(f32[1,256]{1,0:T(1,128)S(1)} %get-tuple-element.146, f32[1,256]{1,0:T(1,128)S(1)} %get-tuple-element.146, f32[1,256]{1,0:T(1,128)S(1)} %get-tuple-element.146, f32[1,256]{1,0:T(1,128)S(1)} %get-tuple-element.146, f32[1,256]{1,0:T(1,128)S(1)} %get-tuple-element.146, f32[1,256]{1,0:T(1,128)S(1)} %get-tuple-element.146, ...), dimensions={0} | concatenate | bytes 24576 | tf_op jit(solution)/shard_map/stack | solution.py:112
  134.9 2.0 %stack.302 = f32[12,256]{1,0:T(8,128)} concatenate(f32[1,256]{1,0:T(1,128)S(1)} %get-tuple-element.147, f32[1,256]{1,0:T(1,128)S(1)} %get-tuple-element.147, f32[1,256]{1,0:T(1,128)S(1)} %get-tuple-element.147, f32[1,256]{1,0:T(1,128)S(1)} %get-tuple-element.147, f32[1,256]{1,0:T(1,128)S(1)} %get-tuple-element.147, f32[1,256]{1,0:T(1,128)S(1)} %get-tuple-element.147, ...), dimensions={0} | concatenate | bytes 24576 | tf_op jit(solution)/shard_map/stack | solution.py:112
  136.9 1.2 stack.301
  138.1 1.2 stack.300
  139.3 1.2 stack.299
  140.5 1.2 stack.298
  141.8 2.0 %stack.297 = f32[12,256]{1,0:T(8,128)} concatenate(f32[1,256]{1,0:T(1,128)S(1)} %get-tuple-element.142, f32[1,256]{1,0:T(1,128)S(1)} %get-tuple-element.142, f32[1,256]{1,0:T(1,128)S(1)} %get-tuple-element.142, f32[1,256]{1,0:T(1,128)S(1)} %get-tuple-element.142, f32[1,256]{1,0:T(1,128)S(1)} %get-tuple-element.142, f32[1,256]{1,0:T(1,128)S(1)} %get-tuple-element.142, ...), dimensions={0} | concatenate | bytes 24576 | tf_op jit(solution)/shard_map/stack | solution.py:112
  143.8 2.0 %stack.296 = f32[12,256]{1,0:T(8,128)} concatenate(f32[1,256]{1,0:T(1,128)S(1)} %get-tuple-element.123, f32[1,256]{1,0:T(1,128)S(1)} %get-tuple-element.123, f32[1,256]{1,0:T(1,128)S(1)} %get-tuple-element.123, f32[1,256]{1,0:T(1,128)S(1)} %get-tuple-element.123, f32[1,256]{1,0:T(1,128)S(1)} %get-tuple-element.123, f32[1,256]{1,0:T(1,128)S(1)} %get-tuple-element.123, ...), dimensions={0} | concatenate | bytes 24576 | tf_op jit(solution)/shard_map/stack | solution.py:112
  145.8 1.2 stack.295
  147.8 13.9 %all-to-all-start.1 = ((f32[16,16,128]{2,1,0:T(8,128)}), f32[16,16,128]{2,1,0:T(8,128)S(1)}, u32[]{:S(2)}, u32[]{:S(2)}) async-start(f32[16,16,128]{2,1,0:T(8,128)} %pad_maximum_fusion.8), calls=%async_computation.1 | async-start | bytes 262144 | tf_op jit(solution)/shard_map/all_to_all | solution.py:186
  161.8 7.2 %collective-permute-start.6 = (f32[18,3,256]{2,1,0:T(4,128)S(1)}, f32[18,3,256]{2,1,0:T(4,128)S(1)}, u32[]{:S(2)}, u32[]{:S(2)}) collective-permute-start(f32[18,3,256]{2,1,0:T(4,128)S(1)} %get-tuple-element.69), channel_id=1, source_target_pairs={{0,15},{1,0},{2,1},{3,2},{4,3},{5,4},{6,5},{7,6},{8,7},{9,8},{10,9... | collective-permute-start | bytes 165896 | tf_op jit(solution)/shard_map/ppermute | solution.py:79
  169.0 1.9 collective-permute-start.7
  172.3 5.8 %collective-permute-done.7 = f32[18,3,256]{2,1,0:T(4,128)S(1)} collective-permute-done((f32[18,3,256]{2,1,0:T(4,128)S(1)}, f32[18,3,256]{2,1,0:T(4,128)S(1)}, u32[]{:S(2)}, u32[]{:S(2)}) %collective-permute-start.7) | collective-permute-done | bytes 55328 | tf_op jit(solution)/shard_map/ppermute | solution.py:78
  179.5 5.5 %all-to-all-start.2 = ((f32[32,8,128]{2,1,0:T(8,128)}), f32[32,8,128]{2,1,0:T(8,128)S(1)}, u32[]{:S(2)}, u32[]{:S(2)}) async-start(f32[32,8,128]{2,1,0:T(8,128)} %broadcast_in_dim.5), calls=%async_computation.2 | async-start | bytes 262144 | tf_op jit(solution)/shard_map/all_to_all | solution.py:194
  185.4 3.9 %fusion.70 = bf16[12,24,256]{2,1,0:T(8,128)(2,1)} fusion(f32[18,27,256]{2,1,0:T(8,128)S(1)} %get-tuple-element.68, f32[12,24,256]{2,1,0:T(8,128)S(1)} %bitcast.320, f32[3,24,256]{2,1,0:T(8,128)S(1)} %get-tuple-element.79, f32[18,27,256]{2,1,0:T(8,128)S(1)} %get-tuple-element.67, f32[3,24,256]{2,1,0:T(8,128)S(1)} %get-tuple-element.80, ...), kind=kLoop, calls=%fused_computation.201 | loop fusion | flops 7815168 | bytes 13646848 | tf_op jit(solution)/shard_map/convert_element_type | solution.py:180
  189.3 3.4 %all-to-all-done.2 = f32[32,8,128]{2,1,0:T(8,128)S(1)} async-done(((f32[32,8,128]{2,1,0:T(8,128)}), f32[32,8,128]{2,1,0:T(8,128)S(1)}, u32[]{:S(2)}, u32[]{:S(2)}) %all-to-all-start.2) | async-done | bytes 131104 | tf_op jit(solution)/shard_map/all_to_all | solution.py:194
  (215 shorter events, 21.8 us)
Async XLA Ops:
  0.6 31.3 %copy-start = (bf16[256,1024]{1,0:T(8,128)(2,1)S(1)}, bf16[256,1024]{1,0:T(8,128)(2,1)}, u32[]{:S(2)}) copy-start(bf16[256,1024]{1,0:T(8,128)(2,1)} %param.10) | copy-start | bytes 1572868
  0.6 17.3 %copy-start.1 = (f32[12,24,256]{2,1,0:T(8,128)S(1)}, f32[12,24,256]{2,1,0:T(8,128)}, u32[]{:S(2)}) copy-start(f32[12,24,256]{2,1,0:T(8,128)} %param.6) | copy-start | bytes 884740
  1.7 16.2 %collective-permute-start = (f32[3,24,256]{2,1,0:T(8,128)S(1)}, f32[3,24,256]{2,1,0:T(8,128)S(1)}, u32[]{:S(2)}, u32[]{:S(2)}) collective-permute-start(f32[3,24,256]{2,1,0:T(8,128)S(1)} %reverse_select_fusion.3), channel_id=1, source_target_pairs={{0,8},{1,9},{2,10},{3,11},{4,12},{5,13},{6,14},{7,15},{8,0},{9,1},... | collective-permute-start | bytes 221192 | tf_op jit(solution)/shard_map/ppermute | solution.py:73
  6.2 11.7 %collective-permute-start.1 = (f32[3,24,256]{2,1,0:T(8,128)S(1)}, f32[3,24,256]{2,1,0:T(8,128)S(1)}, u32[]{:S(2)}, u32[]{:S(2)}) collective-permute-start(f32[3,24,256]{2,1,0:T(8,128)S(1)} %get-tuple-element.78), channel_id=1, source_target_pairs={{0,16},{1,17},{2,18},{3,19},{4,20},{5,21},{6,22},{7,23},{8,24},{9,... | collective-permute-start | bytes 221192 | tf_op jit(solution)/shard_map/ppermute | solution.py:72
  18.0 10.2 %collective-permute-start.2 = (f32[18,3,256]{2,1,0:T(4,128)S(1)}, f32[18,3,256]{2,1,0:T(4,128)S(1)}, u32[]{:S(2)}, u32[]{:S(2)}) collective-permute-start(f32[18,3,256]{2,1,0:T(4,128)S(1)} %get-tuple-element.73), channel_id=1, source_target_pairs={{0,1},{1,2},{2,3},{3,4},{4,5},{5,6},{6,7},{7,8},{8,9},{9,10},{10,1... | collective-permute-start | bytes 165896 | tf_op jit(solution)/shard_map/ppermute | solution.py:78
  19.9 8.7 %collective-permute-start.3 = (f32[18,3,256]{2,1,0:T(4,128)S(1)}, f32[18,3,256]{2,1,0:T(4,128)S(1)}, u32[]{:S(2)}, u32[]{:S(2)}) collective-permute-start(f32[18,3,256]{2,1,0:T(4,128)S(1)} %get-tuple-element.74), channel_id=1, source_target_pairs={{0,15},{1,0},{2,1},{3,2},{4,3},{5,4},{6,5},{7,6},{8,7},{9,8},{10,9... | collective-permute-start | bytes 165896 | tf_op jit(solution)/shard_map/ppermute | solution.py:79
  44.7 12.3 %collective-permute-start.8 = (f32[16,128,128]{2,1,0:T(8,128)}, f32[16,128,128]{2,1,0:T(8,128)}, u32[]{:S(2)}, u32[]{:S(2)}) collective-permute-start(f32[16,128,128]{2,1,0:T(8,128)} %bitcast.151), channel_id=1, source_target_pairs={{0,16},{16,0},{1,17},{17,1},{2,18},{18,2},{3,19},{19,3},{4,20},{20... | collective-permute-start | bytes 3145736 | tf_op jit(solution)/shard_map/ppermute | solution.py:167
  59.4 16.4 %copy-start.23 = (f32[1,256]{1,0:T(1,128)S(1)}, f32[1,256]{1,0:T(1,128)}, u32[]{:S(2)}) copy-start(f32[1,256]{1,0:T(1,128)} %get-tuple-element.103) | copy-start | bytes 3076
  59.4 17.2 %copy-start.22 = (f32[1,256]{1,0:T(1,128)S(1)}, f32[1,256]{1,0:T(1,128)}, u32[]{:S(2)}) copy-start(f32[1,256]{1,0:T(1,128)} %get-tuple-element.104) | copy-start | bytes 3076
  59.4 18.1 %copy-start.21 = (f32[1,256]{1,0:T(1,128)S(1)}, f32[1,256]{1,0:T(1,128)}, u32[]{:S(2)}) copy-start(f32[1,256]{1,0:T(1,128)} %get-tuple-element.105) | copy-start | bytes 3076
  59.4 18.9 %copy-start.20 = (f32[1,256]{1,0:T(1,128)S(1)}, f32[1,256]{1,0:T(1,128)}, u32[]{:S(2)}) copy-start(f32[1,256]{1,0:T(1,128)} %get-tuple-element.106) | copy-start | bytes 3076
  59.4 20.9 %copy-start.19 = (f32[1,256]{1,0:T(1,128)S(1)}, f32[1,256]{1,0:T(1,128)}, u32[]{:S(2)}) copy-start(f32[1,256]{1,0:T(1,128)} %get-tuple-element.107) | copy-start | bytes 3076
  59.4 22.9 %copy-start.18 = (f32[1,256]{1,0:T(1,128)S(1)}, f32[1,256]{1,0:T(1,128)}, u32[]{:S(2)}) copy-start(f32[1,256]{1,0:T(1,128)} %get-tuple-element.108) | copy-start | bytes 3076
  59.4 24.9 %copy-start.16 = (f32[1,256]{1,0:T(1,128)S(1)}, f32[1,256]{1,0:T(1,128)}, u32[]{:S(2)}) copy-start(f32[1,256]{1,0:T(1,128)} %get-tuple-element.109) | copy-start | bytes 3076
  59.5 26.8 %copy-start.15 = (f32[1,256]{1,0:T(1,128)S(1)}, f32[1,256]{1,0:T(1,128)}, u32[]{:S(2)}) copy-start(f32[1,256]{1,0:T(1,128)} %get-tuple-element.110) | copy-start | bytes 3076
  59.5 28.8 %copy-start.14 = (f32[1,256]{1,0:T(1,128)S(1)}, f32[1,256]{1,0:T(1,128)}, u32[]{:S(2)}) copy-start(f32[1,256]{1,0:T(1,128)} %get-tuple-element.111) | copy-start | bytes 3076
  59.5 30.7 %copy-start.13 = (f32[1,256]{1,0:T(1,128)S(1)}, f32[1,256]{1,0:T(1,128)}, u32[]{:S(2)}) copy-start(f32[1,256]{1,0:T(1,128)} %get-tuple-element.112) | copy-start | bytes 3076
  59.5 32.7 %copy-start.12 = (f32[1,256]{1,0:T(1,128)S(1)}, f32[1,256]{1,0:T(1,128)}, u32[]{:S(2)}) copy-start(f32[1,256]{1,0:T(1,128)} %get-tuple-element.113) | copy-start | bytes 3076
  59.5 34.6 %copy-start.11 = (f32[1,256]{1,0:T(1,128)S(1)}, f32[1,256]{1,0:T(1,128)}, u32[]{:S(2)}) copy-start(f32[1,256]{1,0:T(1,128)} %get-tuple-element.114) | copy-start | bytes 3076
  59.5 36.6 %copy-start.10 = (f32[1,256]{1,0:T(1,128)S(1)}, f32[1,256]{1,0:T(1,128)}, u32[]{:S(2)}) copy-start(f32[1,256]{1,0:T(1,128)} %get-tuple-element.115) | copy-start | bytes 3076
  59.5 38.5 %copy-start.9 = (f32[1,256]{1,0:T(1,128)S(1)}, f32[1,256]{1,0:T(1,128)}, u32[]{:S(2)}) copy-start(f32[1,256]{1,0:T(1,128)} %get-tuple-element.116) | copy-start | bytes 3076
  59.5 40.4 %copy-start.8 = (f32[1,256]{1,0:T(1,128)S(1)}, f32[1,256]{1,0:T(1,128)}, u32[]{:S(2)}) copy-start(f32[1,256]{1,0:T(1,128)} %get-tuple-element.117) | copy-start | bytes 3076
  59.5 42.3 %copy-start.7 = (f32[1,256]{1,0:T(1,128)S(1)}, f32[1,256]{1,0:T(1,128)}, u32[]{:S(2)}) copy-start(f32[1,256]{1,0:T(1,128)} %get-tuple-element.118) | copy-start | bytes 3076
  59.5 87.5 %all-to-all-start = ((f32[16,136,128]{2,1,0:T(8,128)}), f32[16,136,128]{2,1,0:T(8,128)S(1)}, u32[]{:S(2)}, u32[]{:S(2)}) async-start(f32[16,136,128]{2,1,0:T(8,128)} %pad_maximum_fusion.1), calls=%async_computation | async-start | bytes 2228224 | tf_op jit(solution)/shard_map/all_to_all | solution.py:182
  66.7 70.2 %copy-start.68 = (f32[1,256]{1,0:T(1,128)S(1)}, f32[1,256]{1,0:T(1,128)}, u32[]{:S(2)}) copy-start(f32[1,256]{1,0:T(1,128)} %get-tuple-element.98) | copy-start | bytes 3076
  66.7 71.4 %copy-start.67 = (f32[1,256]{1,0:T(1,128)S(1)}, f32[1,256]{1,0:T(1,128)}, u32[]{:S(2)}) copy-start(f32[1,256]{1,0:T(1,128)} %get-tuple-element.99) | copy-start | bytes 3076
  66.7 72.6 %copy-start.66 = (f32[1,256]{1,0:T(1,128)S(1)}, f32[1,256]{1,0:T(1,128)}, u32[]{:S(2)}) copy-start(f32[1,256]{1,0:T(1,128)} %get-tuple-element.100) | copy-start | bytes 3076
  66.7 73.8 %copy-start.65 = (f32[1,256]{1,0:T(1,128)S(1)}, f32[1,256]{1,0:T(1,128)}, u32[]{:S(2)}) copy-start(f32[1,256]{1,0:T(1,128)} %get-tuple-element.101) | copy-start | bytes 3076
  66.7 79.0 %copy-start.17 = (f32[1,256]{1,0:T(1,128)S(1)}, f32[1,256]{1,0:T(1,128)}, u32[]{:S(2)}) copy-start(f32[1,256]{1,0:T(1,128)} %get-tuple-element.102) | copy-start | bytes 3076
  66.7 79.0 %copy-start.64 = (f32[1,256]{1,0:T(1,128)S(1)}, f32[1,256]{1,0:T(1,128)}, u32[]{:S(2)}) copy-start(f32[1,256]{1,0:T(1,128)} %get-tuple-element.83) | copy-start | bytes 3076
  67.4 79.6 %collective-permute-start.4 = (f32[3,24,256]{2,1,0:T(8,128)S(1)}, f32[3,24,256]{2,1,0:T(8,128)S(1)}, u32[]{:S(2)}, u32[]{:S(2)}) collective-permute-start(f32[3,24,256]{2,1,0:T(8,128)S(1)} %reverse_select_fusion.2), channel_id=1, source_target_pairs={{0,8},{1,9},{2,10},{3,11},{4,12},{5,13},{6,14},{7,15},{8,0},{9,1},... | collective-permute-start | bytes 221192 | tf_op jit(solution)/shard_map/ppermute | solution.py:73
  71.1 75.8 %collective-permute-start.5 = (f32[3,24,256]{2,1,0:T(8,128)S(1)}, f32[3,24,256]{2,1,0:T(8,128)S(1)}, u32[]{:S(2)}, u32[]{:S(2)}) collective-permute-start(f32[3,24,256]{2,1,0:T(8,128)S(1)} %bitcast.331), channel_id=1, source_target_pairs={{0,16},{1,17},{2,18},{3,19},{4,20},{5,21},{6,22},{7,23},{8,24},{9,... | collective-permute-start | bytes 221192 | tf_op jit(solution)/shard_map/ppermute | solution.py:72
  147.1 23.9 %copy-start.6 = (bf16[1024,256]{1,0:T(8,128)(2,1)S(1)}, bf16[1024,256]{1,0:T(8,128)(2,1)}, u32[]{:S(2)}) copy-start(bf16[1024,256]{1,0:T(8,128)(2,1)} %param.11) | copy-start | bytes 1572868
  147.8 30.4 %all-to-all-start.1 = ((f32[16,16,128]{2,1,0:T(8,128)}), f32[16,16,128]{2,1,0:T(8,128)S(1)}, u32[]{:S(2)}, u32[]{:S(2)}) async-start(f32[16,16,128]{2,1,0:T(8,128)} %pad_maximum_fusion.8), calls=%async_computation.1 | async-start | bytes 262144 | tf_op jit(solution)/shard_map/all_to_all | solution.py:186
  161.8 10.5 %collective-permute-start.6 = (f32[18,3,256]{2,1,0:T(4,128)S(1)}, f32[18,3,256]{2,1,0:T(4,128)S(1)}, u32[]{:S(2)}, u32[]{:S(2)}) collective-permute-start(f32[18,3,256]{2,1,0:T(4,128)S(1)} %get-tuple-element.69), channel_id=1, source_target_pairs={{0,15},{1,0},{2,1},{3,2},{4,3},{5,4},{6,5},{7,6},{8,7},{9,8},{10,9... | collective-permute-start | bytes 165896 | tf_op jit(solution)/shard_map/ppermute | solution.py:79
  169.0 9.1 %collective-permute-start.7 = (f32[18,3,256]{2,1,0:T(4,128)S(1)}, f32[18,3,256]{2,1,0:T(4,128)S(1)}, u32[]{:S(2)}, u32[]{:S(2)}) collective-permute-start(f32[18,3,256]{2,1,0:T(4,128)S(1)} %get-tuple-element.70), channel_id=1, source_target_pairs={{0,1},{1,2},{2,3},{3,4},{4,5},{5,6},{6,7},{7,8},{8,9},{9,10},{10,1... | collective-permute-start | bytes 165896 | tf_op jit(solution)/shard_map/ppermute | solution.py:78
  171.9 13.1 %copy-start.28 = (f32[12,256]{1,0:T(8,128)S(1)}, f32[12,256]{1,0:T(8,128)}, u32[]{:S(2)}) copy-start(f32[12,256]{1,0:T(8,128)} %stack.328) | copy-start | bytes 36868
  172.0 13.1 %copy-start.29 = (f32[12,256]{1,0:T(8,128)S(1)}, f32[12,256]{1,0:T(8,128)}, u32[]{:S(2)}) copy-start(f32[12,256]{1,0:T(8,128)} %stack.327) | copy-start | bytes 36868
  172.0 13.1 %copy-start.30 = (f32[12,256]{1,0:T(8,128)S(1)}, f32[12,256]{1,0:T(8,128)}, u32[]{:S(2)}) copy-start(f32[12,256]{1,0:T(8,128)} %stack.326) | copy-start | bytes 36868
  172.0 13.1 %copy-start.31 = (f32[12,256]{1,0:T(8,128)S(1)}, f32[12,256]{1,0:T(8,128)}, u32[]{:S(2)}) copy-start(f32[12,256]{1,0:T(8,128)} %stack.325) | copy-start | bytes 36868
  172.0 13.1 %copy-start.32 = (f32[12,256]{1,0:T(8,128)S(1)}, f32[12,256]{1,0:T(8,128)}, u32[]{:S(2)}) copy-start(f32[12,256]{1,0:T(8,128)} %stack.324) | copy-start | bytes 36868
  172.0 13.1 %copy-start.33 = (f32[12,256]{1,0:T(8,128)S(1)}, f32[12,256]{1,0:T(8,128)}, u32[]{:S(2)}) copy-start(f32[12,256]{1,0:T(8,128)} %stack.323) | copy-start | bytes 36868
  172.0 13.1 %copy-start.34 = (f32[12,256]{1,0:T(8,128)S(1)}, f32[12,256]{1,0:T(8,128)}, u32[]{:S(2)}) copy-start(f32[12,256]{1,0:T(8,128)} %stack.322) | copy-start | bytes 36868
  172.0 13.1 %copy-start.35 = (f32[12,256]{1,0:T(8,128)S(1)}, f32[12,256]{1,0:T(8,128)}, u32[]{:S(2)}) copy-start(f32[12,256]{1,0:T(8,128)} %stack.321) | copy-start | bytes 36868
  172.0 13.1 %copy-start.36 = (f32[12,256]{1,0:T(8,128)S(1)}, f32[12,256]{1,0:T(8,128)}, u32[]{:S(2)}) copy-start(f32[12,256]{1,0:T(8,128)} %stack.320) | copy-start | bytes 36868
  172.0 13.1 %copy-start.37 = (f32[12,256]{1,0:T(8,128)S(1)}, f32[12,256]{1,0:T(8,128)}, u32[]{:S(2)}) copy-start(f32[12,256]{1,0:T(8,128)} %stack.319) | copy-start | bytes 36868
  172.0 13.1 %copy-start.38 = (f32[12,256]{1,0:T(8,128)S(1)}, f32[12,256]{1,0:T(8,128)}, u32[]{:S(2)}) copy-start(f32[12,256]{1,0:T(8,128)} %stack.318) | copy-start | bytes 36868
  172.1 13.1 %copy-start.39 = (f32[12,256]{1,0:T(8,128)S(1)}, f32[12,256]{1,0:T(8,128)}, u32[]{:S(2)}) copy-start(f32[12,256]{1,0:T(8,128)} %stack.316) | copy-start | bytes 36868
  172.1 13.1 %copy-start.40 = (f32[12,256]{1,0:T(8,128)S(1)}, f32[12,256]{1,0:T(8,128)}, u32[]{:S(2)}) copy-start(f32[12,256]{1,0:T(8,128)} %stack.315) | copy-start | bytes 36868
  172.1 13.1 %copy-start.41 = (f32[12,256]{1,0:T(8,128)S(1)}, f32[12,256]{1,0:T(8,128)}, u32[]{:S(2)}) copy-start(f32[12,256]{1,0:T(8,128)} %stack.314) | copy-start | bytes 36868
  172.1 13.1 %copy-start.42 = (f32[12,256]{1,0:T(8,128)S(1)}, f32[12,256]{1,0:T(8,128)}, u32[]{:S(2)}) copy-start(f32[12,256]{1,0:T(8,128)} %stack.313) | copy-start | bytes 36868
  172.1 13.1 %copy-start.43 = (f32[12,256]{1,0:T(8,128)S(1)}, f32[12,256]{1,0:T(8,128)}, u32[]{:S(2)}) copy-start(f32[12,256]{1,0:T(8,128)} %stack.312) | copy-start | bytes 36868
  172.1 13.1 %copy-start.44 = (f32[12,256]{1,0:T(8,128)S(1)}, f32[12,256]{1,0:T(8,128)}, u32[]{:S(2)}) copy-start(f32[12,256]{1,0:T(8,128)} %stack.311) | copy-start | bytes 36868
  172.1 13.1 %copy-start.45 = (f32[12,256]{1,0:T(8,128)S(1)}, f32[12,256]{1,0:T(8,128)}, u32[]{:S(2)}) copy-start(f32[12,256]{1,0:T(8,128)} %stack.310) | copy-start | bytes 36868
  172.1 13.1 %copy-start.46 = (f32[12,256]{1,0:T(8,128)S(1)}, f32[12,256]{1,0:T(8,128)}, u32[]{:S(2)}) copy-start(f32[12,256]{1,0:T(8,128)} %stack.309) | copy-start | bytes 36868
  172.1 13.1 %copy-start.47 = (f32[12,256]{1,0:T(8,128)S(1)}, f32[12,256]{1,0:T(8,128)}, u32[]{:S(2)}) copy-start(f32[12,256]{1,0:T(8,128)} %stack.308) | copy-start | bytes 36868
  172.1 13.1 %copy-start.48 = (f32[12,256]{1,0:T(8,128)S(1)}, f32[12,256]{1,0:T(8,128)}, u32[]{:S(2)}) copy-start(f32[12,256]{1,0:T(8,128)} %stack.307) | copy-start | bytes 36868
  172.2 13.1 %copy-start.49 = (f32[12,256]{1,0:T(8,128)S(1)}, f32[12,256]{1,0:T(8,128)}, u32[]{:S(2)}) copy-start(f32[12,256]{1,0:T(8,128)} %stack.306) | copy-start | bytes 36868
  172.2 13.1 %copy-start.50 = (f32[12,256]{1,0:T(8,128)S(1)}, f32[12,256]{1,0:T(8,128)}, u32[]{:S(2)}) copy-start(f32[12,256]{1,0:T(8,128)} %stack.305) | copy-start | bytes 36868
  172.2 13.1 %copy-start.51 = (f32[12,256]{1,0:T(8,128)S(1)}, f32[12,256]{1,0:T(8,128)}, u32[]{:S(2)}) copy-start(f32[12,256]{1,0:T(8,128)} %stack.304) | copy-start | bytes 36868
  172.2 13.1 %copy-start.52 = (f32[12,256]{1,0:T(8,128)S(1)}, f32[12,256]{1,0:T(8,128)}, u32[]{:S(2)}) copy-start(f32[12,256]{1,0:T(8,128)} %stack.303) | copy-start | bytes 36868
  172.2 13.1 %copy-start.53 = (f32[12,256]{1,0:T(8,128)S(1)}, f32[12,256]{1,0:T(8,128)}, u32[]{:S(2)}) copy-start(f32[12,256]{1,0:T(8,128)} %stack.302) | copy-start | bytes 36868
  172.2 13.1 %copy-start.54 = (f32[12,256]{1,0:T(8,128)S(1)}, f32[12,256]{1,0:T(8,128)}, u32[]{:S(2)}) copy-start(f32[12,256]{1,0:T(8,128)} %stack.301) | copy-start | bytes 36868
  179.5 13.2 %all-to-all-start.2 = ((f32[32,8,128]{2,1,0:T(8,128)}), f32[32,8,128]{2,1,0:T(8,128)S(1)}, u32[]{:S(2)}, u32[]{:S(2)}) async-start(f32[32,8,128]{2,1,0:T(8,128)} %broadcast_in_dim.5), calls=%async_computation.2 | async-start | bytes 262144 | tf_op jit(solution)/shard_map/all_to_all | solution.py:194
  (21 other events, 193.2 us)

commit v2 on v1

v2 whole, which is shorter than its diff:
```python
import functools
import math

import jax
import jax.numpy as jnp
from jax import lax
from jax.experimental import pallas as pl
from jax.experimental.pallas import tpu as pltpu
from jax.sharding import Mesh, PartitionSpec as P

AXES = ("zh", "x", "core", "y", "zl")
SIZES = (4, 4, 2, 4, 4)
LAT = 32
LON = 16


def lat_lon():
    lat = (lax.axis_index("zh") * 4 + lax.axis_index("x")) * 2 + lax.axis_index("core")
    return lat, lax.axis_index("y") * 4 + lax.axis_index("zl")


def row_pairs():
    first, second = [], []
    for lat in range(LAT):
        for lon in range(LON):
            here = lat * LON + lon
            first.append((here, (lat ^ 1) * LON + lon))
            if lat == 0 or lat == LAT - 1:
                peer = lat * LON + (lon + LON // 2) % LON
            else:
                peer = (lat - 1 if lat % 2 == 0 else lat + 1) * LON + lon
            second.append((here, peer))
    return first, second


def column_pairs():
    right, left = [], []
    for lat in range(LAT):
        for lon in range(LON):
            here = lat * LON + lon
            right.append((here, lat * LON + (lon + 1) % LON))
            left.append((here, lat * LON + (lon - 1) % LON))
    return right, left


H = 12
W = 24
C = 256
FF = 1024
CELLS = H * W
PARAMS = pltpu.CompilerParams(vmem_limit_bytes=48 * 1024 * 1024)


def gelu_parts(values):
    phi = 0.5 * (1.0 + lax.erf(values * 0.7071067811865476))
    slope = phi + values * jnp.exp(-0.5 * values * values) * 0.3989422804014327
    return values * phi, slope


def fill(wide_ref, above, below, centre, before, after):
    wide_ref[0:3, 8 : 8 + W, :] = above[...]
    wide_ref[3 : 3 + H, 8 : 8 + W, :] = centre[...]
    wide_ref[3 + H :, 8 : 8 + W, :] = below[...]
    wide_ref[:, 5:8, :] = before[...]
    wide_ref[:, 8 + W : 11 + W, :] = after[...]


def window(wide_ref, row, col, lanes):
    return wide_ref[row, 5 + col : 5 + col + W, lanes]


def convolve(wide_ref, weight, lanes):
    total = [None] * H
    for col in range(7):
        for row in range(H + 6):
            part = window(wide_ref, row, col, lanes)
            for tap in range(7):
                out = row - tap
                if 0 <= out < H:
                    term = weight(row, tap, col, lanes) * part
                    total[out] = term if total[out] is None else total[out] + term
    return total


def forward_kernel(
    core_ref, above, below, state, before, after, cot, taps, gain, w_in, w_out,
    block_out, grad_conv, mine, theirs, gain_sum,
    wide, conv, hidden, grad_pre,
):
    fill(wide, above, below, state, before, after)
    for half in range(2):
        lanes = slice(128 * half, 128 * half + 128)
        total = convolve(
            wide, lambda row, tap, col, ln: taps[7 * tap + col : 7 * tap + col + 1, ln], lanes
        )
        for out in range(H):
            conv[W * out : W * out + W, lanes] = total[out]
    values = conv[...]
    centred = values - jnp.mean(values, axis=-1, keepdims=True)
    variance = jnp.mean(centred * centred, axis=-1, keepdims=True)
    inv_std = 1.0 / jnp.sqrt(variance + 1e-06)
    centred = centred * inv_std
    conv[...] = centred
    normed = (centred * gain[...]).astype(jnp.bfloat16)
    cotangent = cot[...]
    branch = state[...].reshape(CELLS, C)
    grad_normed = jnp.zeros((CELLS, C), jnp.float32)
    for part in range(4):
        cols = slice(256 * part, 256 * part + 256)
        pre_act = jnp.dot(normed, w_in[:, cols], preferred_element_type=jnp.float32)
        grad_hidden = lax.dot_general(
            cotangent, w_out[cols, :], (((1,), (1,)), ((), ())), preferred_element_type=jnp.float32
        )
        value, slope = gelu_parts(pre_act)
        hid = value.astype(jnp.bfloat16)
        gpre = (grad_hidden * slope).astype(jnp.bfloat16)
        hidden[:, cols] = hid
        grad_pre[:, cols] = gpre
    core = core_ref[0]
    for part in range(4):
        cols = slice(256 * part, 256 * part + 256)
        hid = hidden[:, cols]
        gpre = grad_pre[:, cols]
        branch = branch + jnp.dot(hid, w_out[cols, :], preferred_element_type=jnp.float32)
        grad_normed = grad_normed + lax.dot_general(
            gpre, w_in[:, cols], (((1,), (1,)), ((), ())), preferred_element_type=jnp.float32
        )
        for side, (left, right) in enumerate(((gpre, normed), (hid, cotangent))):
            product = lax.dot_general(
                left, right, (((0,), (0,)), ((), ())), preferred_element_type=jnp.float32
            )
            for x in range(4):
                for run in range(2):
                    lanes = slice(128 * run, 128 * run + 128)
                    ours = product[64 * x : 64 * x + 32, lanes]
                    other = product[64 * x + 32 : 64 * x + 64, lanes]
                    keep = jnp.where(core == 0, ours, other)
                    send = jnp.where(core == 0, other, ours)
                    row = 32 * (2 * side + run) + 8 * part
                    mine[4 * x : 4 * x + 4, row : row + 8, :] = keep.reshape(4, 8, 128)
                    theirs[4 * x : 4 * x + 4, row : row + 8, :] = send.reshape(4, 8, 128)
    block_out[...] = branch.astype(jnp.bfloat16)
    centred = conv[...]
    scaled = grad_normed * gain[...]
    grad = inv_std * (
        scaled
        - jnp.mean(scaled, axis=-1, keepdims=True)
        - centred * jnp.mean(scaled * centred, axis=-1, keepdims=True)
    )
    gain_sum[...] = jnp.sum(grad_normed * centred, axis=0, keepdims=True)
    grad_conv[...] = grad.reshape(H, W, C)


def tap_kernel(above, below, state, before, after, grad_conv, gain_sum, out, wide):
    fill(wide, above, below, state, before, after)
    for half in range(2):
        lanes = slice(128 * half, 128 * half + 128)
        grad = [grad_conv[row, :, lanes] for row in range(H)]
        for col in range(7):
            total = [jnp.zeros((8, 128), jnp.float32)] * 7
            for row in range(H + 6):
                part = window(wide, row, col, lanes)
                for tap in range(7):
                    if 0 <= row - tap < H:
                        term = part * grad[row - tap]
                        total[tap] = total[tap] + ((term[0:8] + term[8:16]) + term[16:24])
            for tap in range(7):
                place = 64 * half + 7 * tap + col
                out[place : place + 1, :] = jnp.sum(total[tap], axis=0, keepdims=True)
        out[64 * half + 49 : 64 * half + 50, :] = gain_sum[:, lanes]
        out[64 * half + 50 : 64 * half + 64, :] = jnp.zeros((14, 128), jnp.float32)


def adjoint_kernel(lat_ref, above, below, grad_conv, before, after, cot, taps, out, wide, rim, grad):
    fill(wide, above, below, grad_conv, before, after)
    lat = lat_ref[0]
    for tap in range(7):
        here = taps[7 * tap : 7 * tap + 7, :]
        turned = taps[7 * (6 - tap) : 7 * (6 - tap) + 7, :]
        rim[0, tap, 0:7, :] = jnp.where(lat == 0, turned, here)
        rim[1, tap, 0:7, :] = jnp.where(lat == LAT - 1, turned, here)

    def weight(row, tap, col, lanes):
        if row < 3:
            return rim[0, 6 - tap, 6 - col : 7 - col, lanes]
        if row >= H + 3:
            return rim[1, 6 - tap, 6 - col : 7 - col, lanes]
        place = 7 * (6 - tap) + 6 - col
        return taps[place : place + 1, lanes]

    for half in range(2):
        lanes = slice(128 * half, 128 * half + 128)
        total = convolve(wide, weight, lanes)
        for row in range(H):
            grad[W * row : W * row + W, lanes] = total[row]
    out[...] = (cot[...].astype(jnp.float32) + grad[...]).astype(jnp.bfloat16)


def join_kernel(mine, theirs, taps, out):
    out[:, 0:128, :] = mine[...] + theirs[...]
    out[:, 128:136, :] = taps[...].reshape(16, 8, 128)


def plane_kernel(got, out):
    total = got[0]
    for peer in range(1, 16):
        total = total + got[peer]
    for zh in range(4):
        for zl in range(4):
            place = 4 * zh + zl
            for run in range(4):
                row = 32 * run + 8 * zh + 2 * zl
                out[place, 2 * run : 2 * run + 2, :] = total[row : row + 2]
            out[place, 8:16, :] = total[128:136]


def column_kernel(scale, got, weight_grads, shared):
    total = got[0]
    for peer in range(1, 16):
        total = total + got[peer]
    total = total * scale
    for run in range(4):
        weight_grads[:, 128 * run : 128 * run + 128] = total[2 * run : 2 * run + 2]
    for peer in range(32):
        shared[peer] = total[8:16]


def total_kernel(got, taps, gain):
    for half in range(2):
        rows = []
        for place in range(8 * half, 8 * half + 8):
            x, y = place // 4, place % 4
            rows.append(got[8 * x + y] + got[8 * x + 4 + y])
        table = jnp.concatenate(rows, 0)
        taps[:, 128 * half : 128 * half + 128] = table[0:49]
        gain[:, 128 * half : 128 * half + 128] = table[49:50]


def call(kernel, out, *args, scratch=(), scalars=0):
    vmem = pl.BlockSpec(memory_space=pltpu.VMEM)
    smem = pl.BlockSpec(memory_space=pltpu.SMEM)
    many = isinstance(out, list)
    return pl.pallas_call(
        kernel,
        out_shape=[jax.ShapeDtypeStruct(s, d) for s, d in (out if many else [out])],
        in_specs=[smem] * scalars + [vmem] * (len(args) - scalars),
        out_specs=[vmem] * (len(out) if many else 1),
        scratch_shapes=[pltpu.VMEM(s, d) for s, d in scratch],
        compiler_params=PARAMS,
    )(*args)


F32 = jnp.float32
BF16 = jnp.bfloat16
WIDE = ((H + 6, 40, C), F32)


def halo(values):
    lat, _ = lat_lon()
    even = lat % 2 == 0
    pole = (lat == 0) | (lat == LAT - 1)
    head, tail = values[:3], values[-3:]
    first, second = row_pairs()
    outer = jnp.where(even, head, tail)
    outer = jnp.where(pole, jnp.flip(outer, 0), outer)
    got_first = lax.ppermute(jnp.where(even, tail, head), AXES, first)
    got_second = lax.ppermute(outer, AXES, second)
    above = jnp.where(even, got_second, got_first)
    below = jnp.where(even, got_first, got_second)
    right, left = column_pairs()
    edge = jnp.concatenate([above[:, -3:], values[:, -3:], below[:, -3:]], 0)
    before = lax.ppermute(edge, AXES, right)
    edge = jnp.concatenate([above[:, :3], values[:, :3], below[:, :3]], 0)
    after = lax.ppermute(edge, AXES, left)
    return above, below, values, before, after


def body(state_field, cotangent, depthwise, norm_gain, w_in, w_out):
    grad_scale = 1.0 / math.sqrt(CELLS * LAT * LON)
    lat, _ = lat_lon()
    lat = lat.astype(jnp.int32).reshape(1)
    core = lax.axis_index("core").astype(jnp.int32).reshape(1)
    cot = cotangent.reshape(CELLS, C)
    pieces = halo(state_field)
    block_out, grad_conv, mine, theirs, gain_sum = call(
        forward_kernel,
        [
            ((CELLS, C), BF16),
            ((H, W, C), F32),
            ((16, 128, 128), F32),
            ((16, 128, 128), F32),
            ((1, C), F32),
        ],
        core, *pieces, cot, depthwise, norm_gain.reshape(1, C), w_in, w_out,
        scratch=[WIDE, ((CELLS, C), F32), ((CELLS, FF), BF16), ((CELLS, FF), BF16)],
        scalars=1,
    )
    theirs = lax.ppermute(theirs, "core", [(0, 1), (1, 0)])
    (taps,) = call(tap_kernel, ((128, 128), F32), *pieces, grad_conv, gain_sum, scratch=[WIDE])
    grad_pieces = halo(grad_conv)
    (joined,) = call(join_kernel, ((16, 136, 128), F32), mine, theirs, taps)
    plane = lax.all_to_all(joined, ("x", "y"), split_axis=0, concat_axis=0, tiled=True)
    (spread,) = call(plane_kernel, ((16, 16, 128), F32), plane)
    column = lax.all_to_all(spread, ("zh", "zl"), split_axis=0, concat_axis=0, tiled=True)
    weight_grads, shared = call(
        functools.partial(column_kernel, grad_scale), [((2, 512), F32), ((32, 8, 128), F32)], column
    )
    shared = lax.all_to_all(shared, ("x", "core", "y"), split_axis=0, concat_axis=0, tiled=True)
    (grad_input,) = call(
        adjoint_kernel,
        ((CELLS, C), BF16),
        lat, *grad_pieces, cot, depthwise,
        scratch=[WIDE, ((2, 7, 8, C), F32), ((CELLS, C), F32)],
        scalars=1,
    )
    tap_total, gain_total = call(total_kernel, [((49, C), F32), ((1, C), F32)], shared)
    return (
        block_out.reshape(H, W, C),
        grad_input.reshape(H, W, C),
        weight_grads,
        tap_total,
        gain_total.reshape(C),
    )


def solution(mesh):
    split = Mesh(mesh.devices.reshape(SIZES), AXES)
    cells = P(("zh", "x", "core"), ("y", "zl"), None)
    return jax.shard_map(
        body,
        mesh=split,
        in_specs=(cells, cells, P(), P(), P(), P()),
        out_specs=(cells, cells, P(AXES, None), P(), P()),
        check_vma=False,
    )
```

time: 196 us -> 111 us (0.57)
  local copies, waits for them, and re-layouts: 90.9 us -> 2.07 us
  other arithmetic: 19.9 us -> 1.15 us
  Pallas kernels: 0 us -> 12.5 us
  waiting for transfers between devices: 9.63 us -> 20.3 us
  starting transfers between devices: 66.2 us -> 73.5 us
  matrix products: 5.32 us -> 0 us
    another operation x52 -> x0, local copies, waits for them, and re-layouts: 80.2 us -> none  [the longest x48 75.1 us: adjoint_taps(): weight = jnp.stack(weight, 0)[:, None, :]]
    pallas_call x0 -> x7, Pallas kernels: none -> 12.5 us  [call(): pl.pallas_call(kernel, out_shape=[jax.ShapeDtypeStruct(s, d) for s, d in...]
    ppermute x2, waiting for transfers between devices: 0.01 us -> 7.61 us  [halo(): got_second = lax.ppermute(outer, AXES, second)]
    reduce_sum x9 -> x0, other arithmetic: 6.36 us -> none  [the longest x4 3.73 us: tap_sums(): jnp.sum(extended[row_off:row_off + height, col_off:col_off + breadth] * g...]
    all_to_all x3, waiting for transfers between devices: 3.38 us -> 9.41 us  [the longest x1 8.67 us: body(): lax.all_to_all(spread, ('zh', 'zl'), split_axis=0, concat_axis=0, tiled=T...]
    dot_general x6 -> x0, matrix products: 5.32 us -> none  [the longest x1 1.64 us: body(): lax.dot_general(grad_pre, w_in, (((1,), (1,)), ((), ())), preferred_eleme...]
    all_to_all x3, starting transfers between devices: 26.6 us -> 31.9 us  [the longest x1 18.9 us: body(): lax.all_to_all(spread, ('zh', 'zl'), split_axis=0, concat_axis=0, tiled=T...]
    convert_element_type x1 -> x0, other arithmetic: 3.89 us -> none  [body(): grad_input = (cotangent.astype(jnp.float32) + adjoint_taps(wide, depthwis...]
  transfers between devices with their start and end apart: 12 -> 12, of which waited for: 3 -> 6; matrix products, arithmetic and copies ran while one was open for 48% -> 1% of each run, Pallas kernels for 0% -> 5%
where the time goes in v2:
time: 111 us; the launch traced here: 110 us
  starting transfers between devices  73.5 us (66%)
  waiting for transfers between devices  20.3 us (18%)
  Pallas kernels  12.5 us (11%)
  local copies, waits for them, and re-layouts  2.07 us (2%)
  other arithmetic  1.15 us (1%)
    all_to_all x1, starting transfers between devices, body(): lax.all_to_all(spread, ('zh', 'zl'), split_axis=0, concat_axis=0, tiled=T...  18.9 us
    pallas_call x7, Pallas kernels, call(): pl.pallas_call(kernel, out_shape=[jax.ShapeDtypeStruct(s, d) for s, d in...  12.5 us
    ppermute x2, starting transfers between devices, halo(): after = lax.ppermute(edge, AXES, left)  11.9 us
    ppermute x2, starting transfers between devices, halo(): got_first = lax.ppermute(jnp.where(even, tail, head), AXES, first)  10 us
    all_to_all x1, waiting for transfers between devices, body(): lax.all_to_all(spread, ('zh', 'zl'), split_axis=0, concat_axis=0, tiled=T...  8.67 us
    ppermute x2, starting transfers between devices, halo(): got_second = lax.ppermute(outer, AXES, second)  8.6 us
    all_to_all x1, starting transfers between devices, body(): lax.all_to_all(shared, ('x', 'core', 'y'), split_axis=0, concat_axis=0, t...  8.52 us
    ppermute x2, waiting for transfers between devices, halo(): got_second = lax.ppermute(outer, AXES, second)  7.61 us
  transfers between devices with their start and end apart: 12, of which 6 were waited for; matrix products, arithmetic and copies ran while one was open for 1% of the time, Pallas kernels for 5%

profile of v2, /device:TPU:1, one launch (start us, length us, event | category | flops | bytes accessed | tf_op | source)
XLA Modules:
  0.0 110.5 jit_solution(9223033316953573464)
XLA Ops:
  0.6 0.0 copy-start
  0.6 0.0 copy-start.4
  0.7 0.0 copy-start.2
  0.7 0.0 copy-start.5
  0.7 0.0 copy-start.1
  0.7 1.0 slice_select_fusion.2
  1.7 4.5 %collective-permute-start = (f32[3,24,256]{2,1,0:T(8,128)S(1)}, f32[3,24,256]{2,1,0:T(8,128)S(1)}, u32[]{:S(2)}, u32[]{:S(2)}) collective-permute-start(f32[3,24,256]{2,1,0:T(8,128)S(1)} %reverse_select_fusion.1), channel_id=1, source_target_pairs={{0,8},{1,9},{2,10},{3,11},{4,12},{5,13},{6,14},{7,15},{8,0},{9,1},... | collective-permute-start | bytes 221192 | tf_op jit(solution)/shard_map/ppermute | solution.py:267
  6.3 6.2 %collective-permute-start.1 = (f32[3,24,256]{2,1,0:T(8,128)S(1)}, f32[3,24,256]{2,1,0:T(8,128)S(1)}, u32[]{:S(2)}, u32[]{:S(2)}) collective-permute-start(f32[3,24,256]{2,1,0:T(8,128)S(1)} %get-tuple-element.29), channel_id=1, source_target_pairs={{0,16},{1,17},{2,18},{3,19},{4,20},{5,21},{6,22},{7,23},{8,24},{9,... | collective-permute-start | bytes 221192 | tf_op jit(solution)/shard_map/ppermute | solution.py:266
  12.5 1.0 fusion.1
  13.4 0.0 collective-permute-done
  13.4 0.0 collective-permute-done.1
  13.5 1.9 %collective-permute-start.2 = (f32[18,3,256]{2,1,0:T(4,128)S(1)}, f32[18,3,256]{2,1,0:T(4,128)S(1)}, u32[]{:S(2)}, u32[]{:S(2)}) collective-permute-start(f32[18,3,256]{2,1,0:T(4,128)S(1)} %pad_maximum_fusion), channel_id=1, source_target_pairs={{0,1},{1,2},{2,3},{3,4},{4,5},{5,6},{6,7},{7,8},{8,9},{9,10},{10,1... | collective-permute-start | bytes 165896 | tf_op jit(solution)/shard_map/ppermute | solution.py:272
  15.5 7.3 %collective-permute-start.3 = (f32[18,3,256]{2,1,0:T(4,128)S(1)}, f32[18,3,256]{2,1,0:T(4,128)S(1)}, u32[]{:S(2)}, u32[]{:S(2)}) collective-permute-start(f32[18,3,256]{2,1,0:T(4,128)S(1)} %pad_maximum_fusion.1), channel_id=1, source_target_pairs={{0,15},{1,0},{2,1},{3,2},{4,3},{5,4},{6,5},{7,6},{8,7},{9,8},{10,9... | collective-permute-start | bytes 165896 | tf_op jit(solution)/shard_map/ppermute | solution.py:274
  22.7 0.0 collective-permute-done.2.before
  22.8 1.4 %collective-permute-done.3.after = f32[18,3,256]{2,1,0:T(4,128)S(1)} collective-permute-done((f32[18,3,256]{2,1,0:T(4,128)S(1)}, f32[18,3,256]{2,1,0:T(4,128)S(1)}, u32[]{:S(2)}, u32[]{:S(2)}) %collective-permute-start.3) | collective-permute-done | bytes 55328 | tf_op jit(solution)/shard_map/ppermute | solution.py:274
  24.1 0.0 copy-done
  24.1 0.0 copy-done.4
  24.1 0.0 copy-done.2
  24.1 0.0 copy-done.5
  24.1 0.0 copy-done.1
  24.2 0.0 copy-start.3
  24.2 1.0 copy-done.3
  25.2 4.6 %shard_map.101 = (bf16[288,256]{1,0:T(8,128)(2,1)}, f32[12,24,256]{2,1,0:T(8,128)S(1)}, f32[16,128,128]{2,1,0:T(8,128)S(1)}, f32[16,128,128]{2,1,0:T(8,128)S(1)}, f32[1,256]{1,0:T(1,128)S(1)}) custom-call(s32[1]{0:T(128)} %bitcast.core_ref, f32[3,24,256]{2,1,0:T(8,128)S(1)} %get-tuple-element.34.above, f32[3,24,256]{2,1,0:T(8,128)S(1)} %get-tuple-element.33.below, ...), custom_call_target="tpu_custom_call" | custom-call | tf_op jit(solution)/shard_map/pallas_call | solution.py:243
  29.8 5.9 %collective-permute-start.8 = (f32[16,128,128]{2,1,0:T(8,128)S(1)}, f32[16,128,128]{2,1,0:T(8,128)S(1)}, u32[]{:S(2)}, u32[]{:S(2)}) collective-permute-start(f32[16,128,128]{2,1,0:T(8,128)S(1)} %get-tuple-element.17), channel_id=1, source_target_pairs={{0,16},{16,0},{1,17},{17,1},{2,18},{18,2},{3,19},{19,3},{4,20},{20... | collective-permute-start | bytes 3145736 | tf_op jit(solution)/shard_map/ppermute | solution.py:298
  35.8 1.7 %shard_map.103.taps = f32[128,128]{1,0:T(8,128)S(1)} custom-call(f32[3,24,256]{2,1,0:T(8,128)S(1)} %get-tuple-element.34.above, f32[3,24,256]{2,1,0:T(8,128)S(1)} %get-tuple-element.33.below, f32[12,24,256]{2,1,0:T(8,128)S(1)} %copy-done, f32[18,3,256]{2,1,0:T(4,128)S(1)} %collective-permute-done.2.before, f32[18,3,256]{2,1,0:T(4,128)S(1)} %collective-permute-done.3.after, ...), custom_call_target="tpu_custom_call" | custom-call | tf_op jit(solution)/shard_map/pallas_call | solution.py:243
  37.5 0.5 collective-permute-done.8.theirs
  38.1 1.1 %shard_map.104 = f32[16,136,128]{2,1,0:T(8,128)} custom-call(f32[16,128,128]{2,1,0:T(8,128)S(1)} %get-tuple-element.16.mine, f32[16,128,128]{2,1,0:T(8,128)S(1)} %collective-permute-done.8.theirs, f32[128,128]{1,0:T(8,128)S(1)} %shard_map.103.taps), custom_call_target="tpu_custom_call" | custom-call | tf_op jit(solution)/shard_map/pallas_call | solution.py:243
  39.2 4.5 %all-to-all-start = ((f32[16,136,128]{2,1,0:T(8,128)}), f32[16,136,128]{2,1,0:T(8,128)S(1)}, u32[]{:S(2)}, u32[]{:S(2)}) async-start(f32[16,136,128]{2,1,0:T(8,128)} %shard_map.104), calls=%async_computation | async-start | bytes 2228224 | tf_op jit(solution)/shard_map/all_to_all | solution.py:302
  43.7 4.1 %collective-permute-start.4 = (f32[3,24,256]{2,1,0:T(8,128)S(1)}, f32[3,24,256]{2,1,0:T(8,128)S(1)}, u32[]{:S(2)}, u32[]{:S(2)}) collective-permute-start(f32[3,24,256]{2,1,0:T(8,128)S(1)} %reverse_select_fusion), channel_id=1, source_target_pairs={{0,8},{1,9},{2,10},{3,11},{4,12},{5,13},{6,14},{7,15},{8,0},{9,1},... | collective-permute-start | bytes 221192 | tf_op jit(solution)/shard_map/ppermute | solution.py:267
  47.8 3.8 %collective-permute-start.5 = (f32[3,24,256]{2,1,0:T(8,128)S(1)}, f32[3,24,256]{2,1,0:T(8,128)S(1)}, u32[]{:S(2)}, u32[]{:S(2)}) collective-permute-start(f32[3,24,256]{2,1,0:T(8,128)S(1)} %get-tuple-element.25), channel_id=1, source_target_pairs={{0,16},{1,17},{2,18},{3,19},{4,20},{5,21},{6,22},{7,23},{8,24},{9,... | collective-permute-start | bytes 221192 | tf_op jit(solution)/shard_map/ppermute | solution.py:266
  51.6 7.6 %collective-permute-done.4 = f32[3,24,256]{2,1,0:T(8,128)S(1)} collective-permute-done((f32[3,24,256]{2,1,0:T(8,128)S(1)}, f32[3,24,256]{2,1,0:T(8,128)S(1)}, u32[]{:S(2)}, u32[]{:S(2)}) %collective-permute-start.4) | collective-permute-done | bytes 73760 | tf_op jit(solution)/shard_map/ppermute | solution.py:267
  59.2 0.0 collective-permute-done.5
  59.3 0.7 all-to-all-done.got
  60.0 0.7 shard_map.105
  60.7 18.9 %all-to-all-start.1 = ((f32[16,16,128]{2,1,0:T(8,128)}), f32[16,16,128]{2,1,0:T(8,128)S(1)}, u32[]{:S(2)}, u32[]{:S(2)}) async-start(f32[16,16,128]{2,1,0:T(8,128)} %shard_map.105), calls=%async_computation.1 | async-start | bytes 262144 | tf_op jit(solution)/shard_map/all_to_all | solution.py:304
  79.7 3.3 %collective-permute-start.6 = (f32[18,3,256]{2,1,0:T(4,128)S(1)}, f32[18,3,256]{2,1,0:T(4,128)S(1)}, u32[]{:S(2)}, u32[]{:S(2)}) collective-permute-start(f32[18,3,256]{2,1,0:T(4,128)S(1)} %pad_maximum_fusion.2), channel_id=1, source_target_pairs={{0,1},{1,2},{2,3},{3,4},{4,5},{5,6},{6,7},{7,8},{8,9},{9,10},{10,1... | collective-permute-start | bytes 165896 | tf_op jit(solution)/shard_map/ppermute | solution.py:272
  83.0 8.7 %all-to-all-done.1.got = f32[16,16,128]{2,1,0:T(8,128)S(1)} async-done(((f32[16,16,128]{2,1,0:T(8,128)}), f32[16,16,128]{2,1,0:T(8,128)S(1)}, u32[]{:S(2)}, u32[]{:S(2)}) %all-to-all-start.1) | async-done | bytes 131104 | tf_op jit(solution)/shard_map/all_to_all | solution.py:304
  91.6 0.7 shard_map.106
  92.3 8.5 %all-to-all-start.2 = ((f32[32,8,128]{2,1,0:T(8,128)}), f32[32,8,128]{2,1,0:T(8,128)S(1)}, u32[]{:S(2)}, u32[]{:S(2)}) async-start(f32[32,8,128]{2,1,0:T(8,128)} %get-tuple-element.20), calls=%async_computation.2 | async-start | bytes 262144 | tf_op jit(solution)/shard_map/all_to_all | solution.py:308
  100.9 4.6 %collective-permute-start.7 = (f32[18,3,256]{2,1,0:T(4,128)S(1)}, f32[18,3,256]{2,1,0:T(4,128)S(1)}, u32[]{:S(2)}, u32[]{:S(2)}) collective-permute-start(f32[18,3,256]{2,1,0:T(4,128)S(1)} %pad_maximum_fusion.3), channel_id=1, source_target_pairs={{0,15},{1,0},{2,1},{3,2},{4,3},{5,4},{6,5},{7,6},{8,7},{9,8},{10,9... | collective-permute-start | bytes 165896 | tf_op jit(solution)/shard_map/ppermute | solution.py:274
  105.5 0.0 collective-permute-done.6.before
  105.5 1.4 %collective-permute-done.7.after = f32[18,3,256]{2,1,0:T(4,128)S(1)} collective-permute-done((f32[18,3,256]{2,1,0:T(4,128)S(1)}, f32[18,3,256]{2,1,0:T(4,128)S(1)}, u32[]{:S(2)}, u32[]{:S(2)}) %collective-permute-start.7) | collective-permute-done | bytes 55328 | tf_op jit(solution)/shard_map/ppermute | solution.py:274
  106.9 3.0 %shard_map.102 = bf16[288,256]{1,0:T(8,128)(2,1)} custom-call(s32[1]{0:T(128)} %bitcast.4.lat_ref, f32[3,24,256]{2,1,0:T(8,128)S(1)} %get-tuple-element.32.above, f32[3,24,256]{2,1,0:T(8,128)S(1)} %get-tuple-element.31.below, f32[12,24,256]{2,1,0:T(8,128)S(1)} %get-tuple-element.15.grad_conv, f32[18,3,256]{2,1,0:T(4,128)S(1)} %collective-permute-done.6.before, ...), custom_call_target="tpu_custom_call" | custom-call | tf_op jit(solution)/shard_map/pallas_call | solution.py:243
  109.8 0.0 all-to-all-done.2.got
  109.8 0.6 shard_map.107
  (13 shorter events, 0.2 us)
Async XLA Ops:
  0.6 23.5 %copy-start = (f32[12,24,256]{2,1,0:T(8,128)S(1)}, f32[12,24,256]{2,1,0:T(8,128)}, u32[]{:S(2)}) copy-start(f32[12,24,256]{2,1,0:T(8,128)} %state.3) | copy-start | bytes 884740
  0.6 23.5 %copy-start.4 = (f32[49,256]{1,0:T(8,128)S(1)}, f32[49,256]{1,0:T(8,128)}, u32[]{:S(2)}) copy-start(f32[49,256]{1,0:T(8,128)} %taps.3) | copy-start | bytes 150532
  0.7 23.5 %copy-start.2 = (bf16[256,1024]{1,0:T(8,128)(2,1)S(1)}, bf16[256,1024]{1,0:T(8,128)(2,1)}, u32[]{:S(2)}) copy-start(bf16[256,1024]{1,0:T(8,128)(2,1)} %w_in.1) | copy-start | bytes 1572868
  0.7 23.5 %copy-start.5 = (f32[256]{0:T(256)S(1)}, f32[256]{0:T(256)}, u32[]{:S(2)}) copy-start(f32[256]{0:T(256)} %param.9) | copy-start | bytes 3076
  0.7 23.5 %copy-start.1 = (bf16[12,24,256]{2,1,0:T(8,128)(2,1)S(1)}, bf16[12,24,256]{2,1,0:T(8,128)(2,1)}, u32[]{:S(2)}) copy-start(bf16[12,24,256]{2,1,0:T(8,128)(2,1)} %param.7) | copy-start | bytes 442372
  1.7 11.7 %collective-permute-start = (f32[3,24,256]{2,1,0:T(8,128)S(1)}, f32[3,24,256]{2,1,0:T(8,128)S(1)}, u32[]{:S(2)}, u32[]{:S(2)}) collective-permute-start(f32[3,24,256]{2,1,0:T(8,128)S(1)} %reverse_select_fusion.1), channel_id=1, source_target_pairs={{0,8},{1,9},{2,10},{3,11},{4,12},{5,13},{6,14},{7,15},{8,0},{9,1},... | collective-permute-start | bytes 221192 | tf_op jit(solution)/shard_map/ppermute | solution.py:267
  6.3 7.2 %collective-permute-start.1 = (f32[3,24,256]{2,1,0:T(8,128)S(1)}, f32[3,24,256]{2,1,0:T(8,128)S(1)}, u32[]{:S(2)}, u32[]{:S(2)}) collective-permute-start(f32[3,24,256]{2,1,0:T(8,128)S(1)} %get-tuple-element.29), channel_id=1, source_target_pairs={{0,16},{1,17},{2,18},{3,19},{4,20},{5,21},{6,22},{7,23},{8,24},{9,... | collective-permute-start | bytes 221192 | tf_op jit(solution)/shard_map/ppermute | solution.py:266
  13.5 9.2 %collective-permute-start.2 = (f32[18,3,256]{2,1,0:T(4,128)S(1)}, f32[18,3,256]{2,1,0:T(4,128)S(1)}, u32[]{:S(2)}, u32[]{:S(2)}) collective-permute-start(f32[18,3,256]{2,1,0:T(4,128)S(1)} %pad_maximum_fusion), channel_id=1, source_target_pairs={{0,1},{1,2},{2,3},{3,4},{4,5},{5,6},{6,7},{7,8},{8,9},{9,10},{10,1... | collective-permute-start | bytes 165896 | tf_op jit(solution)/shard_map/ppermute | solution.py:272
  15.5 8.7 %collective-permute-start.3 = (f32[18,3,256]{2,1,0:T(4,128)S(1)}, f32[18,3,256]{2,1,0:T(4,128)S(1)}, u32[]{:S(2)}, u32[]{:S(2)}) collective-permute-start(f32[18,3,256]{2,1,0:T(4,128)S(1)} %pad_maximum_fusion.1), channel_id=1, source_target_pairs={{0,15},{1,0},{2,1},{3,2},{4,3},{5,4},{6,5},{7,6},{8,7},{9,8},{10,9... | collective-permute-start | bytes 165896 | tf_op jit(solution)/shard_map/ppermute | solution.py:274
  24.2 1.0 copy-start.3
  29.8 8.2 %collective-permute-start.8 = (f32[16,128,128]{2,1,0:T(8,128)S(1)}, f32[16,128,128]{2,1,0:T(8,128)S(1)}, u32[]{:S(2)}, u32[]{:S(2)}) collective-permute-start(f32[16,128,128]{2,1,0:T(8,128)S(1)} %get-tuple-element.17), channel_id=1, source_target_pairs={{0,16},{16,0},{1,17},{17,1},{2,18},{18,2},{3,19},{19,3},{4,20},{20... | collective-permute-start | bytes 3145736 | tf_op jit(solution)/shard_map/ppermute | solution.py:298
  39.2 20.8 %all-to-all-start = ((f32[16,136,128]{2,1,0:T(8,128)}), f32[16,136,128]{2,1,0:T(8,128)S(1)}, u32[]{:S(2)}, u32[]{:S(2)}) async-start(f32[16,136,128]{2,1,0:T(8,128)} %shard_map.104), calls=%async_computation | async-start | bytes 2228224 | tf_op jit(solution)/shard_map/all_to_all | solution.py:302
  43.7 15.5 %collective-permute-start.4 = (f32[3,24,256]{2,1,0:T(8,128)S(1)}, f32[3,24,256]{2,1,0:T(8,128)S(1)}, u32[]{:S(2)}, u32[]{:S(2)}) collective-permute-start(f32[3,24,256]{2,1,0:T(8,128)S(1)} %reverse_select_fusion), channel_id=1, source_target_pairs={{0,8},{1,9},{2,10},{3,11},{4,12},{5,13},{6,14},{7,15},{8,0},{9,1},... | collective-permute-start | bytes 221192 | tf_op jit(solution)/shard_map/ppermute | solution.py:267
  47.8 11.5 %collective-permute-start.5 = (f32[3,24,256]{2,1,0:T(8,128)S(1)}, f32[3,24,256]{2,1,0:T(8,128)S(1)}, u32[]{:S(2)}, u32[]{:S(2)}) collective-permute-start(f32[3,24,256]{2,1,0:T(8,128)S(1)} %get-tuple-element.25), channel_id=1, source_target_pairs={{0,16},{1,17},{2,18},{3,19},{4,20},{5,21},{6,22},{7,23},{8,24},{9,... | collective-permute-start | bytes 221192 | tf_op jit(solution)/shard_map/ppermute | solution.py:266
  60.7 30.9 %all-to-all-start.1 = ((f32[16,16,128]{2,1,0:T(8,128)}), f32[16,16,128]{2,1,0:T(8,128)S(1)}, u32[]{:S(2)}, u32[]{:S(2)}) async-start(f32[16,16,128]{2,1,0:T(8,128)} %shard_map.105), calls=%async_computation.1 | async-start | bytes 262144 | tf_op jit(solution)/shard_map/all_to_all | solution.py:304
  79.7 25.8 %collective-permute-start.6 = (f32[18,3,256]{2,1,0:T(4,128)S(1)}, f32[18,3,256]{2,1,0:T(4,128)S(1)}, u32[]{:S(2)}, u32[]{:S(2)}) collective-permute-start(f32[18,3,256]{2,1,0:T(4,128)S(1)} %pad_maximum_fusion.2), channel_id=1, source_target_pairs={{0,1},{1,2},{2,3},{3,4},{4,5},{5,6},{6,7},{7,8},{8,9},{9,10},{10,1... | collective-permute-start | bytes 165896 | tf_op jit(solution)/shard_map/ppermute | solution.py:272
  92.3 17.5 %all-to-all-start.2 = ((f32[32,8,128]{2,1,0:T(8,128)}), f32[32,8,128]{2,1,0:T(8,128)S(1)}, u32[]{:S(2)}, u32[]{:S(2)}) async-start(f32[32,8,128]{2,1,0:T(8,128)} %get-tuple-element.20), calls=%async_computation.2 | async-start | bytes 262144 | tf_op jit(solution)/shard_map/all_to_all | solution.py:308
  100.9 6.0 %collective-permute-start.7 = (f32[18,3,256]{2,1,0:T(4,128)S(1)}, f32[18,3,256]{2,1,0:T(4,128)S(1)}, u32[]{:S(2)}, u32[]{:S(2)}) collective-permute-start(f32[18,3,256]{2,1,0:T(4,128)S(1)} %pad_maximum_fusion.3), channel_id=1, source_target_pairs={{0,15},{1,0},{2,1},{3,2},{4,3},{5,4},{6,5},{7,6},{8,7},{9,8},{10,9... | collective-permute-start | bytes 165896 | tf_op jit(solution)/shard_map/ppermute | solution.py:274

commit v3 on v2

v3 whole, which is shorter than its diff:
```python
import functools
import math

import jax
import jax.numpy as jnp
from jax import lax
from jax.experimental import pallas as pl
from jax.experimental.pallas import tpu as pltpu
from jax.sharding import Mesh, PartitionSpec as P

AXES = ("zh", "x", "core", "y", "zl")
SIZES = (4, 4, 2, 4, 4)
LAT = 32
LON = 16


def lat_lon():
    lat = (lax.axis_index("zh") * 4 + lax.axis_index("x")) * 2 + lax.axis_index("core")
    return lat, lax.axis_index("y") * 4 + lax.axis_index("zl")


def row_pairs():
    first, second = [], []
    for lat in range(LAT):
        for lon in range(LON):
            here = lat * LON + lon
            first.append((here, (lat ^ 1) * LON + lon))
            if lat == 0 or lat == LAT - 1:
                peer = lat * LON + (lon + LON // 2) % LON
            else:
                peer = (lat - 1 if lat % 2 == 0 else lat + 1) * LON + lon
            second.append((here, peer))
    return first, second


def column_pairs():
    right, left = [], []
    for lat in range(LAT):
        for lon in range(LON):
            here = lat * LON + lon
            right.append((here, lat * LON + (lon + 1) % LON))
            left.append((here, lat * LON + (lon - 1) % LON))
    return right, left


H = 12
W = 24
C = 256
FF = 1024
V = 32
CELLS = H * W
WIDE_CELLS = H * V
EDGE = 6 * (H + 6) + 3 * H
PARAMS = pltpu.CompilerParams(vmem_limit_bytes=20 * 1024 * 1024)


def gelu_parts(values):
    phi = 0.5 * (1.0 + lax.erf(values * 0.7071067811865476))
    slope = phi + values * jnp.exp(-0.5 * values * values) * 0.3989422804014327
    return values * phi, slope


def window(wide_ref, row, col, width, lanes):
    return wide_ref[row, col : col + width, lanes]


def convolve(wide_ref, weight, base, width, lanes):
    total = [None] * H
    for col in range(7):
        for row in range(H + 6):
            part = window(wide_ref, row, base + col, width, lanes)
            for tap in range(7):
                out = row - tap
                if 0 <= out < H:
                    term = weight(row, tap, col, lanes) * part
                    total[out] = term if total[out] is None else total[out] + term
    return total


def own_edge_kernel(
    state_hbm, cot_hbm, gain_hbm, w_in_hbm, w_out_hbm,
    to_right, to_left, gain, w_in, w_out,
    state, cot, full, sem,
):
    fetches = [
        pltpu.make_async_copy(source, target, sem.at[i])
        for i, (source, target) in enumerate(
            (
                (state_hbm, state),
                (cot_hbm, cot),
                (gain_hbm, gain),
                (w_in_hbm, w_in),
                (w_out_hbm, w_out),
            )
        )
    ]
    for fetch in fetches:
        fetch.start()
    fetches[0].wait()
    for row in range(H):
        to_right[6 * row : 6 * row + 6, :] = state[row, W - 6 : W, :]
        to_left[6 * row : 6 * row + 6, :] = state[row, 0:6, :]
    fetches[1].wait()
    full[...] = cot[...].astype(jnp.float32)
    for row in range(H):
        place = 6 * H + 3 * row
        to_right[place : place + 3, :] = full[W * row + W - 3 : W * row + W, :]
        to_left[place : place + 3, :] = full[W * row : W * row + 3, :]
    for fetch in fetches[2:]:
        fetch.wait()


def edge_kernel(even_ref, first, second, own_right, own_left, above, below, to_right, to_left):
    even = even_ref[0] == 1
    above[...] = jnp.where(even, second[...], first[...])
    below[...] = jnp.where(even, first[...], second[...])
    to_right[0 : 9 * H, :] = own_right[...]
    to_left[0 : 9 * H, :] = own_left[...]
    for row in range(3):
        for place, ref in ((9 * H, above), (9 * H + 18, below)):
            spot = place + 6 * row
            to_right[spot : spot + 6, :] = ref[row, W - 6 : W, :]
            to_left[spot : spot + 6, :] = ref[row, 0:6, :]


def source_row(above, state, below, row):
    if row < 3:
        return above[row], 9 * H + 6 * row
    if row < H + 3:
        return state[row - 3], 6 * (row - 3)
    return below[row - H - 3], 9 * H + 18 + 6 * (row - H - 3)


def forward_kernel(
    core_ref, above, below, state, before, after, cot, taps, gain, w_in, w_out,
    mine, theirs, hidden, grad_pre, centred_out, inv_out,
    wide, conv, cot_all,
):
    wide[:, 32:40, :] = jnp.zeros((H + 6, 8, C), jnp.float32)
    for row in range(H + 6):
        centre, spot = source_row(above, state, below, row)
        wide[row, 8 : 8 + W, :] = centre
        wide[row, 2:8, :] = before[spot : spot + 6, :]
        wide[row, 8 + W : 14 + W, :] = after[spot : spot + 6, :]
    cot_all[:, 24:32, :] = jnp.zeros((H, 8, C), jnp.float32)
    own = cot[...].astype(jnp.float32)
    for row in range(H):
        place = 6 * H + 3 * row
        cot_all[row, 0:3, :] = before[place : place + 3, :]
        cot_all[row, 3 : 3 + W, :] = own[W * row : W * row + W]
        cot_all[row, 3 + W : 6 + W, :] = after[place : place + 3, :]
    for half in range(2):
        lanes = slice(128 * half, 128 * half + 128)
        total = convolve(
            wide, lambda row, tap, col, ln: taps[7 * tap + col : 7 * tap + col + 1, ln], 2, V, lanes
        )
        for out in range(H):
            conv[V * out : V * out + V, lanes] = total[out]
    values = conv[...]
    centred = values - jnp.mean(values, axis=-1, keepdims=True)
    variance = jnp.mean(centred * centred, axis=-1, keepdims=True)
    inv_std = 1.0 / jnp.sqrt(variance + 1e-06)
    centred = centred * inv_std
    centred_out[...] = centred
    inv_out[...] = jnp.broadcast_to(inv_std, (WIDE_CELLS, 128))
    place = lax.broadcasted_iota(jnp.int32, (H, V, C), 1).reshape(WIDE_CELLS, C)
    inside = (place >= 3) & (place < 3 + W)
    normed = centred * gain[...]
    own_normed = jnp.where(inside, normed, 0.0).astype(jnp.bfloat16)
    normed = normed.astype(jnp.bfloat16)
    cotangent = cot_all[...].reshape(WIDE_CELLS, C)
    own_cot = jnp.where(inside, cotangent, 0.0).astype(jnp.bfloat16)
    cotangent = cotangent.astype(jnp.bfloat16)
    core = core_ref[0]
    for part in range(4):
        cols = slice(256 * part, 256 * part + 256)
        pre_act = jnp.dot(normed, w_in[:, cols], preferred_element_type=jnp.float32)
        grad_hidden = lax.dot_general(
            cotangent, w_out[cols, :], (((1,), (1,)), ((), ())), preferred_element_type=jnp.float32
        )
        value, slope = gelu_parts(pre_act)
        hidden[:, cols] = value.astype(jnp.bfloat16)
        grad_pre[:, cols] = (grad_hidden * slope).astype(jnp.bfloat16)
    for part in range(4):
        cols = slice(256 * part, 256 * part + 256)
        for side, (left, right) in enumerate(
            ((grad_pre[:, cols], own_normed), (hidden[:, cols], own_cot))
        ):
            product = lax.dot_general(
                left, right, (((0,), (0,)), ((), ())), preferred_element_type=jnp.float32
            )
            for x in range(4):
                for run in range(2):
                    lanes = slice(128 * run, 128 * run + 128)
                    ours = product[64 * x : 64 * x + 32, lanes]
                    other = product[64 * x + 32 : 64 * x + 64, lanes]
                    keep = jnp.where(core == 0, ours, other)
                    send = jnp.where(core == 0, other, ours)
                    row = 32 * (2 * side + run) + 8 * part
                    mine[4 * x : 4 * x + 4, row : row + 8, :] = keep.reshape(4, 8, 128)
                    theirs[4 * x : 4 * x + 4, row : row + 8, :] = send.reshape(4, 8, 128)


def backward_kernel(
    above, below, state, before, after, gain, w_in, grad_pre, centred_in, inv_in,
    grad_conv, out,
    wide,
):
    for row in range(H + 6):
        centre, spot = source_row(above, state, below, row)
        wide[row, 8 : 8 + W, :] = centre
        wide[row, 5:8, :] = before[spot + 3 : spot + 6, :]
        wide[row, 8 + W : 11 + W, :] = after[spot : spot + 3, :]
    grad_normed = lax.dot_general(
        grad_pre[...], w_in[...], (((1,), (1,)), ((), ())), preferred_element_type=jnp.float32
    )
    centred = centred_in[...]
    inv_std = inv_in[...][:, 0:1]
    scaled = grad_normed * gain[...]
    grad = inv_std * (
        scaled
        - jnp.mean(scaled, axis=-1, keepdims=True)
        - centred * jnp.mean(scaled * centred, axis=-1, keepdims=True)
    )
    place = lax.broadcasted_iota(jnp.int32, (H, V, C), 1).reshape(WIDE_CELLS, C)
    inside = (place >= 3) & (place < 3 + W)
    gain_sum = jnp.sum(jnp.where(inside, grad_normed * centred, 0.0), axis=0, keepdims=True)
    grad_conv[...] = grad.reshape(H, V, C)
    for half in range(2):
        lanes = slice(128 * half, 128 * half + 128)
        grads = [grad_conv[row, 3 : 3 + W, lanes] for row in range(H)]
        for col in range(7):
            total = [jnp.zeros((8, 128), jnp.float32)] * 7
            for row in range(H + 6):
                part = window(wide, row, 5 + col, W, lanes)
                for tap in range(7):
                    if 0 <= row - tap < H:
                        term = part * grads[row - tap]
                        total[tap] = total[tap] + ((term[0:8] + term[8:16]) + term[16:24])
            for tap in range(7):
                spot = 64 * half + 7 * tap + col
                out[spot : spot + 1, :] = jnp.sum(total[tap], axis=0, keepdims=True)
        out[64 * half + 49 : 64 * half + 50, :] = gain_sum[:, lanes]
        out[64 * half + 50 : 64 * half + 64, :] = jnp.zeros((14, 128), jnp.float32)


def adjoint_kernel(
    where_ref, first, second, grad_conv, cot, taps, state, hidden, w_out,
    out, block_out,
    wide, rim, grad, branch_ref,
):
    branch = jnp.dot(hidden[...], w_out[...], preferred_element_type=jnp.float32)
    branch_ref[...] = branch.reshape(H, V, C)
    block_out[...] = (state[...] + branch_ref[:, 3 : 3 + W, :]).reshape(CELLS, C).astype(jnp.bfloat16)
    lat = where_ref[0]
    even = where_ref[1] == 1
    wide[0:3] = jnp.where(even, second[...], first[...])
    wide[3 : 3 + H] = grad_conv[...]
    wide[3 + H :] = jnp.where(even, first[...], second[...])
    for tap in range(7):
        here = taps[7 * tap : 7 * tap + 7, :]
        turned = taps[7 * (6 - tap) : 7 * (6 - tap) + 7, :]
        rim[0, tap, 0:7, :] = jnp.where(lat == 0, turned, here)
        rim[1, tap, 0:7, :] = jnp.where(lat == LAT - 1, turned, here)

    def weight(row, tap, col, lanes):
        if row < 3:
            return rim[0, 6 - tap, 6 - col : 7 - col, lanes]
        if row >= H + 3:
            return rim[1, 6 - tap, 6 - col : 7 - col, lanes]
        place = 7 * (6 - tap) + 6 - col
        return taps[place : place + 1, lanes]

    for half in range(2):
        lanes = slice(128 * half, 128 * half + 128)
        total = convolve(wide, weight, 0, W, lanes)
        for row in range(H):
            grad[W * row : W * row + W, lanes] = total[row]
    out[...] = (cot[...].astype(jnp.float32) + grad[...]).astype(jnp.bfloat16)


def join_kernel(mine, theirs, taps, out):
    out[:, 0:128, :] = mine[...] + theirs[...]
    out[:, 128:136, :] = taps[...].reshape(16, 8, 128)


def plane_kernel(got, out):
    total = got[0]
    for peer in range(1, 16):
        total = total + got[peer]
    for zh in range(4):
        for zl in range(4):
            place = 4 * zh + zl
            for run in range(4):
                row = 32 * run + 8 * zh + 2 * zl
                out[place, 2 * run : 2 * run + 2, :] = total[row : row + 2]
            out[place, 8:16, :] = total[128:136]


def column_kernel(scale, got, weight_grads, shared):
    total = got[0]
    for peer in range(1, 16):
        total = total + got[peer]
    total = total * scale
    for run in range(4):
        weight_grads[:, 128 * run : 128 * run + 128] = total[2 * run : 2 * run + 2]
    for peer in range(32):
        shared[peer] = total[8:16]


def total_kernel(got, taps, gain):
    for half in range(2):
        rows = []
        for place in range(8 * half, 8 * half + 8):
            x, y = place // 4, place % 4
            rows.append(got[8 * x + y] + got[8 * x + 4 + y])
        table = jnp.concatenate(rows, 0)
        taps[:, 128 * half : 128 * half + 128] = table[0:49]
        gain[:, 128 * half : 128 * half + 128] = table[49:50]


def call(kernel, out, *args, scratch=(), scalars=0, held=()):
    vmem = pl.BlockSpec(memory_space=pltpu.VMEM)
    smem = pl.BlockSpec(memory_space=pltpu.SMEM)
    anywhere = pl.BlockSpec(memory_space=pltpu.HBM)
    return pl.pallas_call(
        kernel,
        out_shape=[jax.ShapeDtypeStruct(s, d) for s, d in out],
        in_specs=[
            smem if i < scalars else anywhere if i in held else vmem for i in range(len(args))
        ],
        out_specs=[vmem] * len(out),
        scratch_shapes=[pltpu.VMEM(*s) if isinstance(s, tuple) else s for s in scratch],
        compiler_params=PARAMS,
    )(*args)


F32 = jnp.float32
BF16 = jnp.bfloat16
WIDE = ((H + 6, 40, C), F32)


def row_exchange(values, even, pole):
    head, tail = values[:3], values[-3:]
    first, second = row_pairs()
    outer = jnp.where(even, head, tail)
    outer = jnp.where(pole, jnp.flip(outer, 0), outer)
    got_first = lax.ppermute(jnp.where(even, tail, head), AXES, first)
    got_second = lax.ppermute(outer, AXES, second)
    return got_first, got_second


def body(state_field, cotangent, depthwise, norm_gain, w_in, w_out):
    grad_scale = 1.0 / math.sqrt(CELLS * LAT * LON)
    lat, _ = lat_lon()
    lat = lat.astype(jnp.int32)
    even = lat % 2 == 0
    pole = (lat == 0) | (lat == LAT - 1)
    parity = even.astype(jnp.int32)
    core = lax.axis_index("core").astype(jnp.int32).reshape(1)
    cot = cotangent.reshape(CELLS, C)
    gain = norm_gain.reshape(1, C)
    *own_edges, gain, w_in, w_out = call(
        own_edge_kernel,
        [
            ((9 * H, C), F32),
            ((9 * H, C), F32),
            ((1, C), F32),
            ((C, FF), BF16),
            ((FF, C), BF16),
        ],
        state_field, cot, gain, w_in, w_out,
        scratch=[
            ((H, W, C), F32),
            ((CELLS, C), BF16),
            ((CELLS, C), F32),
            pltpu.SemaphoreType.DMA((5,)),
        ],
        held=(0, 1, 2, 3, 4),
    )
    rows = row_exchange(state_field, even, pole)
    above, below, to_right, to_left = call(
        edge_kernel,
        [((3, W, C), F32), ((3, W, C), F32), ((EDGE, C), F32), ((EDGE, C), F32)],
        parity.reshape(1), *rows, *own_edges,
        scalars=1,
    )
    right, left = column_pairs()
    before = lax.ppermute(to_right, AXES, right)
    after = lax.ppermute(to_left, AXES, left)
    pieces = (above, below, state_field, before, after)
    mine, theirs, hidden, grad_pre, centred, inv_std = call(
        forward_kernel,
        [
            ((16, 128, 128), F32),
            ((16, 128, 128), F32),
            ((WIDE_CELLS, FF), BF16),
            ((WIDE_CELLS, FF), BF16),
            ((WIDE_CELLS, C), F32),
            ((WIDE_CELLS, 128), F32),
        ],
        core, *pieces, cot, depthwise, gain, w_in, w_out,
        scratch=[
            WIDE,
            ((WIDE_CELLS, C), F32),
            ((H, V, C), F32),
        ],
        scalars=1,
    )
    theirs = lax.ppermute(theirs, "core", [(0, 1), (1, 0)])
    grad_conv, taps = call(
        backward_kernel,
        [((H, V, C), F32), ((128, 128), F32)],
        *pieces, gain, w_in, grad_pre, centred, inv_std,
        scratch=[WIDE],
    )
    (joined,) = call(join_kernel, [((16, 136, 128), F32)], mine, theirs, taps)
    plane = lax.all_to_all(joined, ("x", "y"), split_axis=0, concat_axis=0, tiled=True)
    grad_rows = row_exchange(grad_conv, even, pole)
    plane, grad_rows = lax.optimization_barrier((plane, grad_rows))
    (spread,) = call(plane_kernel, [((16, 16, 128), F32)], plane)
    column = lax.all_to_all(spread, ("zh", "zl"), split_axis=0, concat_axis=0, tiled=True)
    grad_input, block_out = call(
        adjoint_kernel,
        [((CELLS, C), BF16), ((CELLS, C), BF16)],
        jnp.stack([lat, parity]), *grad_rows, grad_conv, cot, depthwise, state_field, hidden, w_out,
        scratch=[
            ((H + 6, V, C), F32),
            ((2, 7, 8, C), F32),
            ((CELLS, C), F32),
            ((H, V, C), F32),
        ],
        scalars=1,
    )
    column, grad_input = lax.optimization_barrier((column, grad_input))
    weight_grads, shared = call(
        functools.partial(column_kernel, grad_scale), [((2, 512), F32), ((32, 8, 128), F32)], column
    )
    shared = lax.all_to_all(shared, ("x", "core", "y"), split_axis=0, concat_axis=0, tiled=True)
    tap_total, gain_total = call(total_kernel, [((49, C), F32), ((1, C), F32)], shared)
    return (
        block_out.reshape(H, W, C),
        grad_input.reshape(H, W, C),
        weight_grads,
        tap_total,
        gain_total.reshape(C),
    )


def solution(mesh):
    split = Mesh(mesh.devices.reshape(SIZES), AXES)
    cells = P(("zh", "x", "core"), ("y", "zl"), None)
    return jax.shard_map(
        body,
        mesh=split,
        in_specs=(cells, cells, P(), P(), P(), P()),
        out_specs=(cells, cells, P(AXES, None), P(), P()),
        check_vma=False,
    )
```

time: 111 us -> 109 us (0.982)
  starting transfers between devices: 73.5 us -> 50.7 us
  blocking collectives: 0 us -> 14.5 us
  local copies, waits for them, and re-layouts: 2.07 us -> 4.64 us
  Pallas kernels: 12.5 us -> 14.8 us
  waiting for transfers between devices: 20.3 us -> 21.5 us
    all_to_all x0 -> x1, blocking collectives: none -> 14.5 us  [body(): lax.all_to_all(shared, ('x', 'core', 'y'), split_axis=0, concat_axis=0, t...]
    all_to_all x1 -> x0, starting transfers between devices: 8.52 us -> none  [body(): lax.all_to_all(shared, ('x', 'core', 'y'), split_axis=0, concat_axis=0, t...]
    ppermute x8 -> x6, starting transfers between devices: 35.7 us -> 27.4 us  [the longest x2 10 us: row_exchange(): got_first = lax.ppermute(jnp.where(even, tail, head), AXES, first)]
    all_to_all x1, starting transfers between devices: 18.9 us -> 11.4 us  [body(): lax.all_to_all(spread, ('zh', 'zl'), split_axis=0, concat_axis=0, tiled=T...]
    all_to_all x1, starting transfers between devices: 4.46 us -> 8.8 us  [body(): lax.all_to_all(joined, ('x', 'y'), split_axis=0, concat_axis=0, tiled=True)]
    unnamed x12 -> x16, local copies, waits for them, and re-layouts: 1.06 us -> 4.64 us
    ppermute x1, starting transfers between devices: 5.95 us -> 3.02 us  [body(): theirs = lax.ppermute(theirs, 'core', [(0, 1), (1, 0)])]
    pallas_call x7 -> x9, Pallas kernels: 12.5 us -> 14.8 us  [call(): pl.pallas_call(kernel, out_shape=[jax.ShapeDtypeStruct(s, d) for s, d in...]
  transfers between devices with their start and end apart: 12 -> 9, of which waited for: 6 -> 5; matrix products, arithmetic and copies ran while one was open for 1% -> 0% of each run, Pallas kernels for 5% -> 6%
where the time goes in v3:
time: 109 us; the launch traced here: 108 us
  starting transfers between devices  50.7 us (47%)
  waiting for transfers between devices  21.5 us (20%)
  Pallas kernels  14.8 us (14%)
  blocking collectives  14.5 us (13%)
  local copies, waits for them, and re-layouts  4.64 us (4%)
  other arithmetic  1.11 us (1%)
    pallas_call x9, Pallas kernels, call(): pl.pallas_call(kernel, out_shape=[jax.ShapeDtypeStruct(s, d) for s, d in...  14.8 us
    all_to_all x1, blocking collectives, body(): lax.all_to_all(shared, ('x', 'core', 'y'), split_axis=0, concat_axis=0, t...  14.5 us
    all_to_all x1, starting transfers between devices, body(): lax.all_to_all(spread, ('zh', 'zl'), split_axis=0, concat_axis=0, tiled=T...  11.4 us
    ppermute x2, starting transfers between devices, row_exchange(): got_first = lax.ppermute(jnp.where(even, tail, head), AXES, first)  10 us
    all_to_all x1, starting transfers between devices, body(): lax.all_to_all(joined, ('x', 'y'), split_axis=0, concat_axis=0, tiled=True)  8.8 us
    all_to_all x1, waiting for transfers between devices, body(): lax.all_to_all(spread, ('zh', 'zl'), split_axis=0, concat_axis=0, tiled=T...  8.3 us
    ppermute x2, waiting for transfers between devices, row_exchange(): got_second = lax.ppermute(outer, AXES, second)  8.25 us
    ppermute x2, starting transfers between devices, row_exchange(): got_second = lax.ppermute(outer, AXES, second)  8.24 us
  transfers between devices with their start and end apart: 9, of which 5 were waited for; matrix products, arithmetic and copies ran while one was open for 0% of the time, Pallas kernels for 6%

profile of v3, /device:TPU:1, one launch (start us, length us, event | category | flops | bytes accessed | tf_op | source)
XLA Modules:
  0.0 108.0 jit_solution(852972779559360541)
XLA Ops:
  0.7 0.0 copy-start.1
  0.7 0.0 copy-start.3
  0.7 1.0 slice_select_fusion.2
  1.7 4.5 %collective-permute-start.1 = (f32[3,24,256]{2,1,0:T(8,128)S(1)}, f32[3,24,256]{2,1,0:T(8,128)S(1)}, u32[]{:S(2)}, u32[]{:S(2)}) collective-permute-start(f32[3,24,256]{2,1,0:T(8,128)S(1)} %reverse_select_fusion.1), channel_id=1, source_target_pairs={{0,8},{1,9},{2,10},{3,11},{4,12},{5,13},{6,14},{7,15},{8,0},{9,1},... | collective-permute-start | bytes 221192 | tf_op jit(solution)/shard_map/ppermute | solution.py:349
  6.2 6.2 %collective-permute-start = (f32[3,24,256]{2,1,0:T(8,128)S(1)}, f32[3,24,256]{2,1,0:T(8,128)S(1)}, u32[]{:S(2)}, u32[]{:S(2)}) collective-permute-start(f32[3,24,256]{2,1,0:T(8,128)S(1)} %get-tuple-element.64), channel_id=1, source_target_pairs={{0,16},{1,17},{2,18},{3,19},{4,20},{5,21},{6,22},{7,23},{8,24},{9,... | collective-permute-start | bytes 221192 | tf_op jit(solution)/shard_map/ppermute | solution.py:348
  12.4 0.0 copy-start
  12.4 1.0 copy-done
  13.4 0.0 copy-start.2
  13.4 0.9 copy-done.2
  14.3 0.0 copy-start.4
  14.3 1.0 copy-done.4
  15.3 0.0 copy-start.5
  15.3 1.0 copy-done.5
  16.4 0.0 copy-start.7
  16.4 0.7 copy-done.7
  17.0 0.0 copy-start.6
  17.0 0.4 shard_map.101
  17.5 0.0 collective-permute-done.1.second
  17.5 0.0 collective-permute-done.first
  17.6 1.9 %collective-permute-start.2 = (f32[144,256]{1,0:T(8,128)S(1)}, f32[144,256]{1,0:T(8,128)S(1)}, u32[]{:S(2)}, u32[]{:S(2)}) collective-permute-start(f32[144,256]{1,0:T(8,128)S(1)} %get-tuple-element.37), channel_id=1, source_target_pairs={{0,1},{1,2},{2,3},{3,4},{4,5},{5,6},{6,7},{7,8},{8,9},{9,10},{10,1... | collective-permute-start | bytes 442376 | tf_op jit(solution)/shard_map/ppermute | solution.py:389
  19.5 7.3 %collective-permute-start.3 = (f32[144,256]{1,0:T(8,128)S(1)}, f32[144,256]{1,0:T(8,128)S(1)}, u32[]{:S(2)}, u32[]{:S(2)}) collective-permute-start(f32[144,256]{1,0:T(8,128)S(1)} %get-tuple-element.38), channel_id=1, source_target_pairs={{0,15},{1,0},{2,1},{3,2},{4,3},{5,4},{6,5},{7,6},{8,7},{9,8},{10,9... | collective-permute-start | bytes 442376 | tf_op jit(solution)/shard_map/ppermute | solution.py:390
  26.8 2.1 %collective-permute-done.2.before = f32[144,256]{1,0:T(8,128)S(1)} collective-permute-done((f32[144,256]{1,0:T(8,128)S(1)}, f32[144,256]{1,0:T(8,128)S(1)}, u32[]{:S(2)}, u32[]{:S(2)}) %collective-permute-start.2) | collective-permute-done | bytes 147488 | tf_op jit(solution)/shard_map/ppermute | solution.py:389
  28.9 0.8 collective-permute-done.3.after
  29.7 0.0 copy-done.1
  29.7 0.0 copy-done.3
  29.7 0.0 copy-done.6
  29.7 5.0 %shard_map.103 = (f32[16,128,128]{2,1,0:T(8,128)S(1)}, f32[16,128,128]{2,1,0:T(8,128)S(1)}, bf16[384,1024]{1,0:T(8,128)(2,1)S(1)}, bf16[384,1024]{1,0:T(8,128)(2...) custom-call(s32[1]{0:T(128)} %bitcast.2.core_ref, f32[3,24,256]{2,1,0:T(8,128)S(1)} %get-tuple-element.35.above, ...), custom_call_target="tpu_custom_call" | custom-call | tf_op jit(solution)/shard_map/pallas_call | solution.py:326
  34.7 3.0 %collective-permute-start.4 = (f32[16,128,128]{2,1,0:T(8,128)S(1)}, f32[16,128,128]{2,1,0:T(8,128)S(1)}, u32[]{:S(2)}, u32[]{:S(2)}) collective-permute-start(f32[16,128,128]{2,1,0:T(8,128)S(1)} %get-tuple-element.43), channel_id=1, source_target_pairs={{0,16},{16,0},{1,17},{17,1},{2,18},{18,2},{3,19},{19,3},{4,20},{20... | collective-permute-start | bytes 3145736 | tf_op jit(solution)/shard_map/ppermute | solution.py:410
  37.7 2.7 %shard_map.104 = (f32[12,32,256]{2,1,0:T(8,128)S(1)}, f32[128,128]{1,0:T(8,128)S(1)}) custom-call(f32[3,24,256]{2,1,0:T(8,128)S(1)} %get-tuple-element.35.above, f32[3,24,256]{2,1,0:T(8,128)S(1)} %get-tuple-element.36.below, f32[12,24,256]{2,1,0:T(8,128)S(1)} %copy-done.1, f32[144,256]{1,0:T(8,128)S(1)} %collective-permute-done.2.before, ...), custom_call_target="tpu_custom_call" | custom-call | tf_op jit(solution)/shard_map/pallas_call | solution.py:326
  40.4 0.0 collective-permute-done.4.theirs
  40.4 1.1 %shard_map.105 = f32[16,136,128]{2,1,0:T(8,128)} custom-call(f32[16,128,128]{2,1,0:T(8,128)S(1)} %get-tuple-element.42.mine, f32[16,128,128]{2,1,0:T(8,128)S(1)} %collective-permute-done.4.theirs, f32[128,128]{1,0:T(8,128)S(1)} %get-tuple-element.47.taps), custom_call_target="tpu_custom_call" | custom-call | tf_op jit(solution)/shard_map/pallas_call | solution.py:326
  41.5 8.8 %all-to-all-start = ((f32[16,136,128]{2,1,0:T(8,128)}), f32[16,136,128]{2,1,0:T(8,128)S(1)}, u32[]{:S(2)}, u32[]{:S(2)}) async-start(f32[16,136,128]{2,1,0:T(8,128)} %shard_map.105), calls=%async_computation | async-start | bytes 2228224 | tf_op jit(solution)/shard_map/all_to_all | solution.py:418
  50.3 3.7 %collective-permute-start.6 = (f32[3,32,256]{2,1,0:T(8,128)S(1)}, f32[3,32,256]{2,1,0:T(8,128)S(1)}, u32[]{:S(2)}, u32[]{:S(2)}) collective-permute-start(f32[3,32,256]{2,1,0:T(8,128)S(1)} %reverse_select_fusion), channel_id=1, source_target_pairs={{0,8},{1,9},{2,10},{3,11},{4,12},{5,13},{6,14},{7,15},{8,0},{9,1},... | collective-permute-start | bytes 294920 | tf_op jit(solution)/shard_map/ppermute | solution.py:349
  54.1 3.8 %collective-permute-start.5 = (f32[3,32,256]{2,1,0:T(8,128)S(1)}, f32[3,32,256]{2,1,0:T(8,128)S(1)}, u32[]{:S(2)}, u32[]{:S(2)}) collective-permute-start(f32[3,32,256]{2,1,0:T(8,128)S(1)} %get-tuple-element.62), channel_id=1, source_target_pairs={{0,16},{1,17},{2,18},{3,19},{4,20},{5,21},{6,22},{7,23},{8,24},{9,... | collective-permute-start | bytes 294920 | tf_op jit(solution)/shard_map/ppermute | solution.py:348
  57.9 8.3 %collective-permute-done.6.second = f32[3,32,256]{2,1,0:T(8,128)S(1)} collective-permute-done((f32[3,32,256]{2,1,0:T(8,128)S(1)}, f32[3,32,256]{2,1,0:T(8,128)S(1)}, u32[]{:S(2)}, u32[]{:S(2)}) %collective-permute-start.6) | collective-permute-done | bytes 98336 | tf_op jit(solution)/shard_map/ppermute | solution.py:349
  66.1 0.0 collective-permute-done.5.first
  66.1 2.0 %all-to-all-done.got = f32[16,136,128]{2,1,0:T(8,128)S(1)} async-done(((f32[16,136,128]{2,1,0:T(8,128)}), f32[16,136,128]{2,1,0:T(8,128)S(1)}, u32[]{:S(2)}, u32[]{:S(2)}) %all-to-all-start) | async-done | bytes 1114144 | tf_op jit(solution)/shard_map/all_to_all | solution.py:418
  68.1 0.7 shard_map.107
  68.8 11.4 %all-to-all-start.1 = ((f32[16,16,128]{2,1,0:T(8,128)}), f32[16,16,128]{2,1,0:T(8,128)S(1)}, u32[]{:S(2)}, u32[]{:S(2)}) async-start(f32[16,16,128]{2,1,0:T(8,128)} %shard_map.107), calls=%async_computation.1 | async-start | bytes 262144 | tf_op jit(solution)/shard_map/all_to_all | solution.py:422
  80.3 0.1 pad_add_fusion.where_ref
  80.3 3.6 %shard_map.106 = (bf16[288,256]{1,0:T(8,128)(2,1)}, bf16[288,256]{1,0:T(8,128)(2,1)}) custom-call(s32[2]{0:T(128)S(1)} %pad_add_fusion.where_ref, f32[3,32,256]{2,1,0:T(8,128)S(1)} %collective-permute-done.5.first, f32[3,32,256]{2,1,0:T(8,128)S(1)} %collective-permute-done.6.second, f32[12,32,256]{2,1,0:T(8,128)S(1)} %get-tuple-element.48.grad_conv, ...), custom_call_target="tpu_custom_call" | custom-call | tf_op jit(solution)/shard_map/pallas_call | solution.py:326
  83.9 8.3 %all-to-all-done.1.got = f32[16,16,128]{2,1,0:T(8,128)S(1)} async-done(((f32[16,16,128]{2,1,0:T(8,128)}), f32[16,16,128]{2,1,0:T(8,128)S(1)}, u32[]{:S(2)}, u32[]{:S(2)}) %all-to-all-start.1) | async-done | bytes 131104 | tf_op jit(solution)/shard_map/all_to_all | solution.py:422
  92.2 0.6 shard_map.108
  92.9 14.5 %all_to_all.15.got = f32[32,8,128]{2,1,0:T(8,128)S(1)} all-to-all(f32[32,8,128]{2,1,0:T(8,128)S(1)} %get-tuple-element.58), channel_id=1, replica_groups=mesh['zh'=4,'x'=4,'core'=2,'y'=4,'zl'=4] {'x','core','y'}, dimensions={0} | all-to-all | bytes 262144 | tf_op jit(solution)/shard_map/all_to_all | solution.py:439
  107.4 0.6 shard_map.109
  (4 shorter events, 0.1 us)
Async XLA Ops:
  0.7 29.0 %copy-start.1 = (f32[12,24,256]{2,1,0:T(8,128)S(1)}, f32[12,24,256]{2,1,0:T(8,128)}, u32[]{:S(2)}) copy-start(f32[12,24,256]{2,1,0:T(8,128)} %state.5) | copy-start | bytes 884740
  0.7 29.0 %copy-start.3 = (bf16[12,24,256]{2,1,0:T(8,128)(2,1)S(1)}, bf16[12,24,256]{2,1,0:T(8,128)(2,1)}, u32[]{:S(2)}) copy-start(bf16[12,24,256]{2,1,0:T(8,128)(2,1)} %param.7) | copy-start | bytes 442372
  1.7 15.8 %collective-permute-start.1 = (f32[3,24,256]{2,1,0:T(8,128)S(1)}, f32[3,24,256]{2,1,0:T(8,128)S(1)}, u32[]{:S(2)}, u32[]{:S(2)}) collective-permute-start(f32[3,24,256]{2,1,0:T(8,128)S(1)} %reverse_select_fusion.1), channel_id=1, source_target_pairs={{0,8},{1,9},{2,10},{3,11},{4,12},{5,13},{6,14},{7,15},{8,0},{9,1},... | collective-permute-start | bytes 221192 | tf_op jit(solution)/shard_map/ppermute | solution.py:349
  6.2 11.3 %collective-permute-start = (f32[3,24,256]{2,1,0:T(8,128)S(1)}, f32[3,24,256]{2,1,0:T(8,128)S(1)}, u32[]{:S(2)}, u32[]{:S(2)}) collective-permute-start(f32[3,24,256]{2,1,0:T(8,128)S(1)} %get-tuple-element.64), channel_id=1, source_target_pairs={{0,16},{1,17},{2,18},{3,19},{4,20},{5,21},{6,22},{7,23},{8,24},{9,... | collective-permute-start | bytes 221192 | tf_op jit(solution)/shard_map/ppermute | solution.py:348
  12.4 1.0 copy-start
  13.4 0.9 copy-start.2
  14.3 1.0 copy-start.4
  15.3 1.0 copy-start.5
  16.4 0.7 copy-start.7
  17.0 12.7 %copy-start.6 = (f32[49,256]{1,0:T(8,128)S(1)}, f32[49,256]{1,0:T(8,128)}, u32[]{:S(2)}) copy-start(f32[49,256]{1,0:T(8,128)} %taps.3) | copy-start | bytes 150532
  17.6 11.3 %collective-permute-start.2 = (f32[144,256]{1,0:T(8,128)S(1)}, f32[144,256]{1,0:T(8,128)S(1)}, u32[]{:S(2)}, u32[]{:S(2)}) collective-permute-start(f32[144,256]{1,0:T(8,128)S(1)} %get-tuple-element.37), channel_id=1, source_target_pairs={{0,1},{1,2},{2,3},{3,4},{4,5},{5,6},{6,7},{7,8},{8,9},{9,10},{10,1... | collective-permute-start | bytes 442376 | tf_op jit(solution)/shard_map/ppermute | solution.py:389
  19.5 10.2 %collective-permute-start.3 = (f32[144,256]{1,0:T(8,128)S(1)}, f32[144,256]{1,0:T(8,128)S(1)}, u32[]{:S(2)}, u32[]{:S(2)}) collective-permute-start(f32[144,256]{1,0:T(8,128)S(1)} %get-tuple-element.38), channel_id=1, source_target_pairs={{0,15},{1,0},{2,1},{3,2},{4,3},{5,4},{6,5},{7,6},{8,7},{9,8},{10,9... | collective-permute-start | bytes 442376 | tf_op jit(solution)/shard_map/ppermute | solution.py:390
  34.7 5.7 %collective-permute-start.4 = (f32[16,128,128]{2,1,0:T(8,128)S(1)}, f32[16,128,128]{2,1,0:T(8,128)S(1)}, u32[]{:S(2)}, u32[]{:S(2)}) collective-permute-start(f32[16,128,128]{2,1,0:T(8,128)S(1)} %get-tuple-element.43), channel_id=1, source_target_pairs={{0,16},{16,0},{1,17},{17,1},{2,18},{18,2},{3,19},{19,3},{4,20},{20... | collective-permute-start | bytes 3145736 | tf_op jit(solution)/shard_map/ppermute | solution.py:410
  41.5 26.6 %all-to-all-start = ((f32[16,136,128]{2,1,0:T(8,128)}), f32[16,136,128]{2,1,0:T(8,128)S(1)}, u32[]{:S(2)}, u32[]{:S(2)}) async-start(f32[16,136,128]{2,1,0:T(8,128)} %shard_map.105), calls=%async_computation | async-start | bytes 2228224 | tf_op jit(solution)/shard_map/all_to_all | solution.py:418
  50.3 15.8 %collective-permute-start.6 = (f32[3,32,256]{2,1,0:T(8,128)S(1)}, f32[3,32,256]{2,1,0:T(8,128)S(1)}, u32[]{:S(2)}, u32[]{:S(2)}) collective-permute-start(f32[3,32,256]{2,1,0:T(8,128)S(1)} %reverse_select_fusion), channel_id=1, source_target_pairs={{0,8},{1,9},{2,10},{3,11},{4,12},{5,13},{6,14},{7,15},{8,0},{9,1},... | collective-permute-start | bytes 294920 | tf_op jit(solution)/shard_map/ppermute | solution.py:349
  54.1 12.1 %collective-permute-start.5 = (f32[3,32,256]{2,1,0:T(8,128)S(1)}, f32[3,32,256]{2,1,0:T(8,128)S(1)}, u32[]{:S(2)}, u32[]{:S(2)}) collective-permute-start(f32[3,32,256]{2,1,0:T(8,128)S(1)} %get-tuple-element.62), channel_id=1, source_target_pairs={{0,16},{1,17},{2,18},{3,19},{4,20},{5,21},{6,22},{7,23},{8,24},{9,... | collective-permute-start | bytes 294920 | tf_op jit(solution)/shard_map/ppermute | solution.py:348
  68.8 23.4 %all-to-all-start.1 = ((f32[16,16,128]{2,1,0:T(8,128)}), f32[16,16,128]{2,1,0:T(8,128)S(1)}, u32[]{:S(2)}, u32[]{:S(2)}) async-start(f32[16,16,128]{2,1,0:T(8,128)} %shard_map.107), calls=%async_computation.1 | async-start | bytes 262144 | tf_op jit(solution)/shard_map/all_to_all | solution.py:422

commit v4 on v3

--- a/solution.py
+++ b/solution.py
@@ -49,7 +49,8 @@
 FF = 1024
 V = 32
 CELLS = H * W
-WIDE_CELLS = H * V
+M = 16
+HALF_CELLS = H * M
 EDGE = 6 * (H + 6) + 3 * H
 PARAMS = pltpu.CompilerParams(vmem_limit_bytes=20 * 1024 * 1024)
 
@@ -131,47 +132,14 @@
     return below[row - H - 3], 9 * H + 18 + 6 * (row - H - 3)
 
 
-def forward_kernel(
-    core_ref, above, below, state, before, after, cot, taps, gain, w_in, w_out,
-    mine, theirs, hidden, grad_pre, centred_out, inv_out,
-    wide, conv, cot_all,
-):
-    wide[:, 32:40, :] = jnp.zeros((H + 6, 8, C), jnp.float32)
-    for row in range(H + 6):
-        centre, spot = source_row(above, state, below, row)
-        wide[row, 8 : 8 + W, :] = centre
-        wide[row, 2:8, :] = before[spot : spot + 6, :]
-        wide[row, 8 + W : 14 + W, :] = after[spot : spot + 6, :]
-    cot_all[:, 24:32, :] = jnp.zeros((H, 8, C), jnp.float32)
-    own = cot[...].astype(jnp.float32)
-    for row in range(H):
-        place = 6 * H + 3 * row
-        cot_all[row, 0:3, :] = before[place : place + 3, :]
-        cot_all[row, 3 : 3 + W, :] = own[W * row : W * row + W]
-        cot_all[row, 3 + W : 6 + W, :] = after[place : place + 3, :]
-    for half in range(2):
-        lanes = slice(128 * half, 128 * half + 128)
-        total = convolve(
-            wide, lambda row, tap, col, ln: taps[7 * tap + col : 7 * tap + col + 1, ln], 2, V, lanes
-        )
-        for out in range(H):
-            conv[V * out : V * out + V, lanes] = total[out]
-    values = conv[...]
+def normalise(values):
     centred = values - jnp.mean(values, axis=-1, keepdims=True)
     variance = jnp.mean(centred * centred, axis=-1, keepdims=True)
     inv_std = 1.0 / jnp.sqrt(variance + 1e-06)
-    centred = centred * inv_std
-    centred_out[...] = centred
-    inv_out[...] = jnp.broadcast_to(inv_std, (WIDE_CELLS, 128))
-    place = lax.broadcasted_iota(jnp.int32, (H, V, C), 1).reshape(WIDE_CELLS, C)
-    inside = (place >= 3) & (place < 3 + W)
-    normed = centred * gain[...]
-    own_normed = jnp.where(inside, normed, 0.0).astype(jnp.bfloat16)
-    normed = normed.astype(jnp.bfloat16)
-    cotangent = cot_all[...].reshape(WIDE_CELLS, C)
-    own_cot = jnp.where(inside, cotangent, 0.0).astype(jnp.bfloat16)
-    cotangent = cotangent.astype(jnp.bfloat16)
-    core = core_ref[0]
+    return centred * inv_std, inv_std
+
+
+def activate(normed, cotangent, w_in, w_out, hidden, grad_pre):
     for part in range(4):
         cols = slice(256 * part, 256 * part + 256)
         pre_act = jnp.dot(normed, w_in[:, cols], preferred_element_type=jnp.float32)
@@ -181,11 +149,12 @@
         value, slope = gelu_parts(pre_act)
         hidden[:, cols] = value.astype(jnp.bfloat16)
         grad_pre[:, cols] = (grad_hidden * slope).astype(jnp.bfloat16)
+
+
+def weight_products(core, grad_pre, normed, hidden, cotangent, mine, theirs, before):
     for part in range(4):
         cols = slice(256 * part, 256 * part + 256)
-        for side, (left, right) in enumerate(
-            ((grad_pre[:, cols], own_normed), (hidden[:, cols], own_cot))
-        ):
+        for side, (left, right) in enumerate(((grad_pre[:, cols], normed), (hidden[:, cols], cotangent))):
             product = lax.dot_general(
                 left, right, (((0,), (0,)), ((), ())), preferred_element_type=jnp.float32
             )
@@ -194,63 +163,178 @@
                     lanes = slice(128 * run, 128 * run + 128)
                     ours = product[64 * x : 64 * x + 32, lanes]
                     other = product[64 * x + 32 : 64 * x + 64, lanes]
-                    keep = jnp.where(core == 0, ours, other)
-                    send = jnp.where(core == 0, other, ours)
+                    keep = jnp.where(core == 0, ours, other).reshape(4, 8, 128)
+                    send = jnp.where(core == 0, other, ours).reshape(4, 8, 128)
                     row = 32 * (2 * side + run) + 8 * part
-                    mine[4 * x : 4 * x + 4, row : row + 8, :] = keep.reshape(4, 8, 128)
-                    theirs[4 * x : 4 * x + 4, row : row + 8, :] = send.reshape(4, 8, 128)
-
-
-def backward_kernel(
-    above, below, state, before, after, gain, w_in, grad_pre, centred_in, inv_in,
-    grad_conv, out,
-    wide,
-):
-    for row in range(H + 6):
-        centre, spot = source_row(above, state, below, row)
-        wide[row, 8 : 8 + W, :] = centre
-        wide[row, 5:8, :] = before[spot + 3 : spot + 6, :]
-        wide[row, 8 + W : 11 + W, :] = after[spot : spot + 3, :]
+                    places = (slice(4 * x, 4 * x + 4), slice(row, row + 8), slice(None))
+                    if before is not None:
+                        keep = keep + before[0][places]
+                        send = send + before[1][places]
+                    mine[places] = keep
+                    theirs[places] = send
+
+
+def norm_gradient(grad_pre, w_in, gain, centred, inv_std):
     grad_normed = lax.dot_general(
-        grad_pre[...], w_in[...], (((1,), (1,)), ((), ())), preferred_element_type=jnp.float32
-    )
-    centred = centred_in[...]
-    inv_std = inv_in[...][:, 0:1]
-    scaled = grad_normed * gain[...]
+        grad_pre, w_in, (((1,), (1,)), ((), ())), preferred_element_type=jnp.float32
+    )
+    scaled = grad_normed * gain
     grad = inv_std * (
         scaled
         - jnp.mean(scaled, axis=-1, keepdims=True)
         - centred * jnp.mean(scaled * centred, axis=-1, keepdims=True)
     )
-    place = lax.broadcasted_iota(jnp.int32, (H, V, C), 1).reshape(WIDE_CELLS, C)
-    inside = (place >= 3) & (place < 3 + W)
-    gain_sum = jnp.sum(jnp.where(inside, grad_normed * centred, 0.0), axis=0, keepdims=True)
-    grad_conv[...] = grad.reshape(H, V, C)
+    return grad, grad_normed * centred
+
+
+def tap_sums(wide, starts, grads, out, gain_sum, before):
     for half in range(2):
         lanes = slice(128 * half, 128 * half + 128)
-        grads = [grad_conv[row, 3 : 3 + W, lanes] for row in range(H)]
+        pieces = grads(lanes)
         for col in range(7):
             total = [jnp.zeros((8, 128), jnp.float32)] * 7
             for row in range(H + 6):
-                part = window(wide, row, 5 + col, W, lanes)
-                for tap in range(7):
-                    if 0 <= row - tap < H:
-                        term = part * grads[row - tap]
-                        total[tap] = total[tap] + ((term[0:8] + term[8:16]) + term[16:24])
+                for start, piece in zip(starts, pieces):
+                    width = piece[0].shape[0]
+                    part = window(wide, row, start + col, width, lanes)
+                    for tap in range(7):
+                        if 0 <= row - tap < H:
+                            term = part * piece[row - tap]
+                            for tile in range(0, width, 8):
+                                total[tap] = total[tap] + term[tile : tile + 8]
             for tap in range(7):
                 spot = 64 * half + 7 * tap + col
-                out[spot : spot + 1, :] = jnp.sum(total[tap], axis=0, keepdims=True)
-        out[64 * half + 49 : 64 * half + 50, :] = gain_sum[:, lanes]
-        out[64 * half + 50 : 64 * half + 64, :] = jnp.zeros((14, 128), jnp.float32)
+                value = jnp.sum(total[tap], axis=0, keepdims=True)
+                out[spot : spot + 1, :] = (
+                    value if before is None else value + before[spot : spot + 1, :]
+                )
+        spot = 64 * half + 49
+        value = gain_sum[:, lanes]
+        out[spot : spot + 1, :] = value if before is None else value + before[spot : spot + 1, :]
+        out[spot + 1 : spot + 15, :] = jnp.zeros((14, 128), jnp.float32)
+
+
+def tap_weight(taps):
+    return lambda row, tap, col, lanes: taps[7 * tap + col : 7 * tap + col + 1, lanes]
+
+
+def middle_kernel(
+    core_ref, above, below, state, cot, taps, gain, w_in, w_out,
+    mine, theirs, hidden, grad_out, tap_out,
+    wide, conv, full, grad_pre,
+):
+    wide[0:3] = above[...]
+    wide[3 : 3 + H] = state[...]
+    wide[3 + H :] = below[...]
+    full[...] = cot[...].astype(jnp.float32).reshape(H, W, C)
+    for half in range(2):
+        lanes = slice(128 * half, 128 * half + 128)
+        total = convolve(wide, tap_weight(taps), 2, M, lanes)
+        for out in range(H):
+            conv[M * out : M * out + M, lanes] = total[out]
+    centred, inv_std = normalise(conv[...])
+    normed = (centred * gain[...]).astype(jnp.bfloat16)
+    cotangent = full[:, 5 : 5 + M, :].reshape(HALF_CELLS, C).astype(jnp.bfloat16)
+    activate(normed, cotangent, w_in, w_out, hidden, grad_pre)
+    weight_products(core_ref[0], grad_pre, normed, hidden, cotangent, mine, theirs, None)
+    grad, gains = norm_gradient(grad_pre[...], w_in[...], gain[...], centred, inv_std)
+    grad_out[...] = grad.reshape(H, M, C)
+    tap_sums(
+        wide,
+        (2,),
+        lambda lanes: [[grad_out[row, :, lanes] for row in range(H)]],
+        tap_out,
+        jnp.sum(gains, axis=0, keepdims=True),
+        None,
+    )
+
+
+def fill(wide, above, below, state, before, after):
+    wide[:, 32:40, :] = jnp.zeros((H + 6, 8, C), jnp.float32)
+    for row in range(H + 6):
+        centre, spot = source_row(above, state, below, row)
+        wide[row, 8 : 8 + W, :] = centre
+        wide[row, 2:8, :] = before[spot : spot + 6, :]
+        wide[row, 8 + W : 14 + W, :] = after[spot : spot + 6, :]
+
+
+def forward_kernel(
+    core_ref, above, below, state, before, after, cot, taps, gain, w_in, w_out, mine_in, theirs_in,
+    mine, theirs, hidden, grad_pre, centred_out, inv_out,
+    wide, conv, cot_all,
+):
+    fill(wide, above, below, state, before, after)
+    cot_all[:, 8:16, :] = jnp.zeros((H, 8, C), jnp.float32)
+    own = cot[...].astype(jnp.float32)
+    for row in range(H):
+        place = 6 * H + 3 * row
+        cot_all[row, 0:3, :] = before[place : place + 3, :]
+        cot_all[row, 3:8, :] = own[W * row : W * row + 5]
+        cot_all[row, 8:11, :] = own[W * row + W - 3 : W * row + W]
+        cot_all[row, 11:14, :] = after[place : place + 3, :]
+    for half in range(2):
+        lanes = slice(128 * half, 128 * half + 128)
+        for side, base in enumerate((2, 26)):
+            total = convolve(wide, tap_weight(taps), base, 8, lanes)
+            for out in range(H):
+                spot = M * out + 8 * side
+                conv[spot : spot + 8, lanes] = total[out]
+    centred, inv_std = normalise(conv[...])
+    centred_out[...] = centred
+    inv_out[...] = jnp.broadcast_to(inv_std, (HALF_CELLS, 128))
+    inside = is_inside()
+    normed = centred * gain[...]
+    own_normed = jnp.where(inside, normed, 0.0).astype(jnp.bfloat16)
+    normed = normed.astype(jnp.bfloat16)
+    cotangent = cot_all[...].reshape(HALF_CELLS, C)
+    own_cot = jnp.where(inside, cotangent, 0.0).astype(jnp.bfloat16)
+    cotangent = cotangent.astype(jnp.bfloat16)
+    activate(normed, cotangent, w_in, w_out, hidden, grad_pre)
+    weight_products(
+        core_ref[0], grad_pre, own_normed, hidden, own_cot, mine, theirs, (mine_in, theirs_in)
+    )
+
+
+def is_inside():
+    place = lax.broadcasted_iota(jnp.int32, (H, M, C), 1).reshape(HALF_CELLS, C)
+    return (place >= 3) & (place < 11)
+
+
+def backward_kernel(
+    above, below, state, before, after, gain, w_in, grad_pre, centred_in, inv_in, grad_mid, tap_mid,
+    grad_conv, out,
+    wide, own_grad,
+):
+    fill(wide, above, below, state, before, after)
+    grad, gains = norm_gradient(grad_pre[...], w_in[...], gain[...], centred_in[...], inv_in[...][:, 0:1])
+    inside = is_inside()
+    own_grad[...] = jnp.where(inside, grad, 0.0).reshape(H, M, C)
+    grad = grad.reshape(H, M, C)
+    grad_conv[:, 0:8, :] = grad[:, 0:8]
+    grad_conv[:, 8:24, :] = grad_mid[...]
+    grad_conv[:, 24:32, :] = grad[:, 8:16]
+    tap_sums(
+        wide,
+        (2, 26),
+        lambda lanes: [
+            [own_grad[row, spot : spot + 8, lanes] for row in range(H)] for spot in (0, 8)
+        ],
+        out,
+        jnp.sum(jnp.where(inside, gains, 0.0), axis=0, keepdims=True),
+        tap_mid,
+    )
 
 
 def adjoint_kernel(
-    where_ref, first, second, grad_conv, cot, taps, state, hidden, w_out,
+    where_ref, first, second, grad_conv, cot, taps, state, middle, outer, w_out,
     out, block_out,
     wide, rim, grad, branch_ref,
 ):
-    branch = jnp.dot(hidden[...], w_out[...], preferred_element_type=jnp.float32)
-    branch_ref[...] = branch.reshape(H, V, C)
+    branch = jnp.dot(middle[...], w_out[...], preferred_element_type=jnp.float32)
+    branch_ref[:, 8:24, :] = branch.reshape(H, M, C)
+    branch = jnp.dot(outer[...], w_out[...], preferred_element_type=jnp.float32).reshape(H, M, C)
+    branch_ref[:, 0:8, :] = branch[:, 0:8]
+    branch_ref[:, 24:32, :] = branch[:, 8:16]
     block_out[...] = (state[...] + branch_ref[:, 3 : 3 + W, :]).reshape(CELLS, C).astype(jnp.bfloat16)
     lat = where_ref[0]
     even = where_ref[1] == 1
@@ -389,30 +473,39 @@
     before = lax.ppermute(to_right, AXES, right)
     after = lax.ppermute(to_left, AXES, left)
     pieces = (above, below, state_field, before, after)
+    part = ((16, 128, 128), F32)
+    mine, theirs, middle, grad_middle, tap_middle = call(
+        middle_kernel,
+        [part, part, ((HALF_CELLS, FF), BF16), ((H, M, C), F32), ((128, 128), F32)],
+        core, above, below, state_field, cot, depthwise, gain, w_in, w_out,
+        scratch=[
+            ((H + 6, W, C), F32),
+            ((HALF_CELLS, C), F32),
+            ((H, W, C), F32),
+            ((HALF_CELLS, FF), BF16),
+        ],
+        scalars=1,
+    )
     mine, theirs, hidden, grad_pre, centred, inv_std = call(
         forward_kernel,
         [
-            ((16, 128, 128), F32),
-            ((16, 128, 128), F32),
-            ((WIDE_CELLS, FF), BF16),
-            ((WIDE_CELLS, FF), BF16),
-            ((WIDE_CELLS, C), F32),
-            ((WIDE_CELLS, 128), F32),
-        ],
-        core, *pieces, cot, depthwise, gain, w_in, w_out,
-        scratch=[
-            WIDE,
-            ((WIDE_CELLS, C), F32),
-            ((H, V, C), F32),
-        ],
+            part,
+            part,
+            ((HALF_CELLS, FF), BF16),
+            ((HALF_CELLS, FF), BF16),
+            ((HALF_CELLS, C), F32),
+            ((HALF_CELLS, 128), F32),
+        ],
+        core, *pieces, cot, depthwise, gain, w_in, w_out, mine, theirs,
+        scratch=[WIDE, ((HALF_CELLS, C), F32), ((H, M, C), F32)],
         scalars=1,
     )
     theirs = lax.ppermute(theirs, "core", [(0, 1), (1, 0)])
     grad_conv, taps = call(
         backward_kernel,
         [((H, V, C), F32), ((128, 128), F32)],
-        *pieces, gain, w_in, grad_pre, centred, inv_std,
-        scratch=[WIDE],
+        *pieces, gain, w_in, grad_pre, centred, inv_std, grad_middle, tap_middle,
+        scratch=[WIDE, ((H, M, C), F32)],
     )
     (joined,) = call(join_kernel, [((16, 136, 128), F32)], mine, theirs, taps)
     plane = lax.all_to_all(joined, ("x", "y"), split_axis=0, concat_axis=0, tiled=True)
@@ -423,7 +516,7 @@
     grad_input, block_out = call(
         adjoint_kernel,
         [((CELLS, C), BF16), ((CELLS, C), BF16)],
-        jnp.stack([lat, parity]), *grad_rows, grad_conv, cot, depthwise, state_field, hidden, w_out,
+        jnp.stack([lat, parity]), *grad_rows, grad_conv, cot, depthwise, state_field, middle, hidden, w_out,
         scratch=[
             ((H + 6, V, C), F32),
             ((2, 7, 8, C), F32),

time: 109 us -> 107 us (0.982)
  waiting for transfers between devices: 21.5 us -> 16.8 us
  Pallas kernels: 14.8 us -> 17.2 us
    pallas_call x9 -> x10, Pallas kernels: 14.8 us -> 17.2 us  [call(): pl.pallas_call(kernel, out_shape=[jax.ShapeDtypeStruct(s, d) for s, d in...]
    ppermute x1, waiting for transfers between devices: 2.11 us -> 0.01 us  [body(): before = lax.ppermute(to_right, AXES, right)]
    all_to_all x1, starting transfers between devices: 11.4 us -> 13.5 us  [body(): lax.all_to_all(spread, ('zh', 'zl'), split_axis=0, concat_axis=0, tiled=T...]
    all_to_all x1, waiting for transfers between devices: 1.98 us -> 0.5 us  [body(): lax.all_to_all(joined, ('x', 'y'), split_axis=0, concat_axis=0, tiled=True)]
    all_to_all x1, starting transfers between devices: 8.8 us -> 7.51 us  [body(): lax.all_to_all(joined, ('x', 'y'), split_axis=0, concat_axis=0, tiled=True)]
  transfers between devices with their start and end apart: 9 -> 9, of which waited for: 5 -> 4; matrix products, arithmetic and copies ran while one was open for 0% -> 0% of each run, Pallas kernels for 6% -> 10%
where the time goes in v4:
time: 107 us
  starting transfers between devices  51.2 us (48%)
  Pallas kernels  17.2 us (16%)
  waiting for transfers between devices  16.8 us (16%)
  blocking collectives  14.8 us (14%)
  local copies, waits for them, and re-layouts  4.64 us (4%)
  other arithmetic  1.11 us (1%)
    pallas_call x10, Pallas kernels, call(): pl.pallas_call(kernel, out_shape=[jax.ShapeDtypeStruct(s, d) for s, d in...  17.2 us
    all_to_all x1, blocking collectives, body(): lax.all_to_all(shared, ('x', 'core', 'y'), split_axis=0, concat_axis=0, t...  14.8 us
    all_to_all x1, starting transfers between devices, body(): lax.all_to_all(spread, ('zh', 'zl'), split_axis=0, concat_axis=0, tiled=T...  13.5 us
    ppermute x2, starting transfers between devices, row_exchange(): got_first = lax.ppermute(jnp.where(even, tail, head), AXES, first)  10 us
    ppermute x2, starting transfers between devices, row_exchange(): got_second = lax.ppermute(outer, AXES, second)  8.6 us
    all_to_all x1, waiting for transfers between devices, body(): lax.all_to_all(spread, ('zh', 'zl'), split_axis=0, concat_axis=0, tiled=T...  8.3 us
    ppermute x2, waiting for transfers between devices, row_exchange(): got_second = lax.ppermute(outer, AXES, second)  7.9 us
    all_to_all x1, starting transfers between devices, body(): lax.all_to_all(joined, ('x', 'y'), split_axis=0, concat_axis=0, tiled=True)  7.51 us
  transfers between devices with their start and end apart: 9, of which 4 were waited for; matrix products, arithmetic and copies ran while one was open for 0% of the time, Pallas kernels for 10%

profile of v4, /device:TPU:1, one launch (start us, length us, event | category | flops | bytes accessed | tf_op | source)
XLA Modules:
  0.0 106.6 jit_solution(1103209067163226069)
XLA Ops:
  0.7 0.0 copy-start.1
  0.7 0.0 copy-start.3
  0.7 1.0 slice_select_fusion.2
  1.7 4.5 %collective-permute-start.1 = (f32[3,24,256]{2,1,0:T(8,128)S(1)}, f32[3,24,256]{2,1,0:T(8,128)S(1)}, u32[]{:S(2)}, u32[]{:S(2)}) collective-permute-start(f32[3,24,256]{2,1,0:T(8,128)S(1)} %reverse_select_fusion.1), channel_id=1, source_target_pairs={{0,8},{1,9},{2,10},{3,11},{4,12},{5,13},{6,14},{7,15},{8,0},{9,1},... | collective-permute-start | bytes 221192 | tf_op jit(solution)/shard_map/ppermute | solution.py:433
  6.2 6.2 %collective-permute-start = (f32[3,24,256]{2,1,0:T(8,128)S(1)}, f32[3,24,256]{2,1,0:T(8,128)S(1)}, u32[]{:S(2)}, u32[]{:S(2)}) collective-permute-start(f32[3,24,256]{2,1,0:T(8,128)S(1)} %get-tuple-element.74), channel_id=1, source_target_pairs={{0,16},{1,17},{2,18},{3,19},{4,20},{5,21},{6,22},{7,23},{8,24},{9,... | collective-permute-start | bytes 221192 | tf_op jit(solution)/shard_map/ppermute | solution.py:432
  12.4 0.0 copy-start
  12.4 1.0 copy-done
  13.4 0.0 copy-start.2
  13.4 0.9 copy-done.2
  14.3 0.0 copy-start.4
  14.3 1.0 copy-done.4
  15.3 0.0 copy-start.5
  15.3 1.0 copy-done.5
  16.4 0.0 copy-start.7
  16.4 0.7 copy-done.7
  17.1 0.0 copy-start.6
  17.1 0.4 shard_map.101
  17.5 0.0 collective-permute-done.1.second
  17.5 0.0 collective-permute-done.first
  17.6 1.9 %collective-permute-start.2 = (f32[144,256]{1,0:T(8,128)S(1)}, f32[144,256]{1,0:T(8,128)S(1)}, u32[]{:S(2)}, u32[]{:S(2)}) collective-permute-start(f32[144,256]{1,0:T(8,128)S(1)} %get-tuple-element.42), channel_id=1, source_target_pairs={{0,1},{1,2},{2,3},{3,4},{4,5},{5,6},{6,7},{7,8},{8,9},{9,10},{10,1... | collective-permute-start | bytes 442376 | tf_op jit(solution)/shard_map/ppermute | solution.py:473
  19.5 7.3 %collective-permute-start.3 = (f32[144,256]{1,0:T(8,128)S(1)}, f32[144,256]{1,0:T(8,128)S(1)}, u32[]{:S(2)}, u32[]{:S(2)}) collective-permute-start(f32[144,256]{1,0:T(8,128)S(1)} %get-tuple-element.43), channel_id=1, source_target_pairs={{0,15},{1,0},{2,1},{3,2},{4,3},{5,4},{6,5},{7,6},{8,7},{9,8},{10,9... | collective-permute-start | bytes 442376 | tf_op jit(solution)/shard_map/ppermute | solution.py:474
  26.8 0.0 copy-done.1
  26.8 0.0 copy-done.3
  26.8 0.0 copy-done.6
  26.8 4.7 %shard_map.103 = (f32[16,128,128]{2,1,0:T(8,128)S(1)}, f32[16,128,128]{2,1,0:T(8,128)S(1)}, bf16[192,1024]{1,0:T(8,128)(2,1)S(1)}, f32[12,16,256]{2,1,0:T(8,128)S(1)}, f32[128,128]{1,0:T(8,128)S(1)}) custom-call(s32[1]{0:T(128)} %bitcast.2.core_ref, f32[3,24,256]{2,1,0:T(8,128)S(1)} %get-tuple-element.40.above, f32[3,24,256]{2,1,0:T(8,128)S(1)} %get-tuple-element.41.below, ...), custom_call_target="tpu_custom_call" | custom-call | tf_op jit(solution)/shard_map/pallas_call | solution.py:410
  31.5 0.0 collective-permute-done.2.before
  31.5 0.0 collective-permute-done.3.after
  31.5 3.2 %shard_map.104 = (f32[16,128,128]{2,1,0:T(8,128)S(1)}, f32[16,128,128]{2,1,0:T(8,128)S(1)}, bf16[192,1024]{1,0:T(8,128)(2,1)S(1)}, bf16[192,1024]{1,0:T(8,128)(2...) custom-call(s32[1]{0:T(128)} %bitcast.2.core_ref, f32[3,24,256]{2,1,0:T(8,128)S(1)} %get-tuple-element.40.above, ...), custom_call_target="tpu_custom_call" | custom-call | tf_op jit(solution)/shard_map/pallas_call | solution.py:410
  34.7 2.5 %collective-permute-start.4 = (f32[16,128,128]{2,1,0:T(8,128)S(1)}, f32[16,128,128]{2,1,0:T(8,128)S(1)}, u32[]{:S(2)}, u32[]{:S(2)}) collective-permute-start(f32[16,128,128]{2,1,0:T(8,128)S(1)} %get-tuple-element.50), channel_id=1, source_target_pairs={{0,16},{16,0},{1,17},{17,1},{2,18},{18,2},{3,19},{19,3},{4,20},{20... | collective-permute-start | bytes 3145736 | tf_op jit(solution)/shard_map/ppermute | solution.py:503
  37.2 2.2 %shard_map.105 = (f32[12,32,256]{2,1,0:T(8,128)S(1)}, f32[128,128]{1,0:T(8,128)S(1)}) custom-call(f32[3,24,256]{2,1,0:T(8,128)S(1)} %get-tuple-element.40.above, f32[3,24,256]{2,1,0:T(8,128)S(1)} %get-tuple-element.41.below, f32[12,24,256]{2,1,0:T(8,128)S(1)} %copy-done.1, f32[144,256]{1,0:T(8,128)S(1)} %collective-permute-done.2.before, ...), custom_call_target="tpu_custom_call" | custom-call | tf_op jit(solution)/shard_map/pallas_call | solution.py:410
  39.4 0.1 collective-permute-done.4.theirs
  39.4 1.1 %shard_map.106 = f32[16,136,128]{2,1,0:T(8,128)} custom-call(f32[16,128,128]{2,1,0:T(8,128)S(1)} %get-tuple-element.49.mine, f32[16,128,128]{2,1,0:T(8,128)S(1)} %collective-permute-done.4.theirs, f32[128,128]{1,0:T(8,128)S(1)} %get-tuple-element.56.taps), custom_call_target="tpu_custom_call" | custom-call | tf_op jit(solution)/shard_map/pallas_call | solution.py:410
  40.6 7.5 %all-to-all-start = ((f32[16,136,128]{2,1,0:T(8,128)}), f32[16,136,128]{2,1,0:T(8,128)S(1)}, u32[]{:S(2)}, u32[]{:S(2)}) async-start(f32[16,136,128]{2,1,0:T(8,128)} %shard_map.106), calls=%async_computation | async-start | bytes 2228224 | tf_op jit(solution)/shard_map/all_to_all | solution.py:511
  48.1 4.1 %collective-permute-start.6 = (f32[3,32,256]{2,1,0:T(8,128)S(1)}, f32[3,32,256]{2,1,0:T(8,128)S(1)}, u32[]{:S(2)}, u32[]{:S(2)}) collective-permute-start(f32[3,32,256]{2,1,0:T(8,128)S(1)} %reverse_select_fusion), channel_id=1, source_target_pairs={{0,8},{1,9},{2,10},{3,11},{4,12},{5,13},{6,14},{7,15},{8,0},{9,1},... | collective-permute-start | bytes 294920 | tf_op jit(solution)/shard_map/ppermute | solution.py:433
  52.2 3.8 %collective-permute-start.5 = (f32[3,32,256]{2,1,0:T(8,128)S(1)}, f32[3,32,256]{2,1,0:T(8,128)S(1)}, u32[]{:S(2)}, u32[]{:S(2)}) collective-permute-start(f32[3,32,256]{2,1,0:T(8,128)S(1)} %get-tuple-element.72), channel_id=1, source_target_pairs={{0,16},{1,17},{2,18},{3,19},{4,20},{5,21},{6,22},{7,23},{8,24},{9,... | collective-permute-start | bytes 294920 | tf_op jit(solution)/shard_map/ppermute | solution.py:432
  56.0 7.9 %collective-permute-done.6.second = f32[3,32,256]{2,1,0:T(8,128)S(1)} collective-permute-done((f32[3,32,256]{2,1,0:T(8,128)S(1)}, f32[3,32,256]{2,1,0:T(8,128)S(1)}, u32[]{:S(2)}, u32[]{:S(2)}) %collective-permute-start.6) | collective-permute-done | bytes 98336 | tf_op jit(solution)/shard_map/ppermute | solution.py:433
  63.9 0.0 collective-permute-done.5.first
  63.9 0.5 all-to-all-done.got
  64.4 0.7 shard_map.108
  65.2 13.5 %all-to-all-start.1 = ((f32[16,16,128]{2,1,0:T(8,128)}), f32[16,16,128]{2,1,0:T(8,128)S(1)}, u32[]{:S(2)}, u32[]{:S(2)}) async-start(f32[16,16,128]{2,1,0:T(8,128)} %shard_map.108), calls=%async_computation.1 | async-start | bytes 262144 | tf_op jit(solution)/shard_map/all_to_all | solution.py:515
  78.6 0.1 pad_add_fusion.where_ref
  78.7 3.6 %shard_map.107 = (bf16[288,256]{1,0:T(8,128)(2,1)}, bf16[288,256]{1,0:T(8,128)(2,1)}) custom-call(s32[2]{0:T(128)S(1)} %pad_add_fusion.where_ref, f32[3,32,256]{2,1,0:T(8,128)S(1)} %collective-permute-done.5.first, f32[3,32,256]{2,1,0:T(8,128)S(1)} %collective-permute-done.6.second, f32[12,32,256]{2,1,0:T(8,128)S(1)} %get-tuple-element.57.grad_conv, ...), custom_call_target="tpu_custom_call" | custom-call | tf_op jit(solution)/shard_map/pallas_call | solution.py:410
  82.3 8.3 %all-to-all-done.1.got = f32[16,16,128]{2,1,0:T(8,128)S(1)} async-done(((f32[16,16,128]{2,1,0:T(8,128)}), f32[16,16,128]{2,1,0:T(8,128)S(1)}, u32[]{:S(2)}, u32[]{:S(2)}) %all-to-all-start.1) | async-done | bytes 131104 | tf_op jit(solution)/shard_map/all_to_all | solution.py:515
  90.6 0.6 shard_map.109
  91.2 14.8 %all_to_all.15.got = f32[32,8,128]{2,1,0:T(8,128)S(1)} all-to-all(f32[32,8,128]{2,1,0:T(8,128)S(1)} %get-tuple-element.68), channel_id=1, replica_groups=mesh['zh'=4,'x'=4,'core'=2,'y'=4,'zl'=4] {'x','core','y'}, dimensions={0} | all-to-all | bytes 262144 | tf_op jit(solution)/shard_map/all_to_all | solution.py:532
  106.0 0.6 shard_map.110
  (4 shorter events, 0.1 us)
Async XLA Ops:
  0.7 26.1 %copy-start.1 = (f32[12,24,256]{2,1,0:T(8,128)S(1)}, f32[12,24,256]{2,1,0:T(8,128)}, u32[]{:S(2)}) copy-start(f32[12,24,256]{2,1,0:T(8,128)} %state.7) | copy-start | bytes 884740
  0.7 26.1 %copy-start.3 = (bf16[12,24,256]{2,1,0:T(8,128)(2,1)S(1)}, bf16[12,24,256]{2,1,0:T(8,128)(2,1)}, u32[]{:S(2)}) copy-start(bf16[12,24,256]{2,1,0:T(8,128)(2,1)} %param.7) | copy-start | bytes 442372
  1.7 15.8 %collective-permute-start.1 = (f32[3,24,256]{2,1,0:T(8,128)S(1)}, f32[3,24,256]{2,1,0:T(8,128)S(1)}, u32[]{:S(2)}, u32[]{:S(2)}) collective-permute-start(f32[3,24,256]{2,1,0:T(8,128)S(1)} %reverse_select_fusion.1), channel_id=1, source_target_pairs={{0,8},{1,9},{2,10},{3,11},{4,12},{5,13},{6,14},{7,15},{8,0},{9,1},... | collective-permute-start | bytes 221192 | tf_op jit(solution)/shard_map/ppermute | solution.py:433
  6.2 11.3 %collective-permute-start = (f32[3,24,256]{2,1,0:T(8,128)S(1)}, f32[3,24,256]{2,1,0:T(8,128)S(1)}, u32[]{:S(2)}, u32[]{:S(2)}) collective-permute-start(f32[3,24,256]{2,1,0:T(8,128)S(1)} %get-tuple-element.74), channel_id=1, source_target_pairs={{0,16},{1,17},{2,18},{3,19},{4,20},{5,21},{6,22},{7,23},{8,24},{9,... | collective-permute-start | bytes 221192 | tf_op jit(solution)/shard_map/ppermute | solution.py:432
  12.4 1.0 copy-start
  13.4 0.9 copy-start.2
  14.3 1.0 copy-start.4
  15.3 1.0 copy-start.5
  16.4 0.7 copy-start.7
  17.1 9.7 %copy-start.6 = (f32[49,256]{1,0:T(8,128)S(1)}, f32[49,256]{1,0:T(8,128)}, u32[]{:S(2)}) copy-start(f32[49,256]{1,0:T(8,128)} %taps.5) | copy-start | bytes 150532
  17.6 13.9 %collective-permute-start.2 = (f32[144,256]{1,0:T(8,128)S(1)}, f32[144,256]{1,0:T(8,128)S(1)}, u32[]{:S(2)}, u32[]{:S(2)}) collective-permute-start(f32[144,256]{1,0:T(8,128)S(1)} %get-tuple-element.42), channel_id=1, source_target_pairs={{0,1},{1,2},{2,3},{3,4},{4,5},{5,6},{6,7},{7,8},{8,9},{9,10},{10,1... | collective-permute-start | bytes 442376 | tf_op jit(solution)/shard_map/ppermute | solution.py:473
  19.5 12.0 %collective-permute-start.3 = (f32[144,256]{1,0:T(8,128)S(1)}, f32[144,256]{1,0:T(8,128)S(1)}, u32[]{:S(2)}, u32[]{:S(2)}) collective-permute-start(f32[144,256]{1,0:T(8,128)S(1)} %get-tuple-element.43), channel_id=1, source_target_pairs={{0,15},{1,0},{2,1},{3,2},{4,3},{5,4},{6,5},{7,6},{8,7},{9,8},{10,9... | collective-permute-start | bytes 442376 | tf_op jit(solution)/shard_map/ppermute | solution.py:474
  34.7 4.8 %collective-permute-start.4 = (f32[16,128,128]{2,1,0:T(8,128)S(1)}, f32[16,128,128]{2,1,0:T(8,128)S(1)}, u32[]{:S(2)}, u32[]{:S(2)}) collective-permute-start(f32[16,128,128]{2,1,0:T(8,128)S(1)} %get-tuple-element.50), channel_id=1, source_target_pairs={{0,16},{16,0},{1,17},{17,1},{2,18},{18,2},{3,19},{19,3},{4,20},{20... | collective-permute-start | bytes 3145736 | tf_op jit(solution)/shard_map/ppermute | solution.py:503
  40.6 23.9 %all-to-all-start = ((f32[16,136,128]{2,1,0:T(8,128)}), f32[16,136,128]{2,1,0:T(8,128)S(1)}, u32[]{:S(2)}, u32[]{:S(2)}) async-start(f32[16,136,128]{2,1,0:T(8,128)} %shard_map.106), calls=%async_computation | async-start | bytes 2228224 | tf_op jit(solution)/shard_map/all_to_all | solution.py:511
  48.1 15.8 %collective-permute-start.6 = (f32[3,32,256]{2,1,0:T(8,128)S(1)}, f32[3,32,256]{2,1,0:T(8,128)S(1)}, u32[]{:S(2)}, u32[]{:S(2)}) collective-permute-start(f32[3,32,256]{2,1,0:T(8,128)S(1)} %reverse_select_fusion), channel_id=1, source_target_pairs={{0,8},{1,9},{2,10},{3,11},{4,12},{5,13},{6,14},{7,15},{8,0},{9,1},... | collective-permute-start | bytes 294920 | tf_op jit(solution)/shard_map/ppermute | solution.py:433
  52.2 11.7 %collective-permute-start.5 = (f32[3,32,256]{2,1,0:T(8,128)S(1)}, f32[3,32,256]{2,1,0:T(8,128)S(1)}, u32[]{:S(2)}, u32[]{:S(2)}) collective-permute-start(f32[3,32,256]{2,1,0:T(8,128)S(1)} %get-tuple-element.72), channel_id=1, source_target_pairs={{0,16},{1,17},{2,18},{3,19},{4,20},{5,21},{6,22},{7,23},{8,24},{9,... | collective-permute-start | bytes 294920 | tf_op jit(solution)/shard_map/ppermute | solution.py:432
  65.2 25.4 %all-to-all-start.1 = ((f32[16,16,128]{2,1,0:T(8,128)}), f32[16,16,128]{2,1,0:T(8,128)S(1)}, u32[]{:S(2)}, u32[]{:S(2)}) async-start(f32[16,16,128]{2,1,0:T(8,128)} %shard_map.108), calls=%async_computation.1 | async-start | bytes 262144 | tf_op jit(solution)/shard_map/all_to_all | solution.py:515

commit v5 on v4

--- a/solution.py
+++ b/solution.py
@@ -51,6 +51,7 @@
 CELLS = H * W
 M = 16
 HALF_CELLS = H * M
+OWN = H * 8
 EDGE = 6 * (H + 6) + 3 * H
 PARAMS = pltpu.CompilerParams(vmem_limit_bytes=20 * 1024 * 1024)
 
@@ -264,40 +265,42 @@
     wide, conv, cot_all,
 ):
     fill(wide, above, below, state, before, after)
-    cot_all[:, 8:16, :] = jnp.zeros((H, 8, C), jnp.float32)
+    cot_all[H:, :, :] = jnp.zeros((H, 8, C), jnp.float32)
     own = cot[...].astype(jnp.float32)
     for row in range(H):
         place = 6 * H + 3 * row
-        cot_all[row, 0:3, :] = before[place : place + 3, :]
-        cot_all[row, 3:8, :] = own[W * row : W * row + 5]
-        cot_all[row, 8:11, :] = own[W * row + W - 3 : W * row + W]
-        cot_all[row, 11:14, :] = after[place : place + 3, :]
+        cot_all[row, 0:5, :] = own[W * row : W * row + 5]
+        cot_all[row, 5:8, :] = own[W * row + W - 3 : W * row + W]
+        cot_all[H + row, 0:3, :] = before[place : place + 3, :]
+        cot_all[H + row, 3:6, :] = after[place : place + 3, :]
     for half in range(2):
         lanes = slice(128 * half, 128 * half + 128)
-        for side, base in enumerate((2, 26)):
-            total = convolve(wide, tap_weight(taps), base, 8, lanes)
-            for out in range(H):
-                spot = M * out + 8 * side
-                conv[spot : spot + 8, lanes] = total[out]
+        west = convolve(wide, tap_weight(taps), 2, 8, lanes)
+        east = convolve(wide, tap_weight(taps), 26, 8, lanes)
+        for out in range(H):
+            spot = 8 * out
+            conv[spot : spot + 5, lanes] = west[out][3:8]
+            conv[spot + 5 : spot + 8, lanes] = east[out][0:3]
+            spot = OWN + 8 * out
+            conv[spot : spot + 3, lanes] = west[out][0:3]
+            conv[spot + 3 : spot + 8, lanes] = east[out][3:8]
     centred, inv_std = normalise(conv[...])
     centred_out[...] = centred
     inv_out[...] = jnp.broadcast_to(inv_std, (HALF_CELLS, 128))
-    inside = is_inside()
-    normed = centred * gain[...]
-    own_normed = jnp.where(inside, normed, 0.0).astype(jnp.bfloat16)
-    normed = normed.astype(jnp.bfloat16)
-    cotangent = cot_all[...].reshape(HALF_CELLS, C)
-    own_cot = jnp.where(inside, cotangent, 0.0).astype(jnp.bfloat16)
-    cotangent = cotangent.astype(jnp.bfloat16)
+    normed = (centred * gain[...]).astype(jnp.bfloat16)
+    cotangent = cot_all[...].reshape(HALF_CELLS, C).astype(jnp.bfloat16)
     activate(normed, cotangent, w_in, w_out, hidden, grad_pre)
+    own_rows = slice(0, OWN)
     weight_products(
-        core_ref[0], grad_pre, own_normed, hidden, own_cot, mine, theirs, (mine_in, theirs_in)
-    )
-
-
-def is_inside():
-    place = lax.broadcasted_iota(jnp.int32, (H, M, C), 1).reshape(HALF_CELLS, C)
-    return (place >= 3) & (place < 11)
+        core_ref[0],
+        grad_pre[own_rows, :],
+        normed[own_rows],
+        hidden[own_rows, :],
+        cotangent[own_rows],
+        mine,
+        theirs,
+        (mine_in, theirs_in),
+    )
 
 
 def backward_kernel(
@@ -307,12 +310,16 @@
 ):
     fill(wide, above, below, state, before, after)
     grad, gains = norm_gradient(grad_pre[...], w_in[...], gain[...], centred_in[...], inv_in[...][:, 0:1])
-    inside = is_inside()
-    own_grad[...] = jnp.where(inside, grad, 0.0).reshape(H, M, C)
-    grad = grad.reshape(H, M, C)
-    grad_conv[:, 0:8, :] = grad[:, 0:8]
+    own = grad[0:OWN].reshape(H, 8, C)
+    rest = grad[OWN:].reshape(H, 8, C)
+    own_grad[...] = jnp.zeros((H, M, C), jnp.float32)
+    own_grad[:, 3:8, :] = own[:, 0:5]
+    own_grad[:, 8:11, :] = own[:, 5:8]
+    grad_conv[:, 0:3, :] = rest[:, 0:3]
+    grad_conv[:, 3:8, :] = own[:, 0:5]
+    grad_conv[:, 24:27, :] = own[:, 5:8]
+    grad_conv[:, 27:32, :] = rest[:, 3:8]
     grad_conv[:, 8:24, :] = grad_mid[...]
-    grad_conv[:, 24:32, :] = grad[:, 8:16]
     tap_sums(
         wide,
         (2, 26),
@@ -320,7 +327,7 @@
             [own_grad[row, spot : spot + 8, lanes] for row in range(H)] for spot in (0, 8)
         ],
         out,
-        jnp.sum(jnp.where(inside, gains, 0.0), axis=0, keepdims=True),
+        jnp.sum(gains[0:OWN], axis=0, keepdims=True),
         tap_mid,
     )
 
@@ -332,9 +339,10 @@
 ):
     branch = jnp.dot(middle[...], w_out[...], preferred_element_type=jnp.float32)
     branch_ref[:, 8:24, :] = branch.reshape(H, M, C)
-    branch = jnp.dot(outer[...], w_out[...], preferred_element_type=jnp.float32).reshape(H, M, C)
-    branch_ref[:, 0:8, :] = branch[:, 0:8]
-    branch_ref[:, 24:32, :] = branch[:, 8:16]
+    branch = jnp.dot(outer[0:OWN, :], w_out[...], preferred_element_type=jnp.float32)
+    branch = branch.reshape(H, 8, C)
+    branch_ref[:, 3:8, :] = branch[:, 0:5]
+    branch_ref[:, 24:27, :] = branch[:, 5:8]
     block_out[...] = (state[...] + branch_ref[:, 3 : 3 + W, :]).reshape(CELLS, C).astype(jnp.bfloat16)
     lat = where_ref[0]
     even = where_ref[1] == 1
@@ -381,15 +389,22 @@
             out[place, 8:16, :] = total[128:136]
 
 
-def column_kernel(scale, got, weight_grads, shared):
-    total = got[0]
+def share_kernel(scale, got, shared):
+    total = got[0, 8:16, :]
     for peer in range(1, 16):
-        total = total + got[peer]
+        total = total + got[peer, 8:16, :]
+    total = total * scale
+    for peer in range(32):
+        shared[peer] = total
+
+
+def column_kernel(scale, got, weight_grads):
+    total = got[0, 0:8, :]
+    for peer in range(1, 16):
+        total = total + got[peer, 0:8, :]
     total = total * scale
     for run in range(4):
         weight_grads[:, 128 * run : 128 * run + 128] = total[2 * run : 2 * run + 2]
-    for peer in range(32):
-        shared[peer] = total[8:16]
 
 
 def total_kernel(got, taps, gain):
@@ -497,7 +512,7 @@
             ((HALF_CELLS, 128), F32),
         ],
         core, *pieces, cot, depthwise, gain, w_in, w_out, mine, theirs,
-        scratch=[WIDE, ((HALF_CELLS, C), F32), ((H, M, C), F32)],
+        scratch=[WIDE, ((HALF_CELLS, C), F32), ((2 * H, 8, C), F32)],
         scalars=1,
     )
     theirs = lax.ppermute(theirs, "core", [(0, 1), (1, 0)])
@@ -526,9 +541,8 @@
         scalars=1,
     )
     column, grad_input = lax.optimization_barrier((column, grad_input))
-    weight_grads, shared = call(
-        functools.partial(column_kernel, grad_scale), [((2, 512), F32), ((32, 8, 128), F32)], column
-    )
+    (shared,) = call(functools.partial(share_kernel, grad_scale), [((32, 8, 128), F32)], column)
+    (weight_grads,) = call(functools.partial(column_kernel, grad_scale), [((2, 512), F32)], column)
     shared = lax.all_to_all(shared, ("x", "core", "y"), split_axis=0, concat_axis=0, tiled=True)
     tap_total, gain_total = call(total_kernel, [((49, C), F32), ((1, C), F32)], shared)
     return (

time: 107 us -> 108 us (level)
  blocking collectives: 14.8 us -> 0 us
  starting transfers between devices: 51.2 us -> 58.7 us
  waiting for transfers between devices: 16.8 us -> 24 us
    all_to_all x1 -> x0, blocking collectives: 14.8 us -> none  [body(): lax.all_to_all(shared, ('x', 'core', 'y'), split_axis=0, concat_axis=0, t...]
    all_to_all x0 -> x1, starting transfers between devices: none -> 7.41 us  [body(): lax.all_to_all(shared, ('x', 'core', 'y'), split_axis=0, concat_axis=0, t...]
    all_to_all x0 -> x1, waiting for transfers between devices: none -> 7.01 us  [body(): lax.all_to_all(shared, ('x', 'core', 'y'), split_axis=0, concat_axis=0, t...]
    pallas_call x10 -> x11, Pallas kernels: 17.2 us -> 17.8 us  [call(): pl.pallas_call(kernel, out_shape=[jax.ShapeDtypeStruct(s, d) for s, d in...]
  transfers between devices with their start and end apart: 9 -> 10, of which waited for: 4 -> 5; matrix products, arithmetic and copies ran while one was open for 0% -> 0% of each run, Pallas kernels for 10% -> 11%
where the time goes in v5:
time: 108 us; the launch traced here: 107 us
  starting transfers between devices  58.7 us (54%)
  waiting for transfers between devices  24 us (22%)
  Pallas kernels  17.8 us (16%)
  local copies, waits for them, and re-layouts  4.64 us (4%)
  other arithmetic  1.11 us (1%)
    pallas_call x11, Pallas kernels, call(): pl.pallas_call(kernel, out_shape=[jax.ShapeDtypeStruct(s, d) for s, d in...  17.8 us
    all_to_all x1, starting transfers between devices, body(): lax.all_to_all(spread, ('zh', 'zl'), split_axis=0, concat_axis=0, tiled=T...  13.5 us
    ppermute x2, starting transfers between devices, row_exchange(): got_first = lax.ppermute(jnp.where(even, tail, head), AXES, first)  10 us
    ppermute x2, starting transfers between devices, row_exchange(): got_second = lax.ppermute(outer, AXES, second)  8.6 us
    all_to_all x1, waiting for transfers between devices, body(): lax.all_to_all(spread, ('zh', 'zl'), split_axis=0, concat_axis=0, tiled=T...  8.29 us
    ppermute x2, waiting for transfers between devices, row_exchange(): got_second = lax.ppermute(outer, AXES, second)  7.9 us
    all_to_all x1, starting transfers between devices, body(): lax.all_to_all(joined, ('x', 'y'), split_axis=0, concat_axis=0, tiled=True)  7.51 us
    all_to_all x1, starting transfers between devices, body(): lax.all_to_all(shared, ('x', 'core', 'y'), split_axis=0, concat_axis=0, t...  7.41 us
  transfers between devices with their start and end apart: 10, of which 5 were waited for; matrix products, arithmetic and copies ran while one was open for 0% of the time, Pallas kernels for 11%

profile of v5, /device:TPU:1, one launch (start us, length us, event | category | flops | bytes accessed | tf_op | source)
XLA Modules:
  0.0 107.0 jit_solution(10371313322031498705)
XLA Ops:
  0.7 0.0 copy-start.1
  0.7 0.0 copy-start.3
  0.7 1.0 slice_select_fusion.2
  1.7 4.5 %collective-permute-start.1 = (f32[3,24,256]{2,1,0:T(8,128)S(1)}, f32[3,24,256]{2,1,0:T(8,128)S(1)}, u32[]{:S(2)}, u32[]{:S(2)}) collective-permute-start(f32[3,24,256]{2,1,0:T(8,128)S(1)} %reverse_select_fusion.1), channel_id=1, source_target_pairs={{0,8},{1,9},{2,10},{3,11},{4,12},{5,13},{6,14},{7,15},{8,0},{9,1},... | collective-permute-start | bytes 221192 | tf_op jit(solution)/shard_map/ppermute | solution.py:448
  6.2 6.2 %collective-permute-start = (f32[3,24,256]{2,1,0:T(8,128)S(1)}, f32[3,24,256]{2,1,0:T(8,128)S(1)}, u32[]{:S(2)}, u32[]{:S(2)}) collective-permute-start(f32[3,24,256]{2,1,0:T(8,128)S(1)} %get-tuple-element.70), channel_id=1, source_target_pairs={{0,16},{1,17},{2,18},{3,19},{4,20},{5,21},{6,22},{7,23},{8,24},{9,... | collective-permute-start | bytes 221192 | tf_op jit(solution)/shard_map/ppermute | solution.py:447
  12.4 0.0 copy-start
  12.4 1.0 copy-done
  13.4 0.0 copy-start.2
  13.4 0.9 copy-done.2
  14.3 0.0 copy-start.4
  14.3 1.0 copy-done.4
  15.3 0.0 copy-start.5
  15.3 1.0 copy-done.5
  16.4 0.0 copy-start.7
  16.4 0.7 copy-done.7
  17.1 0.0 copy-start.6
  17.1 0.4 shard_map.101
  17.5 0.0 collective-permute-done.1.second
  17.5 0.0 collective-permute-done.first
  17.6 1.9 %collective-permute-start.2 = (f32[144,256]{1,0:T(8,128)S(1)}, f32[144,256]{1,0:T(8,128)S(1)}, u32[]{:S(2)}, u32[]{:S(2)}) collective-permute-start(f32[144,256]{1,0:T(8,128)S(1)} %get-tuple-element.40), channel_id=1, source_target_pairs={{0,1},{1,2},{2,3},{3,4},{4,5},{5,6},{6,7},{7,8},{8,9},{9,10},{10,1... | collective-permute-start | bytes 442376 | tf_op jit(solution)/shard_map/ppermute | solution.py:488
  19.5 7.3 %collective-permute-start.3 = (f32[144,256]{1,0:T(8,128)S(1)}, f32[144,256]{1,0:T(8,128)S(1)}, u32[]{:S(2)}, u32[]{:S(2)}) collective-permute-start(f32[144,256]{1,0:T(8,128)S(1)} %get-tuple-element.41), channel_id=1, source_target_pairs={{0,15},{1,0},{2,1},{3,2},{4,3},{5,4},{6,5},{7,6},{8,7},{9,8},{10,9... | collective-permute-start | bytes 442376 | tf_op jit(solution)/shard_map/ppermute | solution.py:489
  26.8 0.0 copy-done.1
  26.8 0.0 copy-done.3
  26.8 0.0 copy-done.6
  26.8 4.7 %shard_map.103 = (f32[16,128,128]{2,1,0:T(8,128)S(1)}, f32[16,128,128]{2,1,0:T(8,128)S(1)}, bf16[192,1024]{1,0:T(8,128)(2,1)S(1)}, f32[12,16,256]{2,1,0:T(8,128)S(1)}, f32[128,128]{1,0:T(8,128)S(1)}) custom-call(s32[1]{0:T(128)} %bitcast.2.core_ref, f32[3,24,256]{2,1,0:T(8,128)S(1)} %get-tuple-element.38.above, f32[3,24,256]{2,1,0:T(8,128)S(1)} %get-tuple-element.39.below, ...), custom_call_target="tpu_custom_call" | custom-call | tf_op jit(solution)/shard_map/pallas_call | solution.py:425
  31.5 0.0 collective-permute-done.2.before
  31.5 0.0 collective-permute-done.3.after
  31.5 3.3 %shard_map.104 = (f32[16,128,128]{2,1,0:T(8,128)S(1)}, f32[16,128,128]{2,1,0:T(8,128)S(1)}, bf16[192,1024]{1,0:T(8,128)(2,1)S(1)}, bf16[192,1024]{1,0:T(8,128)(2...) custom-call(s32[1]{0:T(128)} %bitcast.2.core_ref, f32[3,24,256]{2,1,0:T(8,128)S(1)} %get-tuple-element.38.above, ...), custom_call_target="tpu_custom_call" | custom-call | tf_op jit(solution)/shard_map/pallas_call | solution.py:425
  34.8 2.5 %collective-permute-start.4 = (f32[16,128,128]{2,1,0:T(8,128)S(1)}, f32[16,128,128]{2,1,0:T(8,128)S(1)}, u32[]{:S(2)}, u32[]{:S(2)}) collective-permute-start(f32[16,128,128]{2,1,0:T(8,128)S(1)} %get-tuple-element.48), channel_id=1, source_target_pairs={{0,16},{16,0},{1,17},{17,1},{2,18},{18,2},{3,19},{19,3},{4,20},{20... | collective-permute-start | bytes 3145736 | tf_op jit(solution)/shard_map/ppermute | solution.py:518
  37.3 2.0 %shard_map.105 = (f32[12,32,256]{2,1,0:T(8,128)S(1)}, f32[128,128]{1,0:T(8,128)S(1)}) custom-call(f32[3,24,256]{2,1,0:T(8,128)S(1)} %get-tuple-element.38.above, f32[3,24,256]{2,1,0:T(8,128)S(1)} %get-tuple-element.39.below, f32[12,24,256]{2,1,0:T(8,128)S(1)} %copy-done.1, f32[144,256]{1,0:T(8,128)S(1)} %collective-permute-done.2.before, ...), custom_call_target="tpu_custom_call" | custom-call | tf_op jit(solution)/shard_map/pallas_call | solution.py:425
  39.3 0.3 collective-permute-done.4.theirs
  39.5 1.1 %shard_map.106 = f32[16,136,128]{2,1,0:T(8,128)} custom-call(f32[16,128,128]{2,1,0:T(8,128)S(1)} %get-tuple-element.47.mine, f32[16,128,128]{2,1,0:T(8,128)S(1)} %collective-permute-done.4.theirs, f32[128,128]{1,0:T(8,128)S(1)} %get-tuple-element.54.taps), custom_call_target="tpu_custom_call" | custom-call | tf_op jit(solution)/shard_map/pallas_call | solution.py:425
  40.7 7.5 %all-to-all-start = ((f32[16,136,128]{2,1,0:T(8,128)}), f32[16,136,128]{2,1,0:T(8,128)S(1)}, u32[]{:S(2)}, u32[]{:S(2)}) async-start(f32[16,136,128]{2,1,0:T(8,128)} %shard_map.106), calls=%async_computation | async-start | bytes 2228224 | tf_op jit(solution)/shard_map/all_to_all | solution.py:526
  48.2 4.1 %collective-permute-start.6 = (f32[3,32,256]{2,1,0:T(8,128)S(1)}, f32[3,32,256]{2,1,0:T(8,128)S(1)}, u32[]{:S(2)}, u32[]{:S(2)}) collective-permute-start(f32[3,32,256]{2,1,0:T(8,128)S(1)} %reverse_select_fusion), channel_id=1, source_target_pairs={{0,8},{1,9},{2,10},{3,11},{4,12},{5,13},{6,14},{7,15},{8,0},{9,1},... | collective-permute-start | bytes 294920 | tf_op jit(solution)/shard_map/ppermute | solution.py:448
  52.3 3.8 %collective-permute-start.5 = (f32[3,32,256]{2,1,0:T(8,128)S(1)}, f32[3,32,256]{2,1,0:T(8,128)S(1)}, u32[]{:S(2)}, u32[]{:S(2)}) collective-permute-start(f32[3,32,256]{2,1,0:T(8,128)S(1)} %get-tuple-element.68), channel_id=1, source_target_pairs={{0,16},{1,17},{2,18},{3,19},{4,20},{5,21},{6,22},{7,23},{8,24},{9,... | collective-permute-start | bytes 294920 | tf_op jit(solution)/shard_map/ppermute | solution.py:447
  56.1 7.9 %collective-permute-done.6.second = f32[3,32,256]{2,1,0:T(8,128)S(1)} collective-permute-done((f32[3,32,256]{2,1,0:T(8,128)S(1)}, f32[3,32,256]{2,1,0:T(8,128)S(1)}, u32[]{:S(2)}, u32[]{:S(2)}) %collective-permute-start.6) | collective-permute-done | bytes 98336 | tf_op jit(solution)/shard_map/ppermute | solution.py:448
  64.0 0.0 collective-permute-done.5.first
  64.0 0.5 all-to-all-done.got
  64.5 0.7 shard_map.108
  65.2 13.5 %all-to-all-start.1 = ((f32[16,16,128]{2,1,0:T(8,128)}), f32[16,16,128]{2,1,0:T(8,128)S(1)}, u32[]{:S(2)}, u32[]{:S(2)}) async-start(f32[16,16,128]{2,1,0:T(8,128)} %shard_map.108), calls=%async_computation.1 | async-start | bytes 262144 | tf_op jit(solution)/shard_map/all_to_all | solution.py:530
  78.7 0.1 pad_add_fusion.where_ref
  78.8 3.6 %shard_map.107 = (bf16[288,256]{1,0:T(8,128)(2,1)}, bf16[288,256]{1,0:T(8,128)(2,1)}) custom-call(s32[2]{0:T(128)S(1)} %pad_add_fusion.where_ref, f32[3,32,256]{2,1,0:T(8,128)S(1)} %collective-permute-done.5.first, f32[3,32,256]{2,1,0:T(8,128)S(1)} %collective-permute-done.6.second, f32[12,32,256]{2,1,0:T(8,128)S(1)} %get-tuple-element.55.grad_conv, ...), custom_call_target="tpu_custom_call" | custom-call | tf_op jit(solution)/shard_map/pallas_call | solution.py:425
  82.4 8.3 %all-to-all-done.1.got = f32[16,16,128]{2,1,0:T(8,128)S(1)} async-done(((f32[16,16,128]{2,1,0:T(8,128)}), f32[16,16,128]{2,1,0:T(8,128)S(1)}, u32[]{:S(2)}, u32[]{:S(2)}) %all-to-all-start.1) | async-done | bytes 131104 | tf_op jit(solution)/shard_map/all_to_all | solution.py:530
  90.7 0.7 shard_map.110
  91.4 7.4 %all-to-all-start.2 = ((f32[32,8,128]{2,1,0:T(8,128)}), f32[32,8,128]{2,1,0:T(8,128)S(1)}, u32[]{:S(2)}, u32[]{:S(2)}) async-start(f32[32,8,128]{2,1,0:T(8,128)} %shard_map.110), calls=%async_computation.2 | async-start | bytes 262144 | tf_op jit(solution)/shard_map/all_to_all | solution.py:546
  98.8 0.6 shard_map.109
  99.4 7.0 %all-to-all-done.2.got = f32[32,8,128]{2,1,0:T(8,128)S(1)} async-done(((f32[32,8,128]{2,1,0:T(8,128)}), f32[32,8,128]{2,1,0:T(8,128)S(1)}, u32[]{:S(2)}, u32[]{:S(2)}) %all-to-all-start.2) | async-done | bytes 131104 | tf_op jit(solution)/shard_map/all_to_all | solution.py:546
  106.4 0.6 shard_map.111
  (4 shorter events, 0.1 us)
Async XLA Ops:
  0.7 26.1 %copy-start.1 = (f32[12,24,256]{2,1,0:T(8,128)S(1)}, f32[12,24,256]{2,1,0:T(8,128)}, u32[]{:S(2)}) copy-start(f32[12,24,256]{2,1,0:T(8,128)} %state.7) | copy-start | bytes 884740
  0.7 26.1 %copy-start.3 = (bf16[12,24,256]{2,1,0:T(8,128)(2,1)S(1)}, bf16[12,24,256]{2,1,0:T(8,128)(2,1)}, u32[]{:S(2)}) copy-start(bf16[12,24,256]{2,1,0:T(8,128)(2,1)} %param.7) | copy-start | bytes 442372
  1.7 15.8 %collective-permute-start.1 = (f32[3,24,256]{2,1,0:T(8,128)S(1)}, f32[3,24,256]{2,1,0:T(8,128)S(1)}, u32[]{:S(2)}, u32[]{:S(2)}) collective-permute-start(f32[3,24,256]{2,1,0:T(8,128)S(1)} %reverse_select_fusion.1), channel_id=1, source_target_pairs={{0,8},{1,9},{2,10},{3,11},{4,12},{5,13},{6,14},{7,15},{8,0},{9,1},... | collective-permute-start | bytes 221192 | tf_op jit(solution)/shard_map/ppermute | solution.py:448
  6.2 11.3 %collective-permute-start = (f32[3,24,256]{2,1,0:T(8,128)S(1)}, f32[3,24,256]{2,1,0:T(8,128)S(1)}, u32[]{:S(2)}, u32[]{:S(2)}) collective-permute-start(f32[3,24,256]{2,1,0:T(8,128)S(1)} %get-tuple-element.70), channel_id=1, source_target_pairs={{0,16},{1,17},{2,18},{3,19},{4,20},{5,21},{6,22},{7,23},{8,24},{9,... | collective-permute-start | bytes 221192 | tf_op jit(solution)/shard_map/ppermute | solution.py:447
  12.4 1.0 copy-start
  13.4 0.9 copy-start.2
  14.3 1.0 copy-start.4
  15.3 1.0 copy-start.5
  16.4 0.7 copy-start.7
  17.1 9.7 %copy-start.6 = (f32[49,256]{1,0:T(8,128)S(1)}, f32[49,256]{1,0:T(8,128)}, u32[]{:S(2)}) copy-start(f32[49,256]{1,0:T(8,128)} %taps.5) | copy-start | bytes 150532
  17.6 13.9 %collective-permute-start.2 = (f32[144,256]{1,0:T(8,128)S(1)}, f32[144,256]{1,0:T(8,128)S(1)}, u32[]{:S(2)}, u32[]{:S(2)}) collective-permute-start(f32[144,256]{1,0:T(8,128)S(1)} %get-tuple-element.40), channel_id=1, source_target_pairs={{0,1},{1,2},{2,3},{3,4},{4,5},{5,6},{6,7},{7,8},{8,9},{9,10},{10,1... | collective-permute-start | bytes 442376 | tf_op jit(solution)/shard_map/ppermute | solution.py:488
  19.5 12.0 %collective-permute-start.3 = (f32[144,256]{1,0:T(8,128)S(1)}, f32[144,256]{1,0:T(8,128)S(1)}, u32[]{:S(2)}, u32[]{:S(2)}) collective-permute-start(f32[144,256]{1,0:T(8,128)S(1)} %get-tuple-element.41), channel_id=1, source_target_pairs={{0,15},{1,0},{2,1},{3,2},{4,3},{5,4},{6,5},{7,6},{8,7},{9,8},{10,9... | collective-permute-start | bytes 442376 | tf_op jit(solution)/shard_map/ppermute | solution.py:489
  34.8 4.8 %collective-permute-start.4 = (f32[16,128,128]{2,1,0:T(8,128)S(1)}, f32[16,128,128]{2,1,0:T(8,128)S(1)}, u32[]{:S(2)}, u32[]{:S(2)}) collective-permute-start(f32[16,128,128]{2,1,0:T(8,128)S(1)} %get-tuple-element.48), channel_id=1, source_target_pairs={{0,16},{16,0},{1,17},{17,1},{2,18},{18,2},{3,19},{19,3},{4,20},{20... | collective-permute-start | bytes 3145736 | tf_op jit(solution)/shard_map/ppermute | solution.py:518
  40.7 23.9 %all-to-all-start = ((f32[16,136,128]{2,1,0:T(8,128)}), f32[16,136,128]{2,1,0:T(8,128)S(1)}, u32[]{:S(2)}, u32[]{:S(2)}) async-start(f32[16,136,128]{2,1,0:T(8,128)} %shard_map.106), calls=%async_computation | async-start | bytes 2228224 | tf_op jit(solution)/shard_map/all_to_all | solution.py:526
  48.2 15.8 %collective-permute-start.6 = (f32[3,32,256]{2,1,0:T(8,128)S(1)}, f32[3,32,256]{2,1,0:T(8,128)S(1)}, u32[]{:S(2)}, u32[]{:S(2)}) collective-permute-start(f32[3,32,256]{2,1,0:T(8,128)S(1)} %reverse_select_fusion), channel_id=1, source_target_pairs={{0,8},{1,9},{2,10},{3,11},{4,12},{5,13},{6,14},{7,15},{8,0},{9,1},... | collective-permute-start | bytes 294920 | tf_op jit(solution)/shard_map/ppermute | solution.py:448
  52.3 11.7 %collective-permute-start.5 = (f32[3,32,256]{2,1,0:T(8,128)S(1)}, f32[3,32,256]{2,1,0:T(8,128)S(1)}, u32[]{:S(2)}, u32[]{:S(2)}) collective-permute-start(f32[3,32,256]{2,1,0:T(8,128)S(1)} %get-tuple-element.68), channel_id=1, source_target_pairs={{0,16},{1,17},{2,18},{3,19},{4,20},{5,21},{6,22},{7,23},{8,24},{9,... | collective-permute-start | bytes 294920 | tf_op jit(solution)/shard_map/ppermute | solution.py:447
  65.2 25.4 %all-to-all-start.1 = ((f32[16,16,128]{2,1,0:T(8,128)}), f32[16,16,128]{2,1,0:T(8,128)S(1)}, u32[]{:S(2)}, u32[]{:S(2)}) async-start(f32[16,16,128]{2,1,0:T(8,128)} %shard_map.108), calls=%async_computation.1 | async-start | bytes 262144 | tf_op jit(solution)/shard_map/all_to_all | solution.py:530
  91.4 15.0 %all-to-all-start.2 = ((f32[32,8,128]{2,1,0:T(8,128)}), f32[32,8,128]{2,1,0:T(8,128)S(1)}, u32[]{:S(2)}, u32[]{:S(2)}) async-start(f32[32,8,128]{2,1,0:T(8,128)} %shard_map.110), calls=%async_computation.2 | async-start | bytes 262144 | tf_op jit(solution)/shard_map/all_to_all | solution.py:546

commit v6 on v4

--- a/solution.py
+++ b/solution.py
@@ -34,13 +34,13 @@
 
 
 def column_pairs():
-    right, left = [], []
+    near, far = [], []
     for lat in range(LAT):
         for lon in range(LON):
             here = lat * LON + lon
-            right.append((here, lat * LON + (lon + 1) % LON))
-            left.append((here, lat * LON + (lon - 1) % LON))
-    return right, left
+            near.append((here, lat * LON + (lon ^ 1)))
+            far.append((here, lat * LON + (lon - 1 if lon % 2 == 0 else lon + 1) % LON))
+    return near, far
 
 
 H = 12
@@ -111,17 +111,20 @@
         fetch.wait()
 
 
-def edge_kernel(even_ref, first, second, own_right, own_left, above, below, to_right, to_left):
+def edge_kernel(even_ref, first, second, own_right, own_left, above, below, near, far):
     even = even_ref[0] == 1
+    west = even_ref[1] == 1
     above[...] = jnp.where(even, second[...], first[...])
     below[...] = jnp.where(even, first[...], second[...])
-    to_right[0 : 9 * H, :] = own_right[...]
-    to_left[0 : 9 * H, :] = own_left[...]
+    far[0 : 9 * H, :] = jnp.where(west, own_left[...], own_right[...])
+    near[0 : 9 * H, :] = jnp.where(west, own_right[...], own_left[...])
     for row in range(3):
         for place, ref in ((9 * H, above), (9 * H + 18, below)):
             spot = place + 6 * row
-            to_right[spot : spot + 6, :] = ref[row, W - 6 : W, :]
-            to_left[spot : spot + 6, :] = ref[row, 0:6, :]
+            to_right = ref[row, W - 6 : W, :]
+            to_left = ref[row, 0:6, :]
+            far[spot : spot + 6, :] = jnp.where(west, to_left, to_right)
+            near[spot : spot + 6, :] = jnp.where(west, to_right, to_left)
 
 
 def source_row(above, state, below, row):
@@ -259,10 +262,13 @@
 
 
 def forward_kernel(
-    core_ref, above, below, state, before, after, cot, taps, gain, w_in, w_out, mine_in, theirs_in,
-    mine, theirs, hidden, grad_pre, centred_out, inv_out,
+    core_ref, above, below, state, near, far, cot, taps, gain, w_in, w_out, mine_in, theirs_in,
+    mine, theirs, hidden, grad_pre, centred_out, inv_out, before, after,
     wide, conv, cot_all,
 ):
+    west = core_ref[1] == 1
+    before[...] = jnp.where(west, far[...], near[...])
+    after[...] = jnp.where(west, near[...], far[...])
     fill(wide, above, below, state, before, after)
     cot_all[:, 8:16, :] = jnp.zeros((H, 8, C), jnp.float32)
     own = cot[...].astype(jnp.float32)
@@ -436,12 +442,13 @@
 
 def body(state_field, cotangent, depthwise, norm_gain, w_in, w_out):
     grad_scale = 1.0 / math.sqrt(CELLS * LAT * LON)
-    lat, _ = lat_lon()
+    lat, lon = lat_lon()
     lat = lat.astype(jnp.int32)
+    west = (lon % 2 == 0).astype(jnp.int32)
     even = lat % 2 == 0
     pole = (lat == 0) | (lat == LAT - 1)
     parity = even.astype(jnp.int32)
-    core = lax.axis_index("core").astype(jnp.int32).reshape(1)
+    core = jnp.stack([lax.axis_index("core").astype(jnp.int32), west])
     cot = cotangent.reshape(CELLS, C)
     gain = norm_gain.reshape(1, C)
     *own_edges, gain, w_in, w_out = call(
@@ -463,16 +470,15 @@
         held=(0, 1, 2, 3, 4),
     )
     rows = row_exchange(state_field, even, pole)
-    above, below, to_right, to_left = call(
+    above, below, to_near, to_far = call(
         edge_kernel,
         [((3, W, C), F32), ((3, W, C), F32), ((EDGE, C), F32), ((EDGE, C), F32)],
-        parity.reshape(1), *rows, *own_edges,
+        jnp.stack([parity, west]), *rows, *own_edges,
         scalars=1,
     )
-    right, left = column_pairs()
-    before = lax.ppermute(to_right, AXES, right)
-    after = lax.ppermute(to_left, AXES, left)
-    pieces = (above, below, state_field, before, after)
+    near, far = column_pairs()
+    near = lax.ppermute(to_near, AXES, near)
+    far = lax.ppermute(to_far, AXES, far)
     part = ((16, 128, 128), F32)
     mine, theirs, middle, grad_middle, tap_middle = call(
         middle_kernel,
@@ -486,7 +492,7 @@
         ],
         scalars=1,
     )
-    mine, theirs, hidden, grad_pre, centred, inv_std = call(
+    mine, theirs, hidden, grad_pre, centred, inv_std, before, after = call(
         forward_kernel,
         [
             part,
@@ -495,8 +501,10 @@
             ((HALF_CELLS, FF), BF16),
             ((HALF_CELLS, C), F32),
             ((HALF_CELLS, 128), F32),
-        ],
-        core, *pieces, cot, depthwise, gain, w_in, w_out, mine, theirs,
+            ((EDGE, C), F32),
+            ((EDGE, C), F32),
+        ],
+        core, above, below, state_field, near, far, cot, depthwise, gain, w_in, w_out, mine, theirs,
         scratch=[WIDE, ((HALF_CELLS, C), F32), ((H, M, C), F32)],
         scalars=1,
     )
@@ -504,7 +512,7 @@
     grad_conv, taps = call(
         backward_kernel,
         [((H, V, C), F32), ((128, 128), F32)],
-        *pieces, gain, w_in, grad_pre, centred, inv_std, grad_middle, tap_middle,
+        above, below, state_field, before, after, gain, w_in, grad_pre, centred, inv_std, grad_middle, tap_middle,
         scratch=[WIDE, ((H, M, C), F32)],
     )
     (joined,) = call(join_kernel, [((16, 136, 128), F32)], mine, theirs, taps)

time: 107 us -> 108 us (level)
  starting transfers between devices: 51.2 us -> 48.4 us
  Pallas kernels: 17.2 us -> 18.9 us
  waiting for transfers between devices: 16.8 us -> 18.2 us
    ppermute x2, starting transfers between devices: 9.19 us -> 6.47 us  [the longest x1 4.55 us: body(): far = lax.ppermute(to_far, AXES, far)]
    pallas_call x10, Pallas kernels: 17.2 us -> 18.9 us  [call(): pl.pallas_call(kernel, out_shape=[jax.ShapeDtypeStruct(s, d) for s, d in...]
    ppermute x2, waiting for transfers between devices: 0.01 us -> 1.42 us  [the longest x1 1.42 us: body(): far = lax.ppermute(to_far, AXES, far)]
    all_to_all x1, starting transfers between devices: 13.5 us -> 12.2 us  [body(): lax.all_to_all(spread, ('zh', 'zl'), split_axis=0, concat_axis=0, tiled=T...]
  transfers between devices with their start and end apart: 9 -> 9, of which waited for: 4 -> 5; matrix products, arithmetic and copies ran while one was open for 0% -> 0% of each run, Pallas kernels for 10% -> 11%
where the time goes in v6:
time: 108 us; the launch traced here: 107 us
  starting transfers between devices  48.4 us (45%)
  Pallas kernels  18.9 us (17%)
  waiting for transfers between devices  18.2 us (17%)
  blocking collectives  14.6 us (14%)
  local copies, waits for them, and re-layouts  4.64 us (4%)
  other arithmetic  1.26 us (1%)
    pallas_call x10, Pallas kernels, call(): pl.pallas_call(kernel, out_shape=[jax.ShapeDtypeStruct(s, d) for s, d in...  18.9 us
    all_to_all x1, blocking collectives, body(): lax.all_to_all(shared, ('x', 'core', 'y'), split_axis=0, concat_axis=0, t...  14.6 us
    all_to_all x1, starting transfers between devices, body(): lax.all_to_all(spread, ('zh', 'zl'), split_axis=0, concat_axis=0, tiled=T...  12.2 us
    ppermute x2, starting transfers between devices, row_exchange(): got_first = lax.ppermute(jnp.where(even, tail, head), AXES, first)  10 us
    ppermute x2, starting transfers between devices, row_exchange(): got_second = lax.ppermute(outer, AXES, second)  8.73 us
    all_to_all x1, waiting for transfers between devices, body(): lax.all_to_all(spread, ('zh', 'zl'), split_axis=0, concat_axis=0, tiled=T...  8.3 us
    all_to_all x1, starting transfers between devices, body(): lax.all_to_all(joined, ('x', 'y'), split_axis=0, concat_axis=0, tiled=True)  8.24 us
    ppermute x2, waiting for transfers between devices, row_exchange(): got_second = lax.ppermute(outer, AXES, second)  7.9 us
  transfers between devices with their start and end apart: 9, of which 5 were waited for; matrix products, arithmetic and copies ran while one was open for 0% of the time, Pallas kernels for 11%

profile of v6, /device:TPU:1, one launch (start us, length us, event | category | flops | bytes accessed | tf_op | source)
XLA Modules:
  0.0 106.9 jit_solution(6381369752740357569)
XLA Ops:
  0.7 0.0 copy-start.6
  0.7 0.0 copy-start.1
  0.7 1.0 slice_select_fusion.2
  1.7 0.0 copy-start.3
  1.7 4.6 %collective-permute-start.1 = (f32[3,24,256]{2,1,0:T(8,128)S(1)}, f32[3,24,256]{2,1,0:T(8,128)S(1)}, u32[]{:S(2)}, u32[]{:S(2)}) collective-permute-start(f32[3,24,256]{2,1,0:T(8,128)S(1)} %reverse_select_fusion.1), channel_id=1, source_target_pairs={{0,8},{1,9},{2,10},{3,11},{4,12},{5,13},{6,14},{7,15},{8,0},{9,1},... | collective-permute-start | bytes 221192 | tf_op jit(solution)/shard_map/ppermute | solution.py:439
  6.3 6.2 %collective-permute-start = (f32[3,24,256]{2,1,0:T(8,128)S(1)}, f32[3,24,256]{2,1,0:T(8,128)S(1)}, u32[]{:S(2)}, u32[]{:S(2)}) collective-permute-start(f32[3,24,256]{2,1,0:T(8,128)S(1)} %get-tuple-element.78), channel_id=1, source_target_pairs={{0,16},{1,17},{2,18},{3,19},{4,20},{5,21},{6,22},{7,23},{8,24},{9,... | collective-permute-start | bytes 221192 | tf_op jit(solution)/shard_map/ppermute | solution.py:438
  12.6 0.0 copy-start
  12.6 1.0 copy-done
  13.5 0.0 copy-start.2
  13.5 0.9 copy-done.2
  14.4 0.0 copy-start.4
  14.4 1.0 copy-done.4
  15.5 0.0 copy-start.5
  15.5 1.0 copy-done.5
  16.5 0.0 copy-start.7
  16.5 0.7 copy-done.7
  17.2 0.4 shard_map.101
  17.6 0.1 pad_add_fusion.2.even_ref
  17.7 0.0 collective-permute-done.1.second
  17.7 0.0 collective-permute-done.first
  17.7 0.6 shard_map.102
  18.3 1.9 %collective-permute-start.2 = (f32[144,256]{1,0:T(8,128)S(1)}, f32[144,256]{1,0:T(8,128)S(1)}, u32[]{:S(2)}, u32[]{:S(2)}) collective-permute-start(f32[144,256]{1,0:T(8,128)S(1)} %get-tuple-element.44), channel_id=1, source_target_pairs={{0,1},{1,0},{2,3},{3,2},{4,5},{5,4},{6,7},{7,6},{8,9},{9,8},{10,11... | collective-permute-start | bytes 442376 | tf_op jit(solution)/shard_map/ppermute | solution.py:480
  20.2 4.6 %collective-permute-start.3 = (f32[144,256]{1,0:T(8,128)S(1)}, f32[144,256]{1,0:T(8,128)S(1)}, u32[]{:S(2)}, u32[]{:S(2)}) collective-permute-start(f32[144,256]{1,0:T(8,128)S(1)} %get-tuple-element.45), channel_id=1, source_target_pairs={{0,15},{1,2},{2,1},{3,4},{4,3},{5,6},{6,5},{7,8},{8,7},{9,10},{10,... | collective-permute-start | bytes 442376 | tf_op jit(solution)/shard_map/ppermute | solution.py:481
  24.8 0.1 pad_add_fusion.1.core_ref
  24.9 0.0 copy-done.6
  24.9 0.0 copy-done.1
  24.9 0.0 copy-done.3
  24.9 5.2 %shard_map.103 = (f32[16,128,128]{2,1,0:T(8,128)S(1)}, f32[16,128,128]{2,1,0:T(8,128)S(1)}, bf16[192,1024]{1,0:T(8,128)(2,1)S(1)}, f32[12,16,256]{2,1,0:T(8,128)S(1)}, f32[128,128]{1,0:T(8,128)S(1)}) custom-call(s32[2]{0:T(128)S(1)} %pad_add_fusion.1.core_ref, f32[3,24,256]{2,1,0:T(8,128)S(1)} %get-tuple-element.42.above, ...), custom_call_target="tpu_custom_call" | custom-call | tf_op jit(solution)/shard_map/pallas_call | solution.py:416
  30.1 0.0 collective-permute-done.2.near
  30.1 1.4 %collective-permute-done.3.far = f32[144,256]{1,0:T(8,128)S(1)} collective-permute-done((f32[144,256]{1,0:T(8,128)S(1)}, f32[144,256]{1,0:T(8,128)S(1)}, u32[]{:S(2)}, u32[]{:S(2)}) %collective-permute-start.3) | collective-permute-done | bytes 147488 | tf_op jit(solution)/shard_map/ppermute | solution.py:481
  31.6 3.8 %shard_map.104 = (f32[16,128,128]{2,1,0:T(8,128)S(1)}, f32[16,128,128]{2,1,0:T(8,128)S(1)}, bf16[192,1024]{1,0:T(8,128)(2,1)S(1)}, bf16[192,1024]{1,0:T(8,128)(2...) custom-call(s32[2]{0:T(128)S(1)} %pad_add_fusion.1.core_ref, ...), custom_call_target="tpu_custom_call" | custom-call | tf_op jit(solution)/shard_map/pallas_call | solution.py:416
  35.3 2.8 %collective-permute-start.4 = (f32[16,128,128]{2,1,0:T(8,128)S(1)}, f32[16,128,128]{2,1,0:T(8,128)S(1)}, u32[]{:S(2)}, u32[]{:S(2)}) collective-permute-start(f32[16,128,128]{2,1,0:T(8,128)S(1)} %get-tuple-element.52), channel_id=1, source_target_pairs={{0,16},{16,0},{1,17},{17,1},{2,18},{18,2},{3,19},{19,3},{4,20},{20... | collective-permute-start | bytes 3145736 | tf_op jit(solution)/shard_map/ppermute | solution.py:511
  38.1 2.2 %shard_map.105 = (f32[12,32,256]{2,1,0:T(8,128)S(1)}, f32[128,128]{1,0:T(8,128)S(1)}) custom-call(f32[3,24,256]{2,1,0:T(8,128)S(1)} %get-tuple-element.42.above, f32[3,24,256]{2,1,0:T(8,128)S(1)} %get-tuple-element.43.below, f32[12,24,256]{2,1,0:T(8,128)S(1)} %copy-done.1, f32[144,256]{1,0:T(8,128)S(1)} %get-tuple-element.53.before, ...), custom_call_target="tpu_custom_call" | custom-call | tf_op jit(solution)/shard_map/pallas_call | solution.py:416
  40.3 0.1 collective-permute-done.4.theirs
  40.4 1.1 %shard_map.106 = f32[16,136,128]{2,1,0:T(8,128)} custom-call(f32[16,128,128]{2,1,0:T(8,128)S(1)} %get-tuple-element.51.mine, f32[16,128,128]{2,1,0:T(8,128)S(1)} %collective-permute-done.4.theirs, f32[128,128]{1,0:T(8,128)S(1)} %get-tuple-element.60.taps), custom_call_target="tpu_custom_call" | custom-call | tf_op jit(solution)/shard_map/pallas_call | solution.py:416
  41.5 8.2 %all-to-all-start = ((f32[16,136,128]{2,1,0:T(8,128)}), f32[16,136,128]{2,1,0:T(8,128)S(1)}, u32[]{:S(2)}, u32[]{:S(2)}) async-start(f32[16,136,128]{2,1,0:T(8,128)} %shard_map.106), calls=%async_computation | async-start | bytes 2228224 | tf_op jit(solution)/shard_map/all_to_all | solution.py:519
  49.8 4.1 %collective-permute-start.6 = (f32[3,32,256]{2,1,0:T(8,128)S(1)}, f32[3,32,256]{2,1,0:T(8,128)S(1)}, u32[]{:S(2)}, u32[]{:S(2)}) collective-permute-start(f32[3,32,256]{2,1,0:T(8,128)S(1)} %reverse_select_fusion), channel_id=1, source_target_pairs={{0,8},{1,9},{2,10},{3,11},{4,12},{5,13},{6,14},{7,15},{8,0},{9,1},... | collective-permute-start | bytes 294920 | tf_op jit(solution)/shard_map/ppermute | solution.py:439
  53.9 3.8 %collective-permute-start.5 = (f32[3,32,256]{2,1,0:T(8,128)S(1)}, f32[3,32,256]{2,1,0:T(8,128)S(1)}, u32[]{:S(2)}, u32[]{:S(2)}) collective-permute-start(f32[3,32,256]{2,1,0:T(8,128)S(1)} %get-tuple-element.76), channel_id=1, source_target_pairs={{0,16},{1,17},{2,18},{3,19},{4,20},{5,21},{6,22},{7,23},{8,24},{9,... | collective-permute-start | bytes 294920 | tf_op jit(solution)/shard_map/ppermute | solution.py:438
  57.7 7.9 %collective-permute-done.6.second = f32[3,32,256]{2,1,0:T(8,128)S(1)} collective-permute-done((f32[3,32,256]{2,1,0:T(8,128)S(1)}, f32[3,32,256]{2,1,0:T(8,128)S(1)}, u32[]{:S(2)}, u32[]{:S(2)}) %collective-permute-start.6) | collective-permute-done | bytes 98336 | tf_op jit(solution)/shard_map/ppermute | solution.py:439
  65.6 0.0 collective-permute-done.5.first
  65.6 0.5 all-to-all-done.got
  66.1 0.7 shard_map.108
  66.8 12.2 %all-to-all-start.1 = ((f32[16,16,128]{2,1,0:T(8,128)}), f32[16,16,128]{2,1,0:T(8,128)S(1)}, u32[]{:S(2)}, u32[]{:S(2)}) async-start(f32[16,16,128]{2,1,0:T(8,128)} %shard_map.108), calls=%async_computation.1 | async-start | bytes 262144 | tf_op jit(solution)/shard_map/all_to_all | solution.py:523
  79.0 0.1 pad_add_fusion.where_ref
  79.1 3.6 %shard_map.107 = (bf16[288,256]{1,0:T(8,128)(2,1)}, bf16[288,256]{1,0:T(8,128)(2,1)}) custom-call(s32[2]{0:T(128)S(1)} %pad_add_fusion.where_ref, f32[3,32,256]{2,1,0:T(8,128)S(1)} %collective-permute-done.5.first, f32[3,32,256]{2,1,0:T(8,128)S(1)} %collective-permute-done.6.second, f32[12,32,256]{2,1,0:T(8,128)S(1)} %get-tuple-element.61.grad_conv, ...), custom_call_target="tpu_custom_call" | custom-call | tf_op jit(solution)/shard_map/pallas_call | solution.py:416
  82.7 8.3 %all-to-all-done.1.got = f32[16,16,128]{2,1,0:T(8,128)S(1)} async-done(((f32[16,16,128]{2,1,0:T(8,128)}), f32[16,16,128]{2,1,0:T(8,128)S(1)}, u32[]{:S(2)}, u32[]{:S(2)}) %all-to-all-start.1) | async-done | bytes 131104 | tf_op jit(solution)/shard_map/all_to_all | solution.py:523
  91.0 0.6 shard_map.109
  91.6 14.6 %all_to_all.15.got = f32[32,8,128]{2,1,0:T(8,128)S(1)} all-to-all(f32[32,8,128]{2,1,0:T(8,128)S(1)} %get-tuple-element.72), channel_id=1, replica_groups=mesh['zh'=4,'x'=4,'core'=2,'y'=4,'zl'=4] {'x','core','y'}, dimensions={0} | all-to-all | bytes 262144 | tf_op jit(solution)/shard_map/all_to_all | solution.py:540
  106.3 0.6 shard_map.110
  (3 shorter events, 0.0 us)
Async XLA Ops:
  0.7 24.2 %copy-start.6 = (f32[49,256]{1,0:T(8,128)S(1)}, f32[49,256]{1,0:T(8,128)}, u32[]{:S(2)}) copy-start(f32[49,256]{1,0:T(8,128)} %taps.5) | copy-start | bytes 150532
  0.7 24.2 %copy-start.1 = (f32[12,24,256]{2,1,0:T(8,128)S(1)}, f32[12,24,256]{2,1,0:T(8,128)}, u32[]{:S(2)}) copy-start(f32[12,24,256]{2,1,0:T(8,128)} %state.7) | copy-start | bytes 884740
  1.7 23.2 %copy-start.3 = (bf16[12,24,256]{2,1,0:T(8,128)(2,1)S(1)}, bf16[12,24,256]{2,1,0:T(8,128)(2,1)}, u32[]{:S(2)}) copy-start(bf16[12,24,256]{2,1,0:T(8,128)(2,1)} %param.7) | copy-start | bytes 442372
  1.7 16.0 %collective-permute-start.1 = (f32[3,24,256]{2,1,0:T(8,128)S(1)}, f32[3,24,256]{2,1,0:T(8,128)S(1)}, u32[]{:S(2)}, u32[]{:S(2)}) collective-permute-start(f32[3,24,256]{2,1,0:T(8,128)S(1)} %reverse_select_fusion.1), channel_id=1, source_target_pairs={{0,8},{1,9},{2,10},{3,11},{4,12},{5,13},{6,14},{7,15},{8,0},{9,1},... | collective-permute-start | bytes 221192 | tf_op jit(solution)/shard_map/ppermute | solution.py:439
  6.3 11.4 %collective-permute-start = (f32[3,24,256]{2,1,0:T(8,128)S(1)}, f32[3,24,256]{2,1,0:T(8,128)S(1)}, u32[]{:S(2)}, u32[]{:S(2)}) collective-permute-start(f32[3,24,256]{2,1,0:T(8,128)S(1)} %get-tuple-element.78), channel_id=1, source_target_pairs={{0,16},{1,17},{2,18},{3,19},{4,20},{5,21},{6,22},{7,23},{8,24},{9,... | collective-permute-start | bytes 221192 | tf_op jit(solution)/shard_map/ppermute | solution.py:438
  12.6 1.0 copy-start
  13.5 0.9 copy-start.2
  14.4 1.0 copy-start.4
  15.5 1.0 copy-start.5
  16.5 0.7 copy-start.7
  18.3 11.8 %collective-permute-start.2 = (f32[144,256]{1,0:T(8,128)S(1)}, f32[144,256]{1,0:T(8,128)S(1)}, u32[]{:S(2)}, u32[]{:S(2)}) collective-permute-start(f32[144,256]{1,0:T(8,128)S(1)} %get-tuple-element.44), channel_id=1, source_target_pairs={{0,1},{1,0},{2,3},{3,2},{4,5},{5,4},{6,7},{7,6},{8,9},{9,8},{10,11... | collective-permute-start | bytes 442376 | tf_op jit(solution)/shard_map/ppermute | solution.py:480
  20.2 11.3 %collective-permute-start.3 = (f32[144,256]{1,0:T(8,128)S(1)}, f32[144,256]{1,0:T(8,128)S(1)}, u32[]{:S(2)}, u32[]{:S(2)}) collective-permute-start(f32[144,256]{1,0:T(8,128)S(1)} %get-tuple-element.45), channel_id=1, source_target_pairs={{0,15},{1,2},{2,1},{3,4},{4,3},{5,6},{6,5},{7,8},{8,7},{9,10},{10,... | collective-permute-start | bytes 442376 | tf_op jit(solution)/shard_map/ppermute | solution.py:481
  35.3 5.0 %collective-permute-start.4 = (f32[16,128,128]{2,1,0:T(8,128)S(1)}, f32[16,128,128]{2,1,0:T(8,128)S(1)}, u32[]{:S(2)}, u32[]{:S(2)}) collective-permute-start(f32[16,128,128]{2,1,0:T(8,128)S(1)} %get-tuple-element.52), channel_id=1, source_target_pairs={{0,16},{16,0},{1,17},{17,1},{2,18},{18,2},{3,19},{19,3},{4,20},{20... | collective-permute-start | bytes 3145736 | tf_op jit(solution)/shard_map/ppermute | solution.py:511
  41.5 24.6 %all-to-all-start = ((f32[16,136,128]{2,1,0:T(8,128)}), f32[16,136,128]{2,1,0:T(8,128)S(1)}, u32[]{:S(2)}, u32[]{:S(2)}) async-start(f32[16,136,128]{2,1,0:T(8,128)} %shard_map.106), calls=%async_computation | async-start | bytes 2228224 | tf_op jit(solution)/shard_map/all_to_all | solution.py:519
  49.8 15.8 %collective-permute-start.6 = (f32[3,32,256]{2,1,0:T(8,128)S(1)}, f32[3,32,256]{2,1,0:T(8,128)S(1)}, u32[]{:S(2)}, u32[]{:S(2)}) collective-permute-start(f32[3,32,256]{2,1,0:T(8,128)S(1)} %reverse_select_fusion), channel_id=1, source_target_pairs={{0,8},{1,9},{2,10},{3,11},{4,12},{5,13},{6,14},{7,15},{8,0},{9,1},... | collective-permute-start | bytes 294920 | tf_op jit(solution)/shard_map/ppermute | solution.py:439
  53.9 11.7 %collective-permute-start.5 = (f32[3,32,256]{2,1,0:T(8,128)S(1)}, f32[3,32,256]{2,1,0:T(8,128)S(1)}, u32[]{:S(2)}, u32[]{:S(2)}) collective-permute-start(f32[3,32,256]{2,1,0:T(8,128)S(1)} %get-tuple-element.76), channel_id=1, source_target_pairs={{0,16},{1,17},{2,18},{3,19},{4,20},{5,21},{6,22},{7,23},{8,24},{9,... | collective-permute-start | bytes 294920 | tf_op jit(solution)/shard_map/ppermute | solution.py:438
  66.8 24.2 %all-to-all-start.1 = ((f32[16,16,128]{2,1,0:T(8,128)}), f32[16,16,128]{2,1,0:T(8,128)S(1)}, u32[]{:S(2)}, u32[]{:S(2)}) async-start(f32[16,16,128]{2,1,0:T(8,128)} %shard_map.108), calls=%async_computation.1 | async-start | bytes 262144 | tf_op jit(solution)/shard_map/all_to_all | solution.py:523
